TPU v7x, 32 devices: a whole 2x2x4 slice. The times are simulated.
32 devices in a mesh: sub: 16 (over z, y, x), grp: 2 (over core).
Axes of the slice: x: 2, y: 2, z: 4, core: 2. Of those that a mesh axis runs over, the one named last changes fastest.
Arguments:
- applied_loads: float32 [128, 3, 64, 128], P(('sub', 'grp')), may hold values from -12 to 12
- labels: int32 [128, 64], P(('sub', 'grp')), may hold values from 0 to 7
- shear_modulus: float32 [8], replicated, may hold values from 0.05 to 0.25
- stiff_ratio: float32 [8], replicated, may hold values from 0.5 to 2
- local_order: int32 [32, 1152], P(('sub', 'grp')), may hold values from 0 to 1151, each once within a row
- local_inverse: bfloat16 [32, 1152, 1152], P(('sub', 'grp')), may hold values from -0.05 to 0.2
- coarse_basis: float32 [32, 4, 1152], P(('sub', 'grp')), may hold values from -0.1875 to 0.1875
- coarse_inverse: float32 [128, 128], P('sub'), may hold values from -0.05 to 0.2
Outputs:
- solution: float32 [128, 3, 64, 128], P(('sub', 'grp'))
- residual: float32 [128, 3, 64, 128], P(('sub', 'grp'))
- coarse_values: float32 [128, 128], P(('sub', 'grp'))
Inputs may be any that keep to these rules, and one draw needn't show every extreme that they name: `local_order`: every row holds each number from 0 to 1151 once.
All inputs are finite; a program needn't handle non-finite values.
Results may differ from a plain program's by a relative error of at most 0.0015.
Values sent between devices are 32-bit elements; how exact they have to be, the bound alone decides.
No kernel may reach another device: no remote copies, remote signals or barrier semaphores. Data moves between devices by JAX's collectives and lax.ppermute only.
A program may use at most 64 MiB of HBM per device.

v0:
```python
import jax
import jax.numpy as jnp
from jax import lax
from jax.sharding import PartitionSpec as P

NY = 8
NZ = 8
CV_DEV = 4
ITERS = 3


RELAXATION = 0.5
PRECISE = lax.Precision.HIGHEST


def padded_2(cells, sides, width):
    for axis, dim in sides:
        count = lax.axis_size(axis)
        ends = count - 1
        head = lax.slice_in_dim(cells, 0, width, axis=dim)
        tail = lax.slice_in_dim(cells, cells.shape[dim] - width, cells.shape[dim], axis=dim)
        cells = jnp.concatenate(
            [
                lax.ppermute(tail, axis, [(i, (i + 1) % count) for i in range(ends)]),
                cells,
                lax.ppermute(head, axis, [((i + 1) % count, i) for i in range(ends)]),
            ],
            axis=dim,
        )
    return cells


def shifted(values, shifts):
    window = tuple(
        (
            slice(1 + offset, values.shape[dimension] - 1 + offset)
            for dimension, offset in enumerate(shifts)
        )
    )
    return values[window]


def stiffness(displace, shear_ext, normal_ext):
    padded = jnp.pad(displace, ((0, 0), (0, 0), (1, 1), (1, 1), (0, 0)))
    shear_pad = jnp.pad(shear_ext, ((0, 0), (1, 1), (1, 1)))
    normal_pad = jnp.pad(normal_ext, ((0, 0), (1, 1), (1, 1)))
    results = []
    for component in range(3):
        moving = padded[:, component]
        centre = shifted(moving, (0, 0, 0))
        accumulated = jnp.zeros_like(centre)
        for dimension in range(3):
            coefficient = normal_pad if dimension == component else shear_pad
            middle = shifted(coefficient, (0, 0, 0))
            for direction in (-1, 1):
                offsets = tuple((direction if another == dimension else 0 for another in range(3)))
                facing = 0.5 * (middle + shifted(coefficient, offsets))
                accumulated = accumulated + facing[..., None] * (centre - shifted(moving, offsets))
        results.append(accumulated)
    return jnp.stack(results, axis=1)


def lookup(labels, shear_modulus, stiff_ratio):
    onehot = (labels[..., None] == jnp.arange(shear_modulus.shape[0], dtype=jnp.int32)).astype(
        jnp.float32
    )
    shear_node = jnp.sum(onehot * shear_modulus, axis=-1)
    normal_node = jnp.sum(onehot * (shear_modulus * (2.0 + stiff_ratio)), axis=-1)
    return (shear_node, normal_node)


def body(
    applied_loads,
    labels,
    shear_modulus,
    stiff_ratio,
    local_order,
    local_inverse,
    coarse_basis,
    coarse_inverse,
):
    planes, components, node_count, load_cases = applied_loads.shape
    forces = applied_loads.reshape(planes, 3, NY, NZ, load_cases)
    shear_node, normal_node = lookup(labels, shear_modulus, stiff_ratio)
    materials = jnp.stack(
        [shear_node.reshape(planes, NY, NZ), normal_node.reshape(planes, NY, NZ)], axis=1
    )
    ordering = local_order[0]
    inverse = local_inverse[0]
    coarse_local = coarse_basis[0]
    subdomain = (planes + 2) * 3 * node_count
    unknown_rank = (
        jnp.zeros((subdomain,), jnp.int32).at[ordering].set(jnp.arange(subdomain, dtype=jnp.int32))
    )
    natural_inverse = jnp.take(jnp.take(inverse, unknown_rank, axis=0), unknown_rank, axis=1)
    material_ext = padded_2(materials, ((("sub", "grp"), 0),), 2)
    shear_ext = material_ext[:, 0]
    normal_ext = material_ext[:, 1]
    loads_ext = padded_2(forces, ((("sub", "grp"), 0),), 1)
    position = lax.axis_index(("sub", "grp"))
    chain_length = lax.axis_size(("sub", "grp"))
    inside = jnp.concatenate(
        [
            (position > 0).astype(jnp.float32)[None],
            jnp.ones((planes,), jnp.float32),
            (position < chain_length - 1).astype(jnp.float32)[None],
        ]
    )
    inside = inside[:, None, None, None, None]

    def deep_rim(solution):
        return padded_2(solution, ((("sub", "grp"), 0),), 2)

    def subdomain_residual(solution, initial):
        if initial:
            return loads_ext * inside
        extended = deep_rim(solution)
        return (loads_ext - stiffness(extended, shear_ext, normal_ext)) * inside

    own_rows = lax.dynamic_slice_in_dim(coarse_inverse, lax.axis_index("grp") * CV_DEV, CV_DEV, 0)
    solution = jnp.zeros_like(forces)
    coarse_values = jnp.zeros((CV_DEV, load_cases), jnp.float32)
    for iteration in range(ITERS):
        window = subdomain_residual(solution, iteration == 0)
        flattened = window.reshape(subdomain, load_cases)
        coarse_res = jnp.dot(coarse_local, flattened, precision=PRECISE)
        coarse_values = jnp.dot(
            own_rows,
            lax.all_gather(coarse_res, ("sub", "grp"), axis=0, tiled=True),
            precision=PRECISE,
        )
        rounded = flattened.astype(jnp.bfloat16)
        spread = jnp.dot(natural_inverse, rounded, preferred_element_type=jnp.float32)
        spread = spread + jnp.dot(coarse_local.T, coarse_values, precision=PRECISE)
        spread = spread.reshape(planes + 2, 3, NY, NZ, load_cases)
        beside_all = padded_2(spread, ((("sub", "grp"), 0),), 1)
        update = spread[1 : planes + 1]
        update = update.at[0].add(beside_all[0])
        update = update.at[planes - 1].add(beside_all[-1])
        solution = solution + RELAXATION * update
    extended = deep_rim(solution)
    final_residual = forces - stiffness(extended[1:-1], shear_ext[1:-1], normal_ext[1:-1])
    return (
        solution.reshape(planes, 3, node_count, load_cases),
        final_residual.reshape(planes, 3, node_count, load_cases),
        coarse_values,
    )


def solution(mesh):
    return jax.shard_map(
        body,
        mesh=mesh,
        in_specs=(
            P(("sub", "grp"), None, None, None),
            P(("sub", "grp"), None),
            P(),
            P(),
            P(("sub", "grp"), None),
            P(("sub", "grp"), None, None),
            P(("sub", "grp"), None, None),
            P("sub", None),
        ),
        out_specs=(
            P(("sub", "grp"), None, None, None),
            P(("sub", "grp"), None, None, None),
            P(("sub", "grp"), None),
        ),
        check_vma=False,
    )
```

profile of v0, /device:TPU:0, one launch (start us, length us, event | category | flops | bytes accessed | tf_op | source)
XLA Modules:
  0.0 231.9 jit_solution(4371102149384256069)
XLA Ops:
  1.8 2.4 %collective-permute-start = (f32[1,3,8,8,128]{4,3,2,1,0:T(8,128)S(1)}, f32[1,3,8,8,128]{4,3,2,1,0:T(8,128)S(1)}, u32[]{:S(2)}, u32[]{:S(2)}) collective-permute-start(f32[1,3,8,8,128]{4,3,2,1,0:T(8,128)S(1)} %get-tuple-element.116), channel_id=1, source_target_pairs={{0,1},{1,2},{2,3},{3,4},{4,5},{5,6},{6,7},{7,8},{8,9},{9,10},{10,1... | collective-permute-start | bytes 294920 | tf_op jit(solution)/shard_map/ppermute | solution.py:24
  7.1 5.1 %collective-permute-start.4 = (f32[2,2,8,8]{3,2,0,1:T(8,128)S(1)}, f32[2,2,8,8]{3,2,0,1:T(8,128)S(1)}, u32[]{:S(2)}, u32[]{:S(2)}) collective-permute-start(f32[2,2,8,8]{3,2,0,1:T(8,128)S(1)} %get-tuple-element.152), channel_id=1, source_target_pairs={{0,1},{1,2},{2,3},{3,4},{4,5},{5,6},{6,7},{7,8},{8,9},{9,10},{10,1... | collective-permute-start | bytes 3080 | tf_op jit(solution)/shard_map/ppermute | solution.py:24
  12.2 1.3 collective-permute-start.5
  14.2 6.4 %scatter_custom_fusion = s32[1152]{0:T(1024)S(1)} fusion(s32[1152]{0:T(1024)S(1)} %fusion.190, s32[1152]{0:T(1024)S(1)} %iota.7, s32[]{:T(128)} %constant.179.clone.1), kind=kCustom, calls=%fused_computation.347 | custom fusion | bytes 4612 | tf_op jit(solution)/shard_map/scatter | solution.py:93
  20.8 5.1 %gather_fusion = bf16[1152,1152]{1,0:T(8,128)(2,1)} fusion(bf16[1152,1152]{1,0:T(8,128)(2,1)S(1)} %bitcast.236, s32[2048]{0:T(1024)S(1)} %pad_clamp_fusion), kind=kCustom, calls=%fused_computation | custom fusion | bytes 5313024 | tf_op jit(solution)/shard_map/jit(_take)/gather | solution.py:95
  25.9 3.6 %broadcast_select_fusion = bf16[1152,1152]{1,0:T(8,128)(2,1)} fusion(bf16[1152,1152]{1,0:T(8,128)(2,1)} %gather_fusion, pred[1152]{0:T(1024)(128)(4,1)S(1)} %compare_and_fusion), kind=kLoop, calls=%fused_computation.7 | loop fusion | flops 1327104 | bytes 5309568 | tf_op jit(solution)/shard_map/jit(_take)/select_n | solution.py:95
  29.8 5.2 %copy.73 = bf16[1152,1152]{0,1:T(8,128)(2,1)} copy(bf16[1152,1152]{1,0:T(8,128)(2,1)} %broadcast_select_fusion) | data formatting | bytes 5308416 | tf_op jit(solution)/shard_map/jit(_take)/select_n | solution.py:95
  35.0 9.2 %gather_fusion.1 = bf16[1152,1152]{1,0:T(8,128)(2,1)} fusion(bf16[1152,1152]{0,1:T(8,128)(2,1)} %copy.73, s32[2048]{0:T(1024)S(1)} %pad_clamp_fusion), kind=kCustom, calls=%fused_computation.1 | custom fusion | bytes 5313024 | tf_op jit(solution)/shard_map/jit(_take)/gather | solution.py:95
  46.6 44.4 %all-gather = f32[32,4,128]{2,1,0:T(4,128)S(1)} all-gather(f32[1,4,128]{2,1,0:T(4,128)S(1)} %convolution_bitcast_fusion.5), channel_id=1, replica_groups=mesh['sub'=16,'grp'=2] {'sub','grp'}, dimensions={0}, use_global_device_ids=true | all-gather | bytes 67584 | tf_op jit(solution)/shard_map/all_gather | solution.py:129
  93.8 2.2 collective-permute-start.2
  97.7 1.9 collective-permute-done.3
  99.7 4.7 %collective-permute-start.6 = (f32[2,3,8,8,128]{4,3,2,0,1:T(8,128)S(1)}, f32[2,3,8,8,128]{4,3,2,0,1:T(8,128)S(1)}, u32[]{:S(2)}, u32[]{:S(2)}) collective-permute-start(f32[2,3,8,8,128]{4,3,2,0,1:T(8,128)S(1)} %get-tuple-element.114), channel_id=1, source_target_pairs={{0,1},{1,2},{2,3},{3,4},{4,5},{5,6},{6,7},{7,8},{8,9},{9,10},{10,1... | collective-permute-start | bytes 589832 | tf_op jit(solution)/shard_map/ppermute | solution.py:24
  105.7 1.9 collective-permute-done.7
  110.4 40.3 %all-gather.1 = f32[32,4,128]{2,1,0:T(4,128)S(1)} all-gather(f32[1,4,128]{2,1,0:T(4,128)S(1)} %convolution_bitcast_fusion.4), channel_id=1, replica_groups=mesh['sub'=16,'grp'=2] {'sub','grp'}, dimensions={0}, use_global_device_ids=true | all-gather | bytes 67584 | tf_op jit(solution)/shard_map/all_gather | solution.py:129
  153.2 2.2 collective-permute-start.8
  155.6 1.3 collective-permute-start.9
  156.9 1.9 collective-permute-done.9
  160.4 5.3 %collective-permute-start.10 = (f32[2,3,8,8,128]{4,3,2,0,1:T(8,128)}, f32[2,3,8,8,128]{4,3,2,0,1:T(8,128)}, u32[]{:S(2)}, u32[]{:S(2)}) collective-permute-start(f32[2,3,8,8,128]{4,3,2,0,1:T(8,128)} %get-tuple-element.112), channel_id=1, source_target_pairs={{0,1},{1,2},{2,3},{3,4},{4,5},{5,6},{6,7},{7,8},{8,9},{9,10},{10,1... | collective-permute-start | bytes 589832 | tf_op jit(solution)/shard_map/ppermute | solution.py:24
  167.0 1.4 slice.826
  169.4 1.4 select_maximum_fusion
  173.9 39.6 %all-gather.2 = f32[32,4,128]{2,1,0:T(4,128)S(1)} all-gather(f32[1,4,128]{2,1,0:T(4,128)S(1)} %convolution_bitcast_fusion.3), channel_id=1, replica_groups=mesh['sub'=16,'grp'=2] {'sub','grp'}, dimensions={0}, use_global_device_ids=true | all-gather | bytes 67584 | tf_op jit(solution)/shard_map/all_gather | solution.py:129
  216.0 2.4 %collective-permute-start.12 = (f32[1,3,8,8,128]{4,3,2,0,1:T(8,128)S(1)}, f32[1,3,8,8,128]{4,3,2,0,1:T(8,128)S(1)}, u32[]{:S(2)}, u32[]{:S(2)}) collective-permute-start(f32[1,3,8,8,128]{4,3,2,0,1:T(8,128)S(1)} %bitcast.257), channel_id=1, source_target_pairs={{0,1},{1,2},{2,3},{3,4},{4,5},{5,6},{6,7},{7,8},{8,9},{9,10},{10,1... | collective-permute-start | bytes 294920 | tf_op jit(solution)/shard_map/ppermute | solution.py:24
  219.9 1.9 collective-permute-done.13
  221.9 4.7 %collective-permute-start.14 = (f32[2,3,8,8,128]{4,3,2,0,1:T(8,128)S(1)}, f32[2,3,8,8,128]{4,3,2,0,1:T(8,128)S(1)}, u32[]{:S(2)}, u32[]{:S(2)}) collective-permute-start(f32[2,3,8,8,128]{4,3,2,0,1:T(8,128)S(1)} %get-tuple-element.110), channel_id=1, source_target_pairs={{0,1},{1,2},{2,3},{3,4},{4,5},{5,6},{6,7},{7,8},{8,9},{9,10},{10,1... | collective-permute-start | bytes 589832 | tf_op jit(solution)/shard_map/ppermute | solution.py:24
  (205 shorter events, 34.0 us)
Async XLA Ops:
  1.8 42.6 %collective-permute-start = (f32[1,3,8,8,128]{4,3,2,1,0:T(8,128)S(1)}, f32[1,3,8,8,128]{4,3,2,1,0:T(8,128)S(1)}, u32[]{:S(2)}, u32[]{:S(2)}) collective-permute-start(f32[1,3,8,8,128]{4,3,2,1,0:T(8,128)S(1)} %get-tuple-element.116), channel_id=1, source_target_pairs={{0,1},{1,2},{2,3},{3,4},{4,5},{5,6},{6,7},{7,8},{8,9},{9,10},{10,1... | collective-permute-start | bytes 294920 | tf_op jit(solution)/shard_map/ppermute | solution.py:24
  4.1 40.2 %collective-permute-start.1 = (f32[1,3,8,8,128]{4,3,2,1,0:T(8,128)S(1)}, f32[1,3,8,8,128]{4,3,2,1,0:T(8,128)S(1)}, u32[]{:S(2)}, u32[]{:S(2)}) collective-permute-start(f32[1,3,8,8,128]{4,3,2,1,0:T(8,128)S(1)} %get-tuple-element.117), channel_id=1, source_target_pairs={{1,0},{2,1},{3,2},{4,3},{5,4},{6,5},{7,6},{8,7},{9,8},{10,9},{11,1... | collective-permute-start | bytes 294920 | tf_op jit(solution)/shard_map/ppermute | solution.py:26
  7.1 37.2 %copy-start.8 = (f32[4,2,8,8]{3,2,0,1:T(8,128)}, f32[4,2,8,8]{3,2,0,1:T(8,128)S(1)}, u32[]{:S(2)}) copy-start(f32[4,2,8,8]{3,2,0,1:T(8,128)S(1)} %constant_dynamic-update-slice_fusion) | copy-start | bytes 6148
  7.1 37.2 %collective-permute-start.4 = (f32[2,2,8,8]{3,2,0,1:T(8,128)S(1)}, f32[2,2,8,8]{3,2,0,1:T(8,128)S(1)}, u32[]{:S(2)}, u32[]{:S(2)}) collective-permute-start(f32[2,2,8,8]{3,2,0,1:T(8,128)S(1)} %get-tuple-element.152), channel_id=1, source_target_pairs={{0,1},{1,2},{2,3},{3,4},{4,5},{5,6},{6,7},{7,8},{8,9},{9,10},{10,1... | collective-permute-start | bytes 3080 | tf_op jit(solution)/shard_map/ppermute | solution.py:24
  12.2 32.1 %collective-permute-start.5 = (f32[2,2,8,8]{3,2,0,1:T(8,128)S(1)}, f32[2,2,8,8]{3,2,0,1:T(8,128)S(1)}, u32[]{:S(2)}, u32[]{:S(2)}) collective-permute-start(f32[2,2,8,8]{3,2,0,1:T(8,128)S(1)} %get-tuple-element.153), channel_id=1, source_target_pairs={{1,0},{2,1},{3,2},{4,3},{5,4},{6,5},{7,6},{8,7},{9,8},{10,9},{11,1... | collective-permute-start | bytes 3080 | tf_op jit(solution)/shard_map/ppermute | solution.py:26
  29.8 62.6 %copy-start.39 = (f32[1152]{0:T(1024)}, f32[1152]{0:T(1024)S(1)}, u32[]{:S(2)}) copy-start(f32[1152]{0:T(1024)S(1)} %mul.276) | copy-start | bytes 13828
  44.2 46.8 %copy-start.48 = (f32[8,128]{1,0:T(8,128)S(1)}, f32[8,128]{1,0:T(8,128)}, u32[]{:S(2)}) copy-start(f32[8,128]{1,0:T(8,128)} %param.27) | copy-start | bytes 12292
  44.9 47.7 %copy-start.5 = (bf16[1152,1152]{1,0:T(8,128)(2,1)S(1)}, bf16[1152,1152]{1,0:T(8,128)(2,1)}, u32[]{:S(2)}) copy-start(bf16[1152,1152]{1,0:T(8,128)(2,1)} %gather_fusion.1) | copy-start | bytes 7962628
  44.9 47.7 %copy-start.51 = (pred[1152]{0:T(1024)(128)(4,1)S(1)}, pred[1152]{0:T(1024)(128)(4,1)}, u32[]{:S(2)}) copy-start(pred[1152]{0:T(1024)(128)(4,1)} %copy-done.50) | copy-start | bytes 3460
  93.8 3.8 %collective-permute-start.2 = (f32[1,3,8,8,128]{4,3,2,0,1:T(8,128)S(1)}, f32[1,3,8,8,128]{4,3,2,0,1:T(8,128)S(1)}, u32[]{:S(2)}, u32[]{:S(2)}) collective-permute-start(f32[1,3,8,8,128]{4,3,2,0,1:T(8,128)S(1)} %bitcast.254), channel_id=1, source_target_pairs={{0,1},{1,2},{2,3},{3,4},{4,5},{5,6},{6,7},{7,8},{8,9},{9,10},{10,1... | collective-permute-start | bytes 294920 | tf_op jit(solution)/shard_map/ppermute | solution.py:24
  96.4 3.2 %collective-permute-start.3 = (f32[1,3,8,8,128]{4,3,2,0,1:T(8,128)S(1)}, f32[1,3,8,8,128]{4,3,2,0,1:T(8,128)S(1)}, u32[]{:S(2)}, u32[]{:S(2)}) collective-permute-start(f32[1,3,8,8,128]{4,3,2,0,1:T(8,128)S(1)} %bitcast.253), channel_id=1, source_target_pairs={{1,0},{2,1},{3,2},{4,3},{5,4},{6,5},{7,6},{8,7},{9,8},{10,9},{11,1... | collective-permute-start | bytes 294920 | tf_op jit(solution)/shard_map/ppermute | solution.py:26
  99.7 6.1 %collective-permute-start.6 = (f32[2,3,8,8,128]{4,3,2,0,1:T(8,128)S(1)}, f32[2,3,8,8,128]{4,3,2,0,1:T(8,128)S(1)}, u32[]{:S(2)}, u32[]{:S(2)}) collective-permute-start(f32[2,3,8,8,128]{4,3,2,0,1:T(8,128)S(1)} %get-tuple-element.114), channel_id=1, source_target_pairs={{0,1},{1,2},{2,3},{3,4},{4,5},{5,6},{6,7},{7,8},{8,9},{9,10},{10,1... | collective-permute-start | bytes 589832 | tf_op jit(solution)/shard_map/ppermute | solution.py:24
  104.3 3.3 %collective-permute-start.7 = (f32[2,3,8,8,128]{4,3,2,0,1:T(8,128)S(1)}, f32[2,3,8,8,128]{4,3,2,0,1:T(8,128)S(1)}, u32[]{:S(2)}, u32[]{:S(2)}) collective-permute-start(f32[2,3,8,8,128]{4,3,2,0,1:T(8,128)S(1)} %get-tuple-element.115), channel_id=1, source_target_pairs={{1,0},{2,1},{3,2},{4,3},{5,4},{6,5},{7,6},{8,7},{9,8},{10,9},{11,1... | collective-permute-start | bytes 589832 | tf_op jit(solution)/shard_map/ppermute | solution.py:26
  153.2 3.6 %collective-permute-start.8 = (f32[1,3,8,8,128]{4,3,2,0,1:T(8,128)S(1)}, f32[1,3,8,8,128]{4,3,2,0,1:T(8,128)S(1)}, u32[]{:S(2)}, u32[]{:S(2)}) collective-permute-start(f32[1,3,8,8,128]{4,3,2,0,1:T(8,128)S(1)} %bitcast.258), channel_id=1, source_target_pairs={{0,1},{1,2},{2,3},{3,4},{4,5},{5,6},{6,7},{7,8},{8,9},{9,10},{10,1... | collective-permute-start | bytes 294920 | tf_op jit(solution)/shard_map/ppermute | solution.py:24
  155.6 3.2 %collective-permute-start.9 = (f32[1,3,8,8,128]{4,3,2,0,1:T(8,128)S(1)}, f32[1,3,8,8,128]{4,3,2,0,1:T(8,128)S(1)}, u32[]{:S(2)}, u32[]{:S(2)}) collective-permute-start(f32[1,3,8,8,128]{4,3,2,0,1:T(8,128)S(1)} %bitcast.256), channel_id=1, source_target_pairs={{1,0},{2,1},{3,2},{4,3},{5,4},{6,5},{7,6},{8,7},{9,8},{10,9},{11,1... | collective-permute-start | bytes 294920 | tf_op jit(solution)/shard_map/ppermute | solution.py:26
  160.4 8.7 %collective-permute-start.10 = (f32[2,3,8,8,128]{4,3,2,0,1:T(8,128)}, f32[2,3,8,8,128]{4,3,2,0,1:T(8,128)}, u32[]{:S(2)}, u32[]{:S(2)}) collective-permute-start(f32[2,3,8,8,128]{4,3,2,0,1:T(8,128)} %get-tuple-element.112), channel_id=1, source_target_pairs={{0,1},{1,2},{2,3},{3,4},{4,5},{5,6},{6,7},{7,8},{8,9},{9,10},{10,1... | collective-permute-start | bytes 589832 | tf_op jit(solution)/shard_map/ppermute | solution.py:24
  165.7 3.7 %collective-permute-start.11 = (f32[2,3,8,8,128]{4,3,2,0,1:T(8,128)}, f32[2,3,8,8,128]{4,3,2,0,1:T(8,128)}, u32[]{:S(2)}, u32[]{:S(2)}) collective-permute-start(f32[2,3,8,8,128]{4,3,2,0,1:T(8,128)} %get-tuple-element.113), channel_id=1, source_target_pairs={{1,0},{2,1},{3,2},{4,3},{5,4},{6,5},{7,6},{8,7},{9,8},{10,9},{11,1... | collective-permute-start | bytes 589832 | tf_op jit(solution)/shard_map/ppermute | solution.py:26
  173.0 40.5 %copy-start.49 = (f32[8,128]{1,0:T(8,128)S(1)}, f32[8,128]{1,0:T(8,128)}, u32[]{:S(2)}) copy-start(f32[8,128]{1,0:T(8,128)} %param.27) | copy-start | bytes 12292
  173.2 41.6 %copy-start.6 = (bf16[1152,1152]{1,0:T(8,128)(2,1)S(1)}, bf16[1152,1152]{1,0:T(8,128)(2,1)}, u32[]{:S(2)}) copy-start(bf16[1152,1152]{1,0:T(8,128)(2,1)} %gather_fusion.1) | copy-start | bytes 7962628
  173.2 41.6 %copy-start.52 = (pred[1152]{0:T(1024)(128)(4,1)S(1)}, pred[1152]{0:T(1024)(128)(4,1)}, u32[]{:S(2)}) copy-start(pred[1152]{0:T(1024)(128)(4,1)} %copy-done.50) | copy-start | bytes 3460
  216.0 3.8 %collective-permute-start.12 = (f32[1,3,8,8,128]{4,3,2,0,1:T(8,128)S(1)}, f32[1,3,8,8,128]{4,3,2,0,1:T(8,128)S(1)}, u32[]{:S(2)}, u32[]{:S(2)}) collective-permute-start(f32[1,3,8,8,128]{4,3,2,0,1:T(8,128)S(1)} %bitcast.257), channel_id=1, source_target_pairs={{0,1},{1,2},{2,3},{3,4},{4,5},{5,6},{6,7},{7,8},{8,9},{9,10},{10,1... | collective-permute-start | bytes 294920 | tf_op jit(solution)/shard_map/ppermute | solution.py:24
  218.5 3.2 %collective-permute-start.13 = (f32[1,3,8,8,128]{4,3,2,0,1:T(8,128)S(1)}, f32[1,3,8,8,128]{4,3,2,0,1:T(8,128)S(1)}, u32[]{:S(2)}, u32[]{:S(2)}) collective-permute-start(f32[1,3,8,8,128]{4,3,2,0,1:T(8,128)S(1)} %bitcast.255), channel_id=1, source_target_pairs={{1,0},{2,1},{3,2},{4,3},{5,4},{6,5},{7,6},{8,7},{9,8},{10,9},{11,1... | collective-permute-start | bytes 294920 | tf_op jit(solution)/shard_map/ppermute | solution.py:26
  221.9 6.9 %collective-permute-start.14 = (f32[2,3,8,8,128]{4,3,2,0,1:T(8,128)S(1)}, f32[2,3,8,8,128]{4,3,2,0,1:T(8,128)S(1)}, u32[]{:S(2)}, u32[]{:S(2)}) collective-permute-start(f32[2,3,8,8,128]{4,3,2,0,1:T(8,128)S(1)} %get-tuple-element.110), channel_id=1, source_target_pairs={{0,1},{1,2},{2,3},{3,4},{4,5},{5,6},{6,7},{7,8},{8,9},{9,10},{10,1... | collective-permute-start | bytes 589832 | tf_op jit(solution)/shard_map/ppermute | solution.py:24
  226.6 3.3 %collective-permute-start.15 = (f32[2,3,8,8,128]{4,3,2,0,1:T(8,128)S(1)}, f32[2,3,8,8,128]{4,3,2,0,1:T(8,128)S(1)}, u32[]{:S(2)}, u32[]{:S(2)}) collective-permute-start(f32[2,3,8,8,128]{4,3,2,0,1:T(8,128)S(1)} %get-tuple-element.111), channel_id=1, source_target_pairs={{1,0},{2,1},{3,2},{4,3},{5,4},{6,5},{7,6},{8,7},{9,8},{10,9},{11,1... | collective-permute-start | bytes 589832 | tf_op jit(solution)/shard_map/ppermute | solution.py:26
  (46 other events, 248.1 us)
where the time goes:
time: 236 us; the launch traced here: 232 us
  blocking collectives  124 us (53%)
  starting transfers between devices  39.3 us (17%)
  local copies, waits for them, and re-layouts  34.1 us (14%)
  other arithmetic  14.5 us (6%)
  waiting for transfers between devices  8.99 us (4%)
  matrix products  8.73 us (4%)
    all_gather x3, blocking collectives, body(): lax.all_gather(coarse_res, ('sub', 'grp'), axis=0, tiled=True)  124 us
    ppermute x8, starting transfers between devices, padded_2(): lax.ppermute(tail, axis, [(i, (i + 1) % count) for i in range(ends)])  29 us
    ppermute x8, starting transfers between devices, padded_2(): lax.ppermute(head, axis, [((i + 1) % count, i) for i in range(ends)])  10.3 us
    gather x1, local copies, waits for them, and re-layouts, body(): jnp.take(jnp.take(inverse, unknown_rank, axis=0), unknown_rank, axis=1)  9.22 us
    ppermute x8, waiting for transfers between devices, padded_2(): lax.ppermute(head, axis, [((i + 1) % count, i) for i in range(ends)])  8.97 us
    scatter x1, local copies, waits for them, and re-layouts, body(): jnp.zeros((subdomain,), jnp.int32).at[ordering]  6.45 us
    select_n x1, local copies, waits for them, and re-layouts, body(): jnp.take(inverse, unknown_rank, axis=0)  5.24 us
    gather x1, local copies, waits for them, and re-layouts, body(): jnp.take(inverse, unknown_rank, axis=0)  5.11 us
  transfers between devices with their start and end apart: 16, of which 6 were waited for; matrix products, arithmetic and copies ran while one was open for 15% of the time, Pallas kernels for 0%

commit v1 on v0

v1 whole, which is shorter than its diff:
```python
import functools

import jax
import jax.numpy as jnp
from jax import lax
from jax.experimental import pallas as pl
from jax.experimental.pallas import tpu as pltpu
from jax.sharding import PartitionSpec as P

NY = 8
NZ = 8
CV_DEV = 4
ITERS = 3
RELAXATION = 0.5
AXES = ("sub", "grp")
F32 = jnp.float32
BF16 = jnp.bfloat16
VMEM = pl.BlockSpec(memory_space=pltpu.VMEM)
SMEM = pl.BlockSpec(memory_space=pltpu.SMEM)
PARAMS = pltpu.CompilerParams(vmem_limit_bytes=40 * 1024 * 1024)


def lookup(labels, shear_modulus, stiff_ratio):
    onehot = (labels[..., None] == jnp.arange(shear_modulus.shape[0], dtype=jnp.int32)).astype(F32)
    shear_node = jnp.sum(onehot * shear_modulus, axis=-1)
    normal_node = jnp.sum(onehot * (shear_modulus * (2.0 + stiff_ratio)), axis=-1)
    return shear_node, normal_node


def swap_pairs(count):
    near = [(i, i ^ 1) for i in range(count)]
    far = []
    for i in range(1, count - 1, 2):
        far += [(i, i + 1), (i + 1, i)]
    return near, far


def renumber_kernel(order_ref, inverse_ref, out_ref, hot):
    size = inverse_ref.shape[0]
    step = size // 3
    order = order_ref[...]

    def build(i, carry):
        start = pl.multiple_of(i * step, step)
        row = lax.broadcasted_iota(jnp.int32, (step, size), 0) + start
        hot[pl.ds(start, step), :] = jnp.where(row == order, 1.0, 0.0).astype(BF16)
        return carry

    lax.fori_loop(0, 3, build, 0)
    for i in range(3):
        part = slice(i * step, (i + 1) * step)
        columns = lax.dot_general(
            inverse_ref[...], hot[part, :], (((1,), (1,)), ((), ())), preferred_element_type=F32
        ).astype(BF16)
        out_ref[:, part] = jnp.dot(hot[...], columns, preferred_element_type=F32).astype(BF16)


def renumber(order, inverse):
    size = inverse.shape[0]
    return pl.pallas_call(
        renumber_kernel,
        out_shape=jax.ShapeDtypeStruct((size, size), BF16),
        in_specs=[VMEM, VMEM],
        out_specs=VMEM,
        scratch_shapes=[pltpu.VMEM((size, size), BF16)],
        compiler_params=PARAMS,
        cost_estimate=pl.CostEstimate(flops=4 * size**3, bytes_accessed=4 * size * size, transcendentals=0),
    )(order, inverse)


def up_a(u):
    return jnp.concatenate([u[1:], jnp.zeros_like(u[:1])], axis=0)


def down_a(u):
    return jnp.concatenate([jnp.zeros_like(u[:1]), u[:-1]], axis=0)


def up_b(u):
    return pltpu.roll(u, NZ - 1, 1)


def down_b(u):
    return pltpu.roll(u, 1, 1)


def stencil_plane(mats, plane, field):
    b = lax.broadcasted_iota(jnp.int32, (NY, NZ, mats.shape[-1]), 1)
    last, first = b == NZ - 1, b == 0
    near_a, near_b_up, near_b_down, along, diagonal = [], [], [], [], []
    for kind in range(2):
        s = mats[plane, kind]
        half = 0.5 * s
        k_up = 0.5 * up_a(s) + half
        k_down = 0.5 * down_a(s) + half
        b_up = jnp.where(last, 0.0, 0.5 * up_b(s) + half)
        b_down = jnp.where(first, 0.0, 0.5 * down_b(s) + half)
        p_up = 0.5 * mats[plane + 1, kind] + half
        p_down = 0.5 * mats[plane - 1, kind] + half
        near_a.append((k_up, k_down))
        near_b_up.append(b_up)
        near_b_down.append(b_down)
        along.append((p_up, p_down))
        edge = jnp.where(last | first, half, 0.0)
        diagonal.append((p_up + p_down, k_up + k_down, b_up + b_down + edge))
    results = []
    for component in range(3):
        kinds = [1 if dimension == component else 0 for dimension in range(3)]
        u = field(plane, component)
        total = (diagonal[kinds[0]][0] + diagonal[kinds[1]][1] + diagonal[kinds[2]][2]) * u
        total = total - along[kinds[0]][0] * field(plane + 1, component)
        total = total - along[kinds[0]][1] * field(plane - 1, component)
        total = total - near_a[kinds[1]][0] * up_a(u)
        total = total - near_a[kinds[1]][1] * down_a(u)
        total = total - near_b_up[kinds[2]] * up_b(u)
        total = total - near_b_down[kinds[2]] * down_b(u)
        results.append(total)
    return results


def split(x):
    high = x.astype(BF16)
    return high, (x - high.astype(F32)).astype(BF16)


def products(place_ref, inverse_ref, basis_ref, res_ref, t_ref, near_ref, far_ref, q_ref):
    slots, rows, cases = res_ref.shape[0] * 3, NY * NZ, res_ref.shape[-1]
    size = slots * rows
    res = res_ref[...].reshape(size, cases)
    high, low = split(res)
    step = size // 3
    t_planes = t_ref.shape[0]
    for i in range(3):
        block = jnp.dot(inverse_ref[i * step : (i + 1) * step, :], high, preferred_element_type=F32)
        per = t_planes // 3
        t_ref[i * per : (i + 1) * per] = block.reshape(per, 3, NY, NZ, cases)
    even = place_ref[0]
    width = near_ref.shape[0]
    to_right = t_planes - width
    near_ref[...] = t_ref[pl.ds(to_right * even, width)]
    far_ref[...] = t_ref[pl.ds(to_right * (1 - even), width)]
    b_high, b_low = split(basis_ref[...])
    both = jnp.concatenate([b_high, b_low], axis=0)
    first = jnp.dot(both, high, preferred_element_type=F32)
    second = jnp.dot(both, low, preferred_element_type=F32)
    half = basis_ref.shape[0]
    q = (first[:half] + second[:half] + first[half:])[:CV_DEV]
    q_ref[...] = jnp.broadcast_to(q[None], q_ref.shape)


def first_kernel(place_ref, loads_ref, left_ref, right_ref, inverse_ref, basis_ref,
                 res_ref, t_ref, near_ref, far_ref, q_ref):
    planes = loads_ref.shape[0]
    res_ref[0] = left_ref[...]
    res_ref[1 : planes + 1] = loads_ref[...]
    res_ref[planes + 1] = right_ref[...]
    products(place_ref, inverse_ref, basis_ref, res_ref, t_ref, near_ref, far_ref, q_ref)


def correction(place_ref, q_ref, rows_ref, extent_ref, t_ref, near_ref, far_ref, z_ref):
    width = near_ref.shape[0]
    out_planes = t_ref.shape[0] + 2
    cases = t_ref.shape[-1]
    coarse = jnp.dot(rows_ref[...], q_ref[...], precision=lax.Precision.HIGHEST, preferred_element_type=F32)
    c_high, c_low = split(coarse)
    e_high, e_low = split(extent_ref[...])
    spread = lax.dot_general(
        jnp.concatenate([e_high, e_low, e_high], axis=0),
        jnp.concatenate([c_high, c_high, c_low], axis=0),
        (((0,), (0,)), ((), ())),
        preferred_element_type=F32,
    ).reshape(out_planes, 3, NY, NZ, cases)
    even = place_ref[0] == 1
    has_left = place_ref[1].astype(F32)
    has_right = place_ref[2].astype(F32)
    for plane in range(3 - width, out_planes - 3 + width):
        value = spread[plane]
        if 1 <= plane < out_planes - 1:
            value = value + t_ref[plane - 1]
        if plane < 3:
            at = plane - (3 - width)
            value = value + jnp.where(even, far_ref[at], near_ref[at])
        if plane >= out_planes - 3:
            at = plane - (out_planes - 3)
            value = value + jnp.where(even, near_ref[at], far_ref[at])
        if plane < 2:
            value = value * has_left
        if plane >= out_planes - 2:
            value = value * has_right
        z_ref[plane] = value
    return coarse


def middle_kernel(with_solution, place_ref, q_in_ref, rows_ref, extent_ref, mats_ref, t_in_ref, near_in_ref,
                  far_in_ref, res_in_ref, *rest):
    if with_solution:
        solution_in_ref, *rest = rest
    inverse_ref, basis_ref, solution_ref, res_ref, t_ref, near_ref, far_ref, q_ref, z_ref = rest
    correction(place_ref, q_in_ref, rows_ref, extent_ref, t_in_ref, near_in_ref, far_in_ref, z_ref)
    window = res_ref.shape[0]
    for plane in range(1, window + 1):
        applied = stencil_plane(mats_ref, plane, lambda p, c: z_ref[p, c])
        for component in range(3):
            value = res_in_ref[plane - 1, component] - RELAXATION * applied[component]
            if plane == 1:
                value = value * place_ref[1].astype(F32)
            if plane == window:
                value = value * place_ref[2].astype(F32)
            res_ref[plane - 1, component] = value
    own = RELAXATION * z_ref[2 : window]
    solution_ref[...] = solution_in_ref[...] + own if with_solution else own
    products(place_ref, inverse_ref, basis_ref, res_ref, t_ref, near_ref, far_ref, q_ref)


def last_kernel(place_ref, q_in_ref, rows_ref, extent_ref, mats_ref, t_in_ref, near_in_ref, far_in_ref, res_in_ref,
                solution_in_ref, solution_ref, residual_ref, coarse_ref, z_ref):
    coarse = correction(place_ref, q_in_ref, rows_ref, extent_ref, t_in_ref, near_in_ref, far_in_ref, z_ref)
    coarse_ref[...] = coarse[CV_DEV : 2 * CV_DEV]
    planes = solution_ref.shape[0]
    for plane in range(2, planes + 2):
        applied = stencil_plane(mats_ref, plane, lambda p, c: z_ref[p, c])
        for component in range(3):
            residual_ref[plane - 2, component] = (
                res_in_ref[plane - 1, component] - RELAXATION * applied[component]
            )
    solution_ref[...] = solution_in_ref[...] + RELAXATION * z_ref[2 : planes + 2]


def rows_of(matrix):
    k, n = matrix.shape
    blocks = -(-n // 128)
    padded = jnp.pad(matrix, ((0, 0), (0, blocks * 128 - n)))
    return [padded[:, i * 128 : (i + 1) * 128] for i in range(blocks)]


def of_rows(rows, k, n):
    blocks = -(-n // 128)
    return jnp.concatenate([rows[i * k : (i + 1) * k] for i in range(blocks)], axis=1)[:, :n]


def body(
    applied_loads,
    labels,
    shear_modulus,
    stiff_ratio,
    local_order,
    local_inverse,
    coarse_basis,
    coarse_inverse,
):
    planes, components, nodes, cases = applied_loads.shape
    window = planes + 2
    plane_rows = components * nodes
    size = window * plane_rows
    order_coarse = coarse_inverse.shape[1]
    position = lax.axis_index(AXES)
    count = lax.axis_size(AXES)
    even = (position % 2) == 0
    near_pairs, far_pairs = swap_pairs(count)
    place = jnp.stack(
        [even.astype(jnp.int32), (position > 0).astype(jnp.int32), (position < count - 1).astype(jnp.int32)]
    )
    basis = coarse_basis[0]
    own_rows = lax.dynamic_slice_in_dim(coarse_inverse, lax.axis_index("grp") * CV_DEV, CV_DEV, 0)
    mats = jnp.stack(lookup(labels, shear_modulus, stiff_ratio), axis=1)

    part = 3 * plane_rows

    def pack(load_plane, mat_planes, basis_part):
        rows = [load_plane.reshape(plane_rows, cases)]
        rows += rows_of(basis_part) + rows_of(own_rows)
        rows.append(mat_planes.reshape(2 * 2 * nodes // 128, 128))
        return jnp.concatenate(rows, axis=0)

    to_left = pack(applied_loads[0], mats[:2], basis[:, :part])
    to_right = pack(applied_loads[planes - 1], mats[planes - 2 :], basis[:, size - part :])
    near = lax.ppermute(jnp.where(even, to_right, to_left), AXES, near_pairs)
    far = lax.ppermute(jnp.where(even, to_left, to_right), AXES, far_pairs)
    natural = renumber(local_order, local_inverse[0])
    left = jnp.where(even, far, near)
    right = jnp.where(even, near, far)

    def unpack(packed):
        at = plane_rows
        load_plane = packed[:at].reshape(components, NY, NZ, cases)
        basis_rows = CV_DEV * (-(-part // 128))
        basis_part = of_rows(packed[at : at + basis_rows], CV_DEV, part)
        at += basis_rows
        coarse_rows = CV_DEV * (-(-order_coarse // 128))
        inverse_rows = of_rows(packed[at : at + coarse_rows], CV_DEV, order_coarse)
        at += coarse_rows
        return load_plane, basis_part, inverse_rows, packed[at:].reshape(2, 2, nodes)

    left_load, left_basis, left_rows, left_mats = unpack(left)
    right_load, right_basis, right_rows, right_mats = unpack(right)
    mats_all = jnp.concatenate([left_mats, mats, right_mats], axis=0)
    mats_all = jnp.broadcast_to(mats_all[..., None], (planes + 4, 2, nodes, cases))
    mats_all = mats_all.reshape(planes + 4, 2, NY, NZ, cases)
    extent = size + 2 * plane_rows
    extents = jnp.concatenate(
        [
            jnp.pad(left_basis, ((0, 0), (0, extent - part))),
            jnp.pad(basis, ((0, 0), (plane_rows, plane_rows))),
            jnp.pad(right_basis, ((0, CV_DEV), (extent - part, 0))),
        ],
        axis=0,
    )
    inverse_rows = jnp.concatenate([left_rows, own_rows, jnp.pad(right_rows, ((0, CV_DEV), (0, 0)))], axis=0)
    basis_pad = jnp.pad(basis, ((0, 16 - CV_DEV), (0, 0)))

    def field(depth):
        return jax.ShapeDtypeStruct((depth, components, NY, NZ, cases), F32)

    q_shape = jax.ShapeDtypeStruct((count, CV_DEV, cases), F32)
    cost = pl.CostEstimate(flops=2 * size * size * cases, bytes_accessed=2 * size * size, transcendentals=0)
    z_scratch = pltpu.VMEM((planes + 4, components, NY, NZ, cases), F32)
    loads = applied_loads.reshape(planes, components, NY, NZ, cases)

    def move(near_out, far_out, q):
        near_in = lax.ppermute(near_out, AXES, near_pairs)
        far_in = lax.ppermute(far_out, AXES, far_pairs)
        q_all = lax.all_to_all(q, AXES, 0, 0).reshape(count * CV_DEV, cases)
        return near_in, far_in, q_all

    res, t, near_out, far_out, q = pl.pallas_call(
        first_kernel,
        out_shape=[field(window), field(window), field(3), field(3), q_shape],
        in_specs=[SMEM] + [VMEM] * 5,
        out_specs=[VMEM] * 5,
        compiler_params=PARAMS,
        cost_estimate=cost,
    )(place, loads, left_load, right_load, natural, basis_pad)
    near_in, far_in, q_all = move(near_out, far_out, q)
    solution = None
    for iteration in range(1, ITERS):
        width = 2 if iteration == ITERS - 1 else 3
        extra = [] if solution is None else [solution]
        operands = [place, q_all, inverse_rows, extents, mats_all, t, near_in, far_in, res, *extra, natural, basis_pad]
        solution, res, t, near_out, far_out, q = pl.pallas_call(
            functools.partial(middle_kernel, bool(extra)),
            out_shape=[field(planes), field(window), field(window), field(width), field(width), q_shape],
            in_specs=[SMEM] + [VMEM] * (len(operands) - 1),
            out_specs=[VMEM] * 6,
            scratch_shapes=[z_scratch],
            compiler_params=PARAMS,
            cost_estimate=cost,
        )(*operands)
        near_in, far_in, q_all = move(near_out, far_out, q)
    solution, residual, coarse_values = pl.pallas_call(
        last_kernel,
        out_shape=[field(planes), field(planes), jax.ShapeDtypeStruct((CV_DEV, cases), F32)],
        in_specs=[SMEM] + [VMEM] * 9,
        out_specs=[VMEM] * 3,
        scratch_shapes=[z_scratch],
        compiler_params=PARAMS,
    )(place, q_all, inverse_rows, extents, mats_all, t, near_in, far_in, res, solution)
    return (
        solution.reshape(planes, components, nodes, cases),
        residual.reshape(planes, components, nodes, cases),
        coarse_values,
    )


def solution(mesh):
    return jax.shard_map(
        body,
        mesh=mesh,
        in_specs=(
            P(("sub", "grp"), None, None, None),
            P(("sub", "grp"), None),
            P(),
            P(),
            P(("sub", "grp"), None),
            P(("sub", "grp"), None, None),
            P(("sub", "grp"), None, None),
            P("sub", None),
        ),
        out_specs=(
            P(("sub", "grp"), None, None, None),
            P(("sub", "grp"), None, None, None),
            P(("sub", "grp"), None),
        ),
        check_vma=False,
    )
```

time: 236 us -> 86.6 us (0.37); the launches traced: 232 us -> 85.7 us
  blocking collectives: 124 us -> 27.5 us
  starting transfers between devices: 39.3 us -> 17.5 us
  local copies, waits for them, and re-layouts: 34.1 us -> 14.7 us
  Pallas kernels: 0 us -> 19.3 us
  other arithmetic: 14.5 us -> 5.12 us
  matrix products: 8.73 us -> 0 us
  waiting for transfers between devices: 8.99 us -> 0.75 us
    all_gather x3 -> x0, blocking collectives: 124 us -> none  [body(): lax.all_gather(coarse_res, ('sub', 'grp'), axis=0, tiled=True)]
    ppermute x16 -> x8, starting transfers between devices: 39.3 us -> 8.73 us  [the longest x3 4.85 us: move(): near_in = lax.ppermute(near_out, AXES, near_pairs)]
    all_to_all x0 -> x2, blocking collectives: none -> 27.5 us  [move(): q_all = lax.all_to_all(q, AXES, 0, 0).reshape(count * CV_DEV, cases)]
    pallas_call x0 -> x5, Pallas kernels: none -> 19.3 us  [the longest x1 9.46 us: renumber(): pl.pallas_call(renumber_kernel, out_shape=jax.ShapeDtypeStruct((size, siz...]
    gather x2 -> x0, local copies, waits for them, and re-layouts: 14.3 us -> none  [the longest x1 9.22 us: body(): jnp.take(jnp.take(inverse, unknown_rank, axis=0), unknown_rank, axis=1)]
    ppermute x16 -> x8, waiting for transfers between devices: 8.99 us -> 0.02 us  [the longest x3 0.01 us: move(): near_in = lax.ppermute(near_out, AXES, near_pairs)]
    all_to_all x0 -> x1, starting transfers between devices: none -> 8.73 us  [move(): q_all = lax.all_to_all(q, AXES, 0, 0).reshape(count * CV_DEV, cases)]
    dot_general x12 -> x0, matrix products: 8.73 us -> none  [the longest x3 3.62 us: body(): jnp.dot(natural_inverse, rounded, preferred_element_type=jnp.float32)]
  transfers between devices with their start and end apart: 16 -> 9, of which waited for: 6 -> 1; matrix products, arithmetic and copies ran while one was open for 15% -> 7% of each run, Pallas kernels for 0% -> 11%
where the time goes in v1:
time: 86.6 us; the launch traced here: 85.7 us
  blocking collectives  27.5 us (32%)
  Pallas kernels  19.3 us (22%)
  starting transfers between devices  17.5 us (20%)
  local copies, waits for them, and re-layouts  14.7 us (17%)
  other arithmetic  5.12 us (6%)
    all_to_all x2, blocking collectives, move(): q_all = lax.all_to_all(q, AXES, 0, 0).reshape(count * CV_DEV, cases)  27.5 us
    pallas_call x1, Pallas kernels, renumber(): pl.pallas_call(renumber_kernel, out_shape=jax.ShapeDtypeStruct((size, siz...  9.46 us
    all_to_all x1, starting transfers between devices, move(): q_all = lax.all_to_all(q, AXES, 0, 0).reshape(count * CV_DEV, cases)  8.73 us
    unnamed x32, local copies, waits for them, and re-layouts  6.42 us
    pallas_call x2, Pallas kernels, body(): pl.pallas_call(functools.partial(middle_kernel, bool(extra)), out_shape=[...  5.54 us
    ppermute x3, starting transfers between devices, move(): near_in = lax.ppermute(near_out, AXES, near_pairs)  4.85 us
    ppermute x3, starting transfers between devices, move(): far_in = lax.ppermute(far_out, AXES, far_pairs)  2.71 us
    pallas_call x1, Pallas kernels, body(): pl.pallas_call(last_kernel, out_shape=[field(planes), field(planes), jax....  2.14 us
  transfers between devices with their start and end apart: 9, of which 1 were waited for; matrix products, arithmetic and copies ran while one was open for 7% of the time, Pallas kernels for 11%

profile of v1, /device:TPU:0, one launch (start us, length us, event | category | flops | bytes accessed | tf_op | source)
XLA Modules:
  0.0 85.7 jit_solution(16145144161370945348)
XLA Ops:
  0.6 0.8 fusion.3
  1.5 0.8 slice.169
  2.9 0.8 select_reduce_fusion
  4.6 1.0 %fusion.2 = (f32[1,3,64,128]{3,2,1,0:T(8,128)S(1)}, f32[1,3,64,128]{3,2,1,0:T(8,128)S(1)}) fusion(f32[4,3,64,128]{3,2,1,0:T(8,128)} %param.8), kind=kLoop, calls=%fused_computation.36 | loop fusion | bytes 393216 | tf_op jit(solution)/shard_map/slice | solution.py:276
  7.8 0.7 pad.29.basis_ref.rest_1_.rest_2_
  8.5 1.7 %copy-done.3 = bf16[1,1152,1152]{2,1,0:T(8,128)(2,1)S(1)} copy-done((bf16[1,1152,1152]{2,1,0:T(8,128)(2,1)S(1)}, bf16[1,1152,1152]{2,1,0:T(8,128)(2,1)}, u32[]{:S(2)}) %copy-start.3) | copy-done | bytes 2654232
  11.0 9.5 %shard_map.103.inverse_ref.rest_0_.rest_1_ = bf16[1152,1152]{1,0:T(8,128)(2,1)S(1)} custom-call(s32[1,1152]{1,0:T(1,128)S(1)} %copy-done.6, bf16[1152,1152]{1,0:T(8,128)(2,1)S(1)} %bitcast.27), custom_call_target="tpu_custom_call" | custom-call | flops 6115295232 | bytes 5308416 | tf_op jit(solution)/shard_map/pallas_call | solution.py:60
  21.9 2.1 %shard_map.104 = (f32[6,3,8,8,128]{4,3,2,1,0:T(8,128)S(1)}, f32[6,3,8,8,128]{4,3,2,1,0:T(8,128)S(1)}, f32[3,3,8,8,128]{4,3,2,1,0:T(8,128)S(1)}, f32[3,3,8,8,128]{4,3,2,1,0:T(8,128)S(1)}, f32[32,4,128]{2,1,0:T(4,128)}) custom-call(s32[3]{0:T(128)S(1)} %add_convert_fusion.place_ref, f32[4,3,8,8,128]{4,3,2,1,0:T(8,128)S(1)} %bitcast.21, ...), custom_call_target="tpu_custom_call" | custom-call | flops 339738624 | bytes 2654208 | tf_op jit(solution)/shard_map/pallas_call | solution.py:325
  24.0 0.8 copy-done.1
  24.9 0.7 copy-done.4
  25.6 0.7 copy-done.5
  26.3 8.7 %all-to-all-start = ((f32[32,4,128]{2,1,0:T(4,128)}), f32[32,4,128]{2,1,0:T(4,128)S(1)}, u32[]{:S(2)}, u32[]{:S(2)}) async-start(f32[32,4,128]{2,1,0:T(4,128)} %get-tuple-element.23), calls=%async_computation | async-start | bytes 131072 | tf_op jit(solution)/shard_map/all_to_all | solution.py:322
  35.3 1.4 %collective-permute-start.3 = (f32[3,3,8,8,128]{4,3,2,1,0:T(8,128)}, f32[3,3,8,8,128]{4,3,2,1,0:T(8,128)}, u32[]{:S(2)}, u32[]{:S(2)}) collective-permute-start(f32[3,3,8,8,128]{4,3,2,1,0:T(8,128)} %copy-done.4), channel_id=1, source_target_pairs={{1,2},{2,1},{3,4},{4,3},{5,6},{6,5},{7,8},{8,7},{9,10},{10,9},{11,... | collective-permute-start | bytes 884744 | tf_op jit(solution)/shard_map/ppermute | solution.py:321
  36.7 0.8 select_maximum_fusion.extent_ref
  40.4 1.3 %pad_maximum_fusion = f32[8,2,8,8]{3,2,1,0:T(8,128)} fusion(f32[2,2,8,8]{3,2,1,0:T(8,128)} %concatenate.34, f32[4,1,8,8]{3,2,1,0:T(8,128)S(1)} %bitcast.35, f32[4,1,8,8]{3,2,1,0:T(8,128)S(1)} %bitcast.36, f32[2,2,8,8]{3,2,1,0:T(8,128)S(1)} %concatenate.33), kind=kLoop, calls=%fused_computation.7 | loop fusion | flops 3072 | bytes 8192 | tf_op jit(solution)/shard_map/concatenate | solution.py:296
  41.7 0.7 all-to-all-done
  42.4 1.0 %broadcast_in_dim.2.mats_ref = f32[8,2,8,8,128]{4,3,2,1,0:T(8,128)S(1)} broadcast(f32[8,2,8,8]{3,2,1,0:T(8,128)} %pad_maximum_fusion), dimensions={0,1,2,3} | broadcast | bytes 528384 | tf_op jit(solution)/shard_map/broadcast_in_dim | solution.py:297
  43.5 1.1 %copy-done.2 = f32[6,3,8,8,128]{4,3,2,1,0:T(8,128)S(1)} copy-done((f32[6,3,8,8,128]{4,3,2,1,0:T(8,128)S(1)}, f32[6,3,8,8,128]{4,3,2,1,0:T(8,128)}, u32[]{:S(2)}) %copy-start.2) | copy-done | bytes 589848
  44.6 3.0 %shard_map.105 = (f32[4,3,8,8,128]{4,3,2,1,0:T(8,128)S(1)}, f32[6,3,8,8,128]{4,3,2,1,0:T(8,128)S(1)}, f32[6,3,8,8,128]{4,3,2,1,0:T(8,128)S(1)}, f32[3,3,8,8,128]...) custom-call(s32[3]{0:T(128)S(1)} %add_convert_fusion.place_ref, ...), custom_call_target="tpu_custom_call" | custom-call | flops 339738624 | bytes 2654208 | tf_op jit(solution)/shard_map/pallas_call | solution.py:339
  47.6 4.3 %collective-permute-start.4 = (f32[3,3,8,8,128]{4,3,2,1,0:T(8,128)S(1)}, f32[3,3,8,8,128]{4,3,2,1,0:T(8,128)S(1)}, u32[]{:S(2)}, u32[]{:S(2)}) collective-permute-start(f32[3,3,8,8,128]{4,3,2,1,0:T(8,128)S(1)} %get-tuple-element.30), channel_id=1, source_target_pairs={{0,1},{1,0},{2,3},{3,2},{4,5},{5,4},{6,7},{7,6},{8,9},{9,8},{10,11... | collective-permute-start | bytes 884744 | tf_op jit(solution)/shard_map/ppermute | solution.py:320
  52.6 15.5 %all_to_all.15 = f32[32,4,128]{2,1,0:T(4,128)S(1)} all-to-all(f32[32,4,128]{2,1,0:T(4,128)S(1)} %get-tuple-element.28), channel_id=1, replica_groups=mesh['sub'=16,'grp'=2] {'sub','grp'}, dimensions={0} | all-to-all | bytes 131072 | tf_op jit(solution)/shard_map/all_to_all | solution.py:322
  68.1 2.5 %shard_map.106 = (f32[4,3,8,8,128]{4,3,2,1,0:T(8,128)S(1)}, f32[6,3,8,8,128]{4,3,2,1,0:T(8,128)S(1)}, f32[6,3,8,8,128]{4,3,2,1,0:T(8,128)S(1)}, f32[2,3,8,8,128]...) custom-call(s32[3]{0:T(128)S(1)} %add_convert_fusion.place_ref, ...), custom_call_target="tpu_custom_call" | custom-call | flops 339738624 | bytes 2654208 | tf_op jit(solution)/shard_map/pallas_call | solution.py:339
  71.5 12.1 %all_to_all.16 = f32[32,4,128]{2,1,0:T(4,128)S(1)} all-to-all(f32[32,4,128]{2,1,0:T(4,128)S(1)} %get-tuple-element.34), channel_id=1, replica_groups=mesh['sub'=16,'grp'=2] {'sub','grp'}, dimensions={0} | all-to-all | bytes 131072 | tf_op jit(solution)/shard_map/all_to_all | solution.py:322
  83.5 2.1 %shard_map.107 = (f32[4,3,8,8,128]{4,3,2,1,0:T(8,128)}, f32[4,3,8,8,128]{4,3,2,1,0:T(8,128)}, f32[4,128]{1,0:T(4,128)}) custom-call(s32[3]{0:T(128)S(1)} %add_convert_fusion.place_ref, f32[128,128]{1,0:T(8,128)S(1)} %bitcast.26, f32[16,128]{1,0:T(8,128)S(1)} %select_maximum_fusion.2.rows_ref, f32[16,1536]{1,0:T(8,128)S(1)} %select_maximum_fusion.extent_ref, ...), custom_call_target="tpu_custom_call" | custom-call | tf_op jit(solution)/shard_map/pallas_call | solution.py:349
  (66 shorter events, 10.5 us)
Async XLA Ops:
  6.5 14.1 %collective-permute-start.1 = (f32[218,128]{1,0:T(8,128)S(1)}, f32[218,128]{1,0:T(8,128)S(1)}, u32[]{:S(2)}, u32[]{:S(2)}) collective-permute-start(f32[218,128]{1,0:T(8,128)S(1)} %get-tuple-element.49), channel_id=1, source_target_pairs={{0,1},{1,0},{2,3},{3,2},{4,5},{5,4},{6,7},{7,6},{8,9},{9,8},{10,11... | collective-permute-start | bytes 334856 | tf_op jit(solution)/shard_map/ppermute | solution.py:277
  7.0 13.6 %collective-permute-start = (f32[218,128]{1,0:T(8,128)S(1)}, f32[218,128]{1,0:T(8,128)S(1)}, u32[]{:S(2)}, u32[]{:S(2)}) collective-permute-start(f32[218,128]{1,0:T(8,128)S(1)} %get-tuple-element.50), channel_id=1, source_target_pairs={{1,2},{2,1},{3,4},{4,3},{5,6},{6,5},{7,8},{8,7},{9,10},{10,9},{11,... | collective-permute-start | bytes 334856 | tf_op jit(solution)/shard_map/ppermute | solution.py:278
  8.5 1.7 %copy-start.3 = (bf16[1,1152,1152]{2,1,0:T(8,128)(2,1)S(1)}, bf16[1,1152,1152]{2,1,0:T(8,128)(2,1)}, u32[]{:S(2)}) copy-start(bf16[1,1152,1152]{2,1,0:T(8,128)(2,1)} %param.13) | copy-start | bytes 7962628
  10.3 0.7 copy-start.6
  11.0 10.9 %copy-start = (f32[4,3,64,128]{3,2,1,0:T(8,128)S(1)}, f32[4,3,64,128]{3,2,1,0:T(8,128)}, u32[]{:S(2)}) copy-start(f32[4,3,64,128]{3,2,1,0:T(8,128)} %param.8) | copy-start | bytes 1179652
  20.5 16.3 %copy-start.9 = (f32[1,4,1152]{2,1,0:T(4,128)S(1)}, f32[1,4,1152]{2,1,0:T(4,128)}, u32[]{:S(2)}) copy-start(f32[1,4,1152]{2,1,0:T(4,128)} %param.14) | copy-start | bytes 55300
  20.6 0.8 copy-start.7
  20.6 0.8 copy-start.8
  20.7 0.6 copy-start.11
  21.3 0.6 copy-start.10
  24.0 0.8 copy-start.1
  24.9 0.7 copy-start.4
  25.6 0.7 copy-start.5
  26.3 16.2 %all-to-all-start = ((f32[32,4,128]{2,1,0:T(4,128)}), f32[32,4,128]{2,1,0:T(4,128)S(1)}, u32[]{:S(2)}, u32[]{:S(2)}) async-start(f32[32,4,128]{2,1,0:T(4,128)} %get-tuple-element.23), calls=%async_computation | async-start | bytes 131072 | tf_op jit(solution)/shard_map/all_to_all | solution.py:322
  35.0 7.4 %collective-permute-start.2 = (f32[3,3,8,8,128]{4,3,2,1,0:T(8,128)}, f32[3,3,8,8,128]{4,3,2,1,0:T(8,128)}, u32[]{:S(2)}, u32[]{:S(2)}) collective-permute-start(f32[3,3,8,8,128]{4,3,2,1,0:T(8,128)} %copy-done.5), channel_id=1, source_target_pairs={{0,1},{1,0},{2,3},{3,2},{4,5},{5,4},{6,7},{7,6},{8,9},{9,8},{10,11... | collective-permute-start | bytes 884744 | tf_op jit(solution)/shard_map/ppermute | solution.py:320
  35.3 7.1 %collective-permute-start.3 = (f32[3,3,8,8,128]{4,3,2,1,0:T(8,128)}, f32[3,3,8,8,128]{4,3,2,1,0:T(8,128)}, u32[]{:S(2)}, u32[]{:S(2)}) collective-permute-start(f32[3,3,8,8,128]{4,3,2,1,0:T(8,128)} %copy-done.4), channel_id=1, source_target_pairs={{1,2},{2,1},{3,4},{4,3},{5,6},{6,5},{7,8},{8,7},{9,10},{10,9},{11,... | collective-permute-start | bytes 884744 | tf_op jit(solution)/shard_map/ppermute | solution.py:321
  43.5 1.1 %copy-start.2 = (f32[6,3,8,8,128]{4,3,2,1,0:T(8,128)S(1)}, f32[6,3,8,8,128]{4,3,2,1,0:T(8,128)}, u32[]{:S(2)}) copy-start(f32[6,3,8,8,128]{4,3,2,1,0:T(8,128)} %copy-done.1) | copy-start | bytes 1769476
  47.6 20.5 %collective-permute-start.4 = (f32[3,3,8,8,128]{4,3,2,1,0:T(8,128)S(1)}, f32[3,3,8,8,128]{4,3,2,1,0:T(8,128)S(1)}, u32[]{:S(2)}, u32[]{:S(2)}) collective-permute-start(f32[3,3,8,8,128]{4,3,2,1,0:T(8,128)S(1)} %get-tuple-element.30), channel_id=1, source_target_pairs={{0,1},{1,0},{2,3},{3,2},{4,5},{5,4},{6,7},{7,6},{8,9},{9,8},{10,11... | collective-permute-start | bytes 884744 | tf_op jit(solution)/shard_map/ppermute | solution.py:320
  51.9 16.1 %collective-permute-start.5 = (f32[3,3,8,8,128]{4,3,2,1,0:T(8,128)S(1)}, f32[3,3,8,8,128]{4,3,2,1,0:T(8,128)S(1)}, u32[]{:S(2)}, u32[]{:S(2)}) collective-permute-start(f32[3,3,8,8,128]{4,3,2,1,0:T(8,128)S(1)} %get-tuple-element.31), channel_id=1, source_target_pairs={{1,2},{2,1},{3,4},{4,3},{5,6},{6,5},{7,8},{8,7},{9,10},{10,9},{11,... | collective-permute-start | bytes 884744 | tf_op jit(solution)/shard_map/ppermute | solution.py:321
  70.6 12.9 %collective-permute-start.6 = (f32[2,3,8,8,128]{4,3,2,1,0:T(8,128)S(1)}, f32[2,3,8,8,128]{4,3,2,1,0:T(8,128)S(1)}, u32[]{:S(2)}, u32[]{:S(2)}) collective-permute-start(f32[2,3,8,8,128]{4,3,2,1,0:T(8,128)S(1)} %get-tuple-element.36), channel_id=1, source_target_pairs={{0,1},{1,0},{2,3},{3,2},{4,5},{5,4},{6,7},{7,6},{8,9},{9,8},{10,11... | collective-permute-start | bytes 589832 | tf_op jit(solution)/shard_map/ppermute | solution.py:320
  70.8 12.7 %collective-permute-start.7 = (f32[2,3,8,8,128]{4,3,2,1,0:T(8,128)S(1)}, f32[2,3,8,8,128]{4,3,2,1,0:T(8,128)S(1)}, u32[]{:S(2)}, u32[]{:S(2)}) collective-permute-start(f32[2,3,8,8,128]{4,3,2,1,0:T(8,128)S(1)} %get-tuple-element.37), channel_id=1, source_target_pairs={{1,2},{2,1},{3,4},{4,3},{5,6},{6,5},{7,8},{8,7},{9,10},{10,9},{11,... | collective-permute-start | bytes 589832 | tf_op jit(solution)/shard_map/ppermute | solution.py:321

commit v2 on v1

--- a/solution.py
+++ b/solution.py
@@ -17,14 +17,7 @@
 BF16 = jnp.bfloat16
 VMEM = pl.BlockSpec(memory_space=pltpu.VMEM)
 SMEM = pl.BlockSpec(memory_space=pltpu.SMEM)
-PARAMS = pltpu.CompilerParams(vmem_limit_bytes=40 * 1024 * 1024)
-
-
-def lookup(labels, shear_modulus, stiff_ratio):
-    onehot = (labels[..., None] == jnp.arange(shear_modulus.shape[0], dtype=jnp.int32)).astype(F32)
-    shear_node = jnp.sum(onehot * shear_modulus, axis=-1)
-    normal_node = jnp.sum(onehot * (shear_modulus * (2.0 + stiff_ratio)), axis=-1)
-    return shear_node, normal_node
+PARAMS = pltpu.CompilerParams(vmem_limit_bytes=24 * 1024 * 1024)
 
 
 def swap_pairs(count):
@@ -35,34 +28,95 @@
     return near, far
 
 
-def renumber_kernel(order_ref, inverse_ref, out_ref, hot):
+def pack_kernel(place_ref, shear_ref, ratio_ref, loads_ref, labels_ref, wide_ref, coarse_ref,
+                near_ref, far_ref, mats_ref, rows_ref):
+    planes, nodes = labels_ref.shape
+    plane_rows = loads_ref.shape[1] * loads_ref.shape[2]
+    even = place_ref[0] == 1
+    labels = labels_ref[...]
+    shear = jnp.zeros((planes, nodes), F32)
+    normal = jnp.zeros((planes, nodes), F32)
+    for region in range(shear_ref.shape[0]):
+        value = shear_ref[region]
+        here = labels == region
+        shear = jnp.where(here, value, shear)
+        normal = jnp.where(here, value * (2.0 + ratio_ref[region]), normal)
+    both = jnp.concatenate([shear, normal], axis=1)
+    mats_ref[...] = both
+    rows = coarse_ref[:CV_DEV]
+    for member in range(1, coarse_ref.shape[0] // CV_DEV):
+        rows = jnp.where(place_ref[3] == member, coarse_ref[member * CV_DEV : (member + 1) * CV_DEV], rows)
+    rows_ref[...] = rows
+    span = part_blocks(plane_rows)
+    load_l = loads_ref[0].reshape(plane_rows, loads_ref.shape[3])
+    load_r = loads_ref[planes - 1].reshape(plane_rows, loads_ref.shape[3])
+    mats_l, mats_r = both[:2], both[planes - 2 :]
+    start_r = planes * plane_rows
+    start_l = 4 * plane_rows - 128 * span
+    near_ref[:plane_rows] = jnp.where(even, load_r, load_l)
+    far_ref[:plane_rows] = jnp.where(even, load_l, load_r)
+    groups = group_count(plane_rows, coarse_ref.shape[1])
+    for i in range(groups):
+        at = plane_rows + 8 * i
+        if i < span:
+            block_l = wide_ref[:, start_l + 128 * i : start_l + 128 * (i + 1)]
+            block_r = wide_ref[:, start_r + 128 * i : start_r + 128 * (i + 1)]
+            near_ref[at : at + CV_DEV] = jnp.where(even, block_r, block_l)
+            far_ref[at : at + CV_DEV] = jnp.where(even, block_l, block_r)
+        if i * 128 < coarse_ref.shape[1]:
+            near_ref[at + CV_DEV : at + 2 * CV_DEV] = rows[:, 128 * i : 128 * (i + 1)]
+            far_ref[at + CV_DEV : at + 2 * CV_DEV] = rows[:, 128 * i : 128 * (i + 1)]
+    at = plane_rows + 8 * groups
+    near_ref[at : at + 2] = jnp.where(even, mats_r, mats_l)
+    far_ref[at : at + 2] = jnp.where(even, mats_l, mats_r)
+
+
+def part_blocks(plane_rows):
+    return -(-3 * plane_rows // 128)
+
+
+def group_count(plane_rows, coarse_order):
+    return max(part_blocks(plane_rows), coarse_order // 128)
+
+
+def renumber_kernel(order_ref, inverse_ref, out_ref, gather_ref, hot, held, sems):
     size = inverse_ref.shape[0]
     step = size // 3
+    copies = []
+    for i in range(3):
+        part = pl.ds(i * step, step)
+        copy = pltpu.make_async_copy(inverse_ref.at[:, part], held.at[:, part], sems.at[i])
+        copy.start()
+        copies.append(copy)
     order = order_ref[...]
-
-    def build(i, carry):
-        start = pl.multiple_of(i * step, step)
-        row = lax.broadcasted_iota(jnp.int32, (step, size), 0) + start
-        hot[pl.ds(start, step), :] = jnp.where(row == order, 1.0, 0.0).astype(BF16)
-        return carry
-
-    lax.fori_loop(0, 3, build, 0)
+    for i in range(size // 128):
+        row = lax.broadcasted_iota(jnp.int32, (128, size), 0) + i * 128
+        hot[i * 128 : (i + 1) * 128, :] = jnp.where(row == order, 1.0, 0.0).astype(BF16)
+        turned = jnp.transpose(jnp.broadcast_to(order[:, i * 128 : (i + 1) * 128], (128, 128)))
+        for k in range(size // 128):
+            column = lax.broadcasted_iota(jnp.int32, (128, 128), 1) + k * 128
+            gather_ref[i * 128 : (i + 1) * 128, k * 128 : (k + 1) * 128] = jnp.where(
+                turned == column, 1.0, 0.0
+            ).astype(BF16)
     for i in range(3):
         part = slice(i * step, (i + 1) * step)
-        columns = lax.dot_general(
-            inverse_ref[...], hot[part, :], (((1,), (1,)), ((), ())), preferred_element_type=F32
-        ).astype(BF16)
-        out_ref[:, part] = jnp.dot(hot[...], columns, preferred_element_type=F32).astype(BF16)
+        copies[i].wait()
+        out_ref[:, part] = jnp.dot(hot[...], held[:, part], preferred_element_type=F32).astype(BF16)
 
 
 def renumber(order, inverse):
     size = inverse.shape[0]
+    square = jax.ShapeDtypeStruct((size, size), BF16)
     return pl.pallas_call(
         renumber_kernel,
-        out_shape=jax.ShapeDtypeStruct((size, size), BF16),
-        in_specs=[VMEM, VMEM],
-        out_specs=VMEM,
-        scratch_shapes=[pltpu.VMEM((size, size), BF16)],
+        out_shape=[square, square],
+        in_specs=[VMEM, pl.BlockSpec(memory_space=pl.ANY)],
+        out_specs=[VMEM, VMEM],
+        scratch_shapes=[
+            pltpu.VMEM((size, size), BF16),
+            pltpu.VMEM((size, size), BF16),
+            pltpu.SemaphoreType.DMA((3,)),
+        ],
         compiler_params=PARAMS,
         cost_estimate=pl.CostEstimate(flops=4 * size**3, bytes_accessed=4 * size * size, transcendentals=0),
     )(order, inverse)
@@ -123,15 +177,16 @@
     return high, (x - high.astype(F32)).astype(BF16)
 
 
-def products(place_ref, inverse_ref, basis_ref, res_ref, t_ref, near_ref, far_ref, q_ref):
+def products(place_ref, inverse_ref, gather_ref, basis_ref, res_ref, t_ref, near_ref, far_ref, q_ref):
     slots, rows, cases = res_ref.shape[0] * 3, NY * NZ, res_ref.shape[-1]
     size = slots * rows
     res = res_ref[...].reshape(size, cases)
     high, low = split(res)
+    ordered = jnp.dot(gather_ref[...], high, preferred_element_type=F32).astype(BF16)
     step = size // 3
     t_planes = t_ref.shape[0]
     for i in range(3):
-        block = jnp.dot(inverse_ref[i * step : (i + 1) * step, :], high, preferred_element_type=F32)
+        block = jnp.dot(inverse_ref[i * step : (i + 1) * step, :], ordered, preferred_element_type=F32)
         per = t_planes // 3
         t_ref[i * per : (i + 1) * per] = block.reshape(per, 3, NY, NZ, cases)
     even = place_ref[0]
@@ -148,13 +203,48 @@
     q_ref[...] = jnp.broadcast_to(q[None], q_ref.shape)
 
 
-def first_kernel(place_ref, loads_ref, left_ref, right_ref, inverse_ref, basis_ref,
-                 res_ref, t_ref, near_ref, far_ref, q_ref):
-    planes = loads_ref.shape[0]
-    res_ref[0] = left_ref[...]
+def first_kernel(place_ref, loads_ref, near_in_ref, far_in_ref, mats_in_ref, wide_ref, own_rows_ref,
+                 inverse_ref, gather_ref, basis_ref,
+                 res_ref, t_ref, near_ref, far_ref, q_ref, mats_ref, extent_ref, rows_ref):
+    planes, components = loads_ref.shape[:2]
+    cases = loads_ref.shape[-1]
+    plane_rows = components * NY * NZ
+    even = place_ref[0] == 1
+
+    def beside(start, stop):
+        near, far = near_in_ref[start:stop], far_in_ref[start:stop]
+        return jnp.where(even, far, near), jnp.where(even, near, far)
+
+    left, right = beside(0, plane_rows)
+    res_ref[0] = left.reshape(components, NY, NZ, cases)
     res_ref[1 : planes + 1] = loads_ref[...]
-    res_ref[planes + 1] = right_ref[...]
-    products(place_ref, inverse_ref, basis_ref, res_ref, t_ref, near_ref, far_ref, q_ref)
+    res_ref[planes + 1] = right.reshape(components, NY, NZ, cases)
+    products(place_ref, inverse_ref, gather_ref, basis_ref, res_ref, t_ref, near_ref, far_ref, q_ref)
+
+    extent = extent_ref.shape[1]
+    span = part_blocks(plane_rows)
+    extent_ref[...] = jnp.zeros_like(extent_ref)
+    rows_ref[...] = jnp.zeros_like(rows_ref)
+    extent_ref[CV_DEV : 2 * CV_DEV] = wide_ref[...]
+    rows_ref[CV_DEV : 2 * CV_DEV] = own_rows_ref[...]
+    groups = group_count(plane_rows, rows_ref.shape[1])
+    for i in range(groups):
+        at = plane_rows + 8 * i
+        if i < span:
+            left, right = beside(at, at + CV_DEV)
+            extent_ref[:CV_DEV, 128 * i : 128 * (i + 1)] = left
+            start = extent - 128 * span + 128 * i
+            extent_ref[2 * CV_DEV : 3 * CV_DEV, start : start + 128] = right
+        if i * 128 < rows_ref.shape[1]:
+            left, right = beside(at + CV_DEV, at + 2 * CV_DEV)
+            rows_ref[:CV_DEV, 128 * i : 128 * (i + 1)] = left
+            rows_ref[2 * CV_DEV : 3 * CV_DEV, 128 * i : 128 * (i + 1)] = right
+    at = plane_rows + 8 * groups
+    left, right = beside(at, at + 2)
+    everything = [left[0:1], left[1:2]] + [mats_in_ref[p : p + 1] for p in range(planes)] + [right[0:1], right[1:2]]
+    for plane, row in enumerate(everything):
+        turned = jnp.transpose(jnp.broadcast_to(row, (cases, row.shape[1])))
+        mats_ref[plane] = turned.reshape(2, NY, NZ, cases)
 
 
 def correction(place_ref, q_ref, rows_ref, extent_ref, t_ref, near_ref, far_ref, z_ref):
@@ -195,7 +285,7 @@
                   far_in_ref, res_in_ref, *rest):
     if with_solution:
         solution_in_ref, *rest = rest
-    inverse_ref, basis_ref, solution_ref, res_ref, t_ref, near_ref, far_ref, q_ref, z_ref = rest
+    inverse_ref, gather_ref, basis_ref, solution_ref, res_ref, t_ref, near_ref, far_ref, q_ref, z_ref = rest
     correction(place_ref, q_in_ref, rows_ref, extent_ref, t_in_ref, near_in_ref, far_in_ref, z_ref)
     window = res_ref.shape[0]
     for plane in range(1, window + 1):
@@ -209,7 +299,7 @@
             res_ref[plane - 1, component] = value
     own = RELAXATION * z_ref[2 : window]
     solution_ref[...] = solution_in_ref[...] + own if with_solution else own
-    products(place_ref, inverse_ref, basis_ref, res_ref, t_ref, near_ref, far_ref, q_ref)
+    products(place_ref, inverse_ref, gather_ref, basis_ref, res_ref, t_ref, near_ref, far_ref, q_ref)
 
 
 def last_kernel(place_ref, q_in_ref, rows_ref, extent_ref, mats_ref, t_in_ref, near_in_ref, far_in_ref, res_in_ref,
@@ -224,18 +314,6 @@
                 res_in_ref[plane - 1, component] - RELAXATION * applied[component]
             )
     solution_ref[...] = solution_in_ref[...] + RELAXATION * z_ref[2 : planes + 2]
-
-
-def rows_of(matrix):
-    k, n = matrix.shape
-    blocks = -(-n // 128)
-    padded = jnp.pad(matrix, ((0, 0), (0, blocks * 128 - n)))
-    return [padded[:, i * 128 : (i + 1) * 128] for i in range(blocks)]
-
-
-def of_rows(rows, k, n):
-    blocks = -(-n // 128)
-    return jnp.concatenate([rows[i * k : (i + 1) * k] for i in range(blocks)], axis=1)[:, :n]
 
 
 def body(
@@ -252,61 +330,39 @@
     window = planes + 2
     plane_rows = components * nodes
     size = window * plane_rows
-    order_coarse = coarse_inverse.shape[1]
+    coarse_order = coarse_inverse.shape[1]
     position = lax.axis_index(AXES)
     count = lax.axis_size(AXES)
-    even = (position % 2) == 0
     near_pairs, far_pairs = swap_pairs(count)
     place = jnp.stack(
-        [even.astype(jnp.int32), (position > 0).astype(jnp.int32), (position < count - 1).astype(jnp.int32)]
+        [
+            (position % 2 == 0).astype(jnp.int32),
+            (position > 0).astype(jnp.int32),
+            (position < count - 1).astype(jnp.int32),
+            lax.axis_index("grp").astype(jnp.int32),
+        ]
     )
     basis = coarse_basis[0]
-    own_rows = lax.dynamic_slice_in_dim(coarse_inverse, lax.axis_index("grp") * CV_DEV, CV_DEV, 0)
-    mats = jnp.stack(lookup(labels, shear_modulus, stiff_ratio), axis=1)
-
-    part = 3 * plane_rows
-
-    def pack(load_plane, mat_planes, basis_part):
-        rows = [load_plane.reshape(plane_rows, cases)]
-        rows += rows_of(basis_part) + rows_of(own_rows)
-        rows.append(mat_planes.reshape(2 * 2 * nodes // 128, 128))
-        return jnp.concatenate(rows, axis=0)
-
-    to_left = pack(applied_loads[0], mats[:2], basis[:, :part])
-    to_right = pack(applied_loads[planes - 1], mats[planes - 2 :], basis[:, size - part :])
-    near = lax.ppermute(jnp.where(even, to_right, to_left), AXES, near_pairs)
-    far = lax.ppermute(jnp.where(even, to_left, to_right), AXES, far_pairs)
-    natural = renumber(local_order, local_inverse[0])
-    left = jnp.where(even, far, near)
-    right = jnp.where(even, near, far)
-
-    def unpack(packed):
-        at = plane_rows
-        load_plane = packed[:at].reshape(components, NY, NZ, cases)
-        basis_rows = CV_DEV * (-(-part // 128))
-        basis_part = of_rows(packed[at : at + basis_rows], CV_DEV, part)
-        at += basis_rows
-        coarse_rows = CV_DEV * (-(-order_coarse // 128))
-        inverse_rows = of_rows(packed[at : at + coarse_rows], CV_DEV, order_coarse)
-        at += coarse_rows
-        return load_plane, basis_part, inverse_rows, packed[at:].reshape(2, 2, nodes)
-
-    left_load, left_basis, left_rows, left_mats = unpack(left)
-    right_load, right_basis, right_rows, right_mats = unpack(right)
-    mats_all = jnp.concatenate([left_mats, mats, right_mats], axis=0)
-    mats_all = jnp.broadcast_to(mats_all[..., None], (planes + 4, 2, nodes, cases))
-    mats_all = mats_all.reshape(planes + 4, 2, NY, NZ, cases)
+    wide = jnp.pad(basis, ((0, 0), (plane_rows, plane_rows)))
+    basis_pad = jnp.pad(basis, ((0, 16 - CV_DEV), (0, 0)))
     extent = size + 2 * plane_rows
-    extents = jnp.concatenate(
-        [
-            jnp.pad(left_basis, ((0, 0), (0, extent - part))),
-            jnp.pad(basis, ((0, 0), (plane_rows, plane_rows))),
-            jnp.pad(right_basis, ((0, CV_DEV), (extent - part, 0))),
+
+    packed = jax.ShapeDtypeStruct((plane_rows + 8 * group_count(plane_rows, coarse_order) + 8, cases), F32)
+    near_out, far_out, mats_own, own_rows = pl.pallas_call(
+        pack_kernel,
+        out_shape=[
+            packed,
+            packed,
+            jax.ShapeDtypeStruct((planes, 2 * nodes), F32),
+            jax.ShapeDtypeStruct((CV_DEV, coarse_order), F32),
         ],
-        axis=0,
-    )
-    inverse_rows = jnp.concatenate([left_rows, own_rows, jnp.pad(right_rows, ((0, CV_DEV), (0, 0)))], axis=0)
-    basis_pad = jnp.pad(basis, ((0, 16 - CV_DEV), (0, 0)))
+        in_specs=[SMEM] * 3 + [VMEM] * 4,
+        out_specs=[VMEM] * 4,
+        compiler_params=PARAMS,
+    )(place, shear_modulus, stiff_ratio, applied_loads, labels, wide, coarse_inverse)
+    near_in = lax.ppermute(near_out, AXES, near_pairs)
+    far_in = lax.ppermute(far_out, AXES, far_pairs)
+    ordered_inverse, gather = renumber(local_order, local_inverse[0])
 
     def field(depth):
         return jax.ShapeDtypeStruct((depth, components, NY, NZ, cases), F32)
@@ -322,20 +378,30 @@
         q_all = lax.all_to_all(q, AXES, 0, 0).reshape(count * CV_DEV, cases)
         return near_in, far_in, q_all
 
-    res, t, near_out, far_out, q = pl.pallas_call(
+    res, t, near_out, far_out, q, mats_all, extents, inverse_rows = pl.pallas_call(
         first_kernel,
-        out_shape=[field(window), field(window), field(3), field(3), q_shape],
-        in_specs=[SMEM] + [VMEM] * 5,
-        out_specs=[VMEM] * 5,
+        out_shape=[
+            field(window),
+            field(window),
+            field(3),
+            field(3),
+            q_shape,
+            jax.ShapeDtypeStruct((planes + 4, 2, NY, NZ, cases), F32),
+            jax.ShapeDtypeStruct((16, extent), F32),
+            jax.ShapeDtypeStruct((16, coarse_order), F32),
+        ],
+        in_specs=[SMEM] + [VMEM] * 9,
+        out_specs=[VMEM] * 8,
         compiler_params=PARAMS,
         cost_estimate=cost,
-    )(place, loads, left_load, right_load, natural, basis_pad)
+    )(place, loads, near_in, far_in, mats_own, wide, own_rows, ordered_inverse, gather, basis_pad)
     near_in, far_in, q_all = move(near_out, far_out, q)
     solution = None
     for iteration in range(1, ITERS):
         width = 2 if iteration == ITERS - 1 else 3
         extra = [] if solution is None else [solution]
-        operands = [place, q_all, inverse_rows, extents, mats_all, t, near_in, far_in, res, *extra, natural, basis_pad]
+        operands = [place, q_all, inverse_rows, extents, mats_all, t, near_in, far_in, res, *extra,
+                    ordered_inverse, gather, basis_pad]
         solution, res, t, near_out, far_out, q = pl.pallas_call(
             functools.partial(middle_kernel, bool(extra)),
             out_shape=[field(planes), field(window), field(window), field(width), field(width), q_shape],

time: 86.6 us -> 75.5 us (0.87)
  blocking collectives: 27.5 us -> 39.2 us
  starting transfers between devices: 17.5 us -> 7.42 us
  local copies, waits for them, and re-layouts: 14.7 us -> 6.93 us
  other arithmetic: 5.12 us -> 0.08 us
  Pallas kernels: 19.3 us -> 20.6 us
    all_to_all x2 -> x3, blocking collectives: 27.5 us -> 39.2 us  [move(): q_all = lax.all_to_all(q, AXES, 0, 0).reshape(count * CV_DEV, cases)]
    all_to_all x1 -> x0, starting transfers between devices: 8.73 us -> none  [move(): q_all = lax.all_to_all(q, AXES, 0, 0).reshape(count * CV_DEV, cases)]
    slice x11 -> x0, local copies, waits for them, and re-layouts: 4.66 us -> none  [the longest x3 1.55 us: rows_of(): return [padded[:, i * 128:(i + 1) * 128] for i in range(blocks)]]
    concatenate x3 -> x0, other arithmetic: 2.84 us -> none  [the longest x1 1.34 us: body(): mats_all = jnp.concatenate([left_mats, mats, right_mats], axis=0)]
    pallas_call x2, Pallas kernels: 5.54 us -> 8.13 us  [body(): pl.pallas_call(functools.partial(middle_kernel, bool(extra)), out_shape=[...]
    pallas_call x1 -> x2, Pallas kernels: 9.46 us -> 7.12 us  [the longest x1 6.48 us: renumber(): pl.pallas_call(renumber_kernel, out_shape=[square, square], in_specs=[VME...]
    concatenate x6 -> x0, local copies, waits for them, and re-layouts: 1.53 us -> none  [the longest x2 0.78 us: body(): mats_all = jnp.concatenate([left_mats, mats, right_mats], axis=0)]
    pallas_call x1, Pallas kernels: 2.11 us -> 3.17 us  [body(): pl.pallas_call(first_kernel, out_shape=[field(window), field(window), fie...]
  transfers between devices with their start and end apart: 9 -> 8, of which waited for: 1 -> 0; matrix products, arithmetic and copies ran while one was open for 7% -> 0% of each run, Pallas kernels for 11% -> 9%
where the time goes in v2:
time: 75.5 us; the launch traced here: 75.1 us
  blocking collectives  39.2 us (52%)
  Pallas kernels  20.6 us (27%)
  starting transfers between devices  7.42 us (10%)
  local copies, waits for them, and re-layouts  6.93 us (9%)
  between operations  0.78 us (1%)
    all_to_all x3, blocking collectives, move(): q_all = lax.all_to_all(q, AXES, 0, 0).reshape(count * CV_DEV, cases)  39.2 us
    pallas_call x2, Pallas kernels, body(): pl.pallas_call(functools.partial(middle_kernel, bool(extra)), out_shape=[...  8.13 us
    pallas_call x1, Pallas kernels, renumber(): pl.pallas_call(renumber_kernel, out_shape=[square, square], in_specs=[VME...  6.48 us
    unnamed x18, local copies, waits for them, and re-layouts  6.12 us
    ppermute x3, starting transfers between devices, move(): near_in = lax.ppermute(near_out, AXES, near_pairs)  4.3 us
    pallas_call x1, Pallas kernels, body(): pl.pallas_call(first_kernel, out_shape=[field(window), field(window), fie...  3.17 us
    pallas_call x1, Pallas kernels, body(): pl.pallas_call(last_kernel, out_shape=[field(planes), field(planes), jax....  2.21 us
    ppermute x3, starting transfers between devices, move(): far_in = lax.ppermute(far_out, AXES, far_pairs)  2 us
  transfers between devices with their start and end apart: 8, of which 0 were waited for; matrix products, arithmetic and copies ran while one was open for 0% of the time, Pallas kernels for 9%

profile of v2, /device:TPU:0, one launch (start us, length us, event | category | flops | bytes accessed | tf_op | source)
XLA Modules:
  0.0 75.1 jit_solution(12978312470804167082)
XLA Ops:
  0.6 0.8 %pad.8.wide_ref = f32[4,1536]{1,0:T(4,128)S(1)} pad(f32[4,1152]{1,0:T(4,128)} %bitcast.17, f32[]{:T(128)} %constant.25.clone.1), padding=0_0x192_192 | pad | bytes 43012 | tf_op jit(solution)/shard_map/jit(_pad)/pad | solution.py:346
  1.5 1.0 %copy-done = f32[4,3,64,128]{3,2,1,0:T(8,128)S(1)} copy-done((f32[4,3,64,128]{3,2,1,0:T(8,128)S(1)}, f32[4,3,64,128]{3,2,1,0:T(8,128)}, u32[]{:S(2)}) %copy-start) | copy-done | bytes 393240
  2.5 0.7 copy-done.2
  3.2 0.7 copy-done.3
  3.9 0.7 copy-done.4
  4.6 0.7 copy-done.5
  5.2 0.6 shard_map.103
  5.8 0.5 collective-permute-start
  6.3 0.7 collective-permute-start.1
  7.0 1.7 %copy-done.6 = bf16[1,1152,1152]{2,1,0:T(8,128)(2,1)S(1)} copy-done((bf16[1,1152,1152]{2,1,0:T(8,128)(2,1)S(1)}, bf16[1,1152,1152]{2,1,0:T(8,128)(2,1)}, u32[]{:S(2)}) %copy-start.6) | copy-done | bytes 2654232
  8.7 0.7 copy-done.7
  9.4 6.5 %shard_map.104 = (bf16[1152,1152]{1,0:T(8,128)(2,1)S(1)}, bf16[1152,1152]{1,0:T(8,128)(2,1)S(1)}) custom-call(s32[1,1152]{1,0:T(1,128)S(1)} %copy-done.7, bf16[1152,1152]{1,0:T(8,128)(2,1)S(1)} %bitcast.16), custom_call_target="tpu_custom_call" | custom-call | flops 6115295232 | bytes 5308416 | tf_op jit(solution)/shard_map/pallas_call | solution.py:110
  16.0 3.2 %shard_map.105 = (f32[6,3,8,8,128]{4,3,2,1,0:T(8,128)S(1)}, f32[6,3,8,8,128]{4,3,2,1,0:T(8,128)S(1)}, f32[3,3,8,8,128]{4,3,2,1,0:T(8,128)S(1)}, f32[3,3,8,8,128]...) custom-call(s32[4]{0:T(128)S(1)} %pad_add_fusion.place_ref, ...), custom_call_target="tpu_custom_call" | custom-call | flops 339738624 | bytes 2654208 | tf_op jit(solution)/shard_map/pallas_call | solution.py:381
  19.1 3.9 %collective-permute-start.2 = (f32[3,3,8,8,128]{4,3,2,1,0:T(8,128)S(1)}, f32[3,3,8,8,128]{4,3,2,1,0:T(8,128)S(1)}, u32[]{:S(2)}, u32[]{:S(2)}) collective-permute-start(f32[3,3,8,8,128]{4,3,2,1,0:T(8,128)S(1)} %get-tuple-element.43), channel_id=1, source_target_pairs={{0,1},{1,0},{2,3},{3,2},{4,5},{5,4},{6,7},{7,6},{8,9},{9,8},{10,11... | collective-permute-start | bytes 884744 | tf_op jit(solution)/shard_map/ppermute | solution.py:376
  23.1 0.7 collective-permute-start.3
  23.8 15.3 %all_to_all.15 = f32[32,4,128]{2,1,0:T(4,128)S(1)} all-to-all(f32[32,4,128]{2,1,0:T(4,128)S(1)} %get-tuple-element.38), channel_id=1, replica_groups=mesh['sub'=16,'grp'=2] {'sub','grp'}, dimensions={0} | all-to-all | bytes 131072 | tf_op jit(solution)/shard_map/all_to_all | solution.py:378
  39.1 4.1 %shard_map.106 = (f32[4,3,8,8,128]{4,3,2,1,0:T(8,128)S(1)}, f32[6,3,8,8,128]{4,3,2,1,0:T(8,128)S(1)}, f32[6,3,8,8,128]{4,3,2,1,0:T(8,128)S(1)}, f32[3,3,8,8,128]...) custom-call(s32[4]{0:T(128)S(1)} %pad_add_fusion.place_ref, ...), custom_call_target="tpu_custom_call" | custom-call | flops 339738624 | bytes 2654208 | tf_op jit(solution)/shard_map/pallas_call | solution.py:405
  43.3 0.7 collective-permute-start.5
  44.0 11.8 %all_to_all.16 = f32[32,4,128]{2,1,0:T(4,128)S(1)} all-to-all(f32[32,4,128]{2,1,0:T(4,128)S(1)} %get-tuple-element.46), channel_id=1, replica_groups=mesh['sub'=16,'grp'=2] {'sub','grp'}, dimensions={0} | all-to-all | bytes 131072 | tf_op jit(solution)/shard_map/all_to_all | solution.py:378
  55.9 4.1 %shard_map.107 = (f32[4,3,8,8,128]{4,3,2,1,0:T(8,128)S(1)}, f32[6,3,8,8,128]{4,3,2,1,0:T(8,128)S(1)}, f32[6,3,8,8,128]{4,3,2,1,0:T(8,128)S(1)}, f32[2,3,8,8,128]...) custom-call(s32[4]{0:T(128)S(1)} %pad_add_fusion.place_ref, ...), custom_call_target="tpu_custom_call" | custom-call | flops 339738624 | bytes 2654208 | tf_op jit(solution)/shard_map/pallas_call | solution.py:405
  60.0 0.2 collective-permute-start.6
  60.1 0.7 collective-permute-start.7
  60.8 12.0 %all_to_all.17 = f32[32,4,128]{2,1,0:T(4,128)S(1)} all-to-all(f32[32,4,128]{2,1,0:T(4,128)S(1)} %get-tuple-element.52), channel_id=1, replica_groups=mesh['sub'=16,'grp'=2] {'sub','grp'}, dimensions={0} | all-to-all | bytes 131072 | tf_op jit(solution)/shard_map/all_to_all | solution.py:378
  72.9 2.2 %shard_map.108 = (f32[4,3,8,8,128]{4,3,2,1,0:T(8,128)}, f32[4,3,8,8,128]{4,3,2,1,0:T(8,128)}, f32[4,128]{1,0:T(4,128)}) custom-call(s32[4]{0:T(128)S(1)} %pad_add_fusion.place_ref, f32[128,128]{1,0:T(8,128)S(1)} %bitcast.15, f32[16,128]{1,0:T(8,128)S(1)} %get-tuple-element.39.rows_ref, f32[16,1536]{1,0:T(8,128)S(1)} %get-tuple-element.40.extent_ref, ...), custom_call_target="tpu_custom_call" | custom-call | tf_op jit(solution)/shard_map/pallas_call | solution.py:415
  (22 shorter events, 0.3 us)
Async XLA Ops:
  1.5 1.0 %copy-start = (f32[4,3,64,128]{3,2,1,0:T(8,128)S(1)}, f32[4,3,64,128]{3,2,1,0:T(8,128)}, u32[]{:S(2)}) copy-start(f32[4,3,64,128]{3,2,1,0:T(8,128)} %loads_ref.1) | copy-start | bytes 1179652
  2.5 0.7 copy-start.2
  3.2 0.7 copy-start.3
  3.9 0.7 copy-start.4
  4.6 0.7 copy-start.5
  5.8 10.1 %collective-permute-start = (f32[240,128]{1,0:T(8,128)S(1)}, f32[240,128]{1,0:T(8,128)S(1)}, u32[]{:S(2)}, u32[]{:S(2)}) collective-permute-start(f32[240,128]{1,0:T(8,128)S(1)} %get-tuple-element.32), channel_id=1, source_target_pairs={{0,1},{1,0},{2,3},{3,2},{4,5},{5,4},{6,7},{7,6},{8,9},{9,8},{10,11... | collective-permute-start | bytes 368648 | tf_op jit(solution)/shard_map/ppermute | solution.py:363
  6.3 9.6 %collective-permute-start.1 = (f32[240,128]{1,0:T(8,128)S(1)}, f32[240,128]{1,0:T(8,128)S(1)}, u32[]{:S(2)}, u32[]{:S(2)}) collective-permute-start(f32[240,128]{1,0:T(8,128)S(1)} %get-tuple-element.33), channel_id=1, source_target_pairs={{1,2},{2,1},{3,4},{4,3},{5,6},{6,5},{7,8},{8,7},{9,10},{10,9},{11,... | collective-permute-start | bytes 368648 | tf_op jit(solution)/shard_map/ppermute | solution.py:364
  7.0 1.8 %copy-start.6 = (bf16[1,1152,1152]{2,1,0:T(8,128)(2,1)S(1)}, bf16[1,1152,1152]{2,1,0:T(8,128)(2,1)}, u32[]{:S(2)}) copy-start(bf16[1,1152,1152]{2,1,0:T(8,128)(2,1)} %param.13) | copy-start | bytes 7962628
  8.7 0.7 copy-start.7
  9.4 6.5 %copy-start.8 = (f32[1,4,1152]{2,1,0:T(4,128)S(1)}, f32[1,4,1152]{2,1,0:T(4,128)}, u32[]{:S(2)}) copy-start(f32[1,4,1152]{2,1,0:T(4,128)} %param.14) | copy-start | bytes 55300
  9.4 6.5 %copy-start.1 = (f32[4,3,64,128]{3,2,1,0:T(8,128)S(1)}, f32[4,3,64,128]{3,2,1,0:T(8,128)}, u32[]{:S(2)}) copy-start(f32[4,3,64,128]{3,2,1,0:T(8,128)} %loads_ref.1) | copy-start | bytes 1179652
  19.1 19.9 %collective-permute-start.2 = (f32[3,3,8,8,128]{4,3,2,1,0:T(8,128)S(1)}, f32[3,3,8,8,128]{4,3,2,1,0:T(8,128)S(1)}, u32[]{:S(2)}, u32[]{:S(2)}) collective-permute-start(f32[3,3,8,8,128]{4,3,2,1,0:T(8,128)S(1)} %get-tuple-element.43), channel_id=1, source_target_pairs={{0,1},{1,0},{2,3},{3,2},{4,5},{5,4},{6,7},{7,6},{8,9},{9,8},{10,11... | collective-permute-start | bytes 884744 | tf_op jit(solution)/shard_map/ppermute | solution.py:376
  23.1 16.0 %collective-permute-start.3 = (f32[3,3,8,8,128]{4,3,2,1,0:T(8,128)S(1)}, f32[3,3,8,8,128]{4,3,2,1,0:T(8,128)S(1)}, u32[]{:S(2)}, u32[]{:S(2)}) collective-permute-start(f32[3,3,8,8,128]{4,3,2,1,0:T(8,128)S(1)} %get-tuple-element.44), channel_id=1, source_target_pairs={{1,2},{2,1},{3,4},{4,3},{5,6},{6,5},{7,8},{8,7},{9,10},{10,9},{11,... | collective-permute-start | bytes 884744 | tf_op jit(solution)/shard_map/ppermute | solution.py:377
  43.2 12.7 %collective-permute-start.4 = (f32[3,3,8,8,128]{4,3,2,1,0:T(8,128)S(1)}, f32[3,3,8,8,128]{4,3,2,1,0:T(8,128)S(1)}, u32[]{:S(2)}, u32[]{:S(2)}) collective-permute-start(f32[3,3,8,8,128]{4,3,2,1,0:T(8,128)S(1)} %get-tuple-element.48), channel_id=1, source_target_pairs={{0,1},{1,0},{2,3},{3,2},{4,5},{5,4},{6,7},{7,6},{8,9},{9,8},{10,11... | collective-permute-start | bytes 884744 | tf_op jit(solution)/shard_map/ppermute | solution.py:376
  43.3 12.5 %collective-permute-start.5 = (f32[3,3,8,8,128]{4,3,2,1,0:T(8,128)S(1)}, f32[3,3,8,8,128]{4,3,2,1,0:T(8,128)S(1)}, u32[]{:S(2)}, u32[]{:S(2)}) collective-permute-start(f32[3,3,8,8,128]{4,3,2,1,0:T(8,128)S(1)} %get-tuple-element.49), channel_id=1, source_target_pairs={{1,2},{2,1},{3,4},{4,3},{5,6},{6,5},{7,8},{8,7},{9,10},{10,9},{11,... | collective-permute-start | bytes 884744 | tf_op jit(solution)/shard_map/ppermute | solution.py:377
  60.0 12.9 %collective-permute-start.6 = (f32[2,3,8,8,128]{4,3,2,1,0:T(8,128)S(1)}, f32[2,3,8,8,128]{4,3,2,1,0:T(8,128)S(1)}, u32[]{:S(2)}, u32[]{:S(2)}) collective-permute-start(f32[2,3,8,8,128]{4,3,2,1,0:T(8,128)S(1)} %get-tuple-element.54), channel_id=1, source_target_pairs={{0,1},{1,0},{2,3},{3,2},{4,5},{5,4},{6,7},{7,6},{8,9},{9,8},{10,11... | collective-permute-start | bytes 589832 | tf_op jit(solution)/shard_map/ppermute | solution.py:376
  60.1 12.7 %collective-permute-start.7 = (f32[2,3,8,8,128]{4,3,2,1,0:T(8,128)S(1)}, f32[2,3,8,8,128]{4,3,2,1,0:T(8,128)S(1)}, u32[]{:S(2)}, u32[]{:S(2)}) collective-permute-start(f32[2,3,8,8,128]{4,3,2,1,0:T(8,128)S(1)} %get-tuple-element.55), channel_id=1, source_target_pairs={{1,2},{2,1},{3,4},{4,3},{5,6},{6,5},{7,8},{8,7},{9,10},{10,9},{11,... | collective-permute-start | bytes 589832 | tf_op jit(solution)/shard_map/ppermute | solution.py:377

commit v3 on v2

--- a/solution.py
+++ b/solution.py
@@ -16,8 +16,11 @@
 F32 = jnp.float32
 BF16 = jnp.bfloat16
 VMEM = pl.BlockSpec(memory_space=pltpu.VMEM)
+HBM = pl.BlockSpec(memory_space=pltpu.HBM)
 SMEM = pl.BlockSpec(memory_space=pltpu.SMEM)
 PARAMS = pltpu.CompilerParams(vmem_limit_bytes=24 * 1024 * 1024)
+WHOLE = pltpu.CompilerParams(vmem_limit_bytes=56 * 1024 * 1024)
+MOST = pltpu.CompilerParams(vmem_limit_bytes=50 * 1024 * 1024)
 
 
 def swap_pairs(count):
@@ -28,34 +31,53 @@
     return near, far
 
 
-def pack_kernel(place_ref, shear_ref, ratio_ref, loads_ref, labels_ref, wide_ref, coarse_ref,
-                near_ref, far_ref, mats_ref, rows_ref):
+def pack_kernel(place_ref, shear_hbm, ratio_hbm, loads_hbm, labels_hbm, basis_hbm, coarse_hbm,
+                near_ref, far_ref, mats_ref, rows_ref, wide_ref,
+                shear_ref, ratio_ref, near_load, far_load, labels_ref, basis_ref, coarse_ref, sems):
     planes, nodes = labels_ref.shape
-    plane_rows = loads_ref.shape[1] * loads_ref.shape[2]
-    even = place_ref[0] == 1
+    plane_rows, cases = near_load.shape[0] * near_load.shape[1], near_load.shape[2]
+    even = place_ref[0]
+    moves = [
+        (labels_hbm, labels_ref),
+        (shear_hbm, shear_ref),
+        (ratio_hbm, ratio_ref),
+        (basis_hbm, basis_ref),
+        (coarse_hbm, coarse_ref),
+        (loads_hbm.at[(planes - 1) * even], near_load),
+        (loads_hbm.at[(planes - 1) * (1 - even)], far_load),
+    ]
+    copies = [pltpu.make_async_copy(source, target, sems.at[i]) for i, (source, target) in enumerate(moves)]
+    for copy in copies:
+        copy.start()
+    even = even == 1
+    wide_ref[...] = jnp.zeros_like(wide_ref)
+    for copy in copies[:3]:
+        copy.wait()
     labels = labels_ref[...]
     shear = jnp.zeros((planes, nodes), F32)
     normal = jnp.zeros((planes, nodes), F32)
-    for region in range(shear_ref.shape[0]):
-        value = shear_ref[region]
+    for region in range(shear_ref.shape[1]):
+        value = shear_ref[:, region : region + 1]
         here = labels == region
         shear = jnp.where(here, value, shear)
-        normal = jnp.where(here, value * (2.0 + ratio_ref[region]), normal)
+        normal = jnp.where(here, value * (2.0 + ratio_ref[:, region : region + 1]), normal)
     both = jnp.concatenate([shear, normal], axis=1)
     mats_ref[...] = both
+    mats_l, mats_r = both[:2], both[planes - 2 :]
+    groups = group_count(plane_rows, coarse_ref.shape[1])
+    at = plane_rows + 8 * groups
+    near_ref[at : at + 2] = jnp.where(even, mats_r, mats_l)
+    far_ref[at : at + 2] = jnp.where(even, mats_l, mats_r)
+    for copy in copies[3:5]:
+        copy.wait()
+    wide_ref[:, plane_rows : plane_rows + basis_ref.shape[1]] = basis_ref[...]
     rows = coarse_ref[:CV_DEV]
     for member in range(1, coarse_ref.shape[0] // CV_DEV):
         rows = jnp.where(place_ref[3] == member, coarse_ref[member * CV_DEV : (member + 1) * CV_DEV], rows)
     rows_ref[...] = rows
     span = part_blocks(plane_rows)
-    load_l = loads_ref[0].reshape(plane_rows, loads_ref.shape[3])
-    load_r = loads_ref[planes - 1].reshape(plane_rows, loads_ref.shape[3])
-    mats_l, mats_r = both[:2], both[planes - 2 :]
     start_r = planes * plane_rows
     start_l = 4 * plane_rows - 128 * span
-    near_ref[:plane_rows] = jnp.where(even, load_r, load_l)
-    far_ref[:plane_rows] = jnp.where(even, load_l, load_r)
-    groups = group_count(plane_rows, coarse_ref.shape[1])
     for i in range(groups):
         at = plane_rows + 8 * i
         if i < span:
@@ -66,9 +88,10 @@
         if i * 128 < coarse_ref.shape[1]:
             near_ref[at + CV_DEV : at + 2 * CV_DEV] = rows[:, 128 * i : 128 * (i + 1)]
             far_ref[at + CV_DEV : at + 2 * CV_DEV] = rows[:, 128 * i : 128 * (i + 1)]
-    at = plane_rows + 8 * groups
-    near_ref[at : at + 2] = jnp.where(even, mats_r, mats_l)
-    far_ref[at : at + 2] = jnp.where(even, mats_l, mats_r)
+    for copy in copies[5:]:
+        copy.wait()
+    near_ref[:plane_rows] = near_load[...].reshape(plane_rows, cases)
+    far_ref[:plane_rows] = far_load[...].reshape(plane_rows, cases)
 
 
 def part_blocks(plane_rows):
@@ -79,45 +102,40 @@
     return max(part_blocks(plane_rows), coarse_order // 128)
 
 
-def renumber_kernel(order_ref, inverse_ref, out_ref, gather_ref, hot, held, sems):
-    size = inverse_ref.shape[0]
+def renumber_kernel(order_ref, inverse_hbm, out_ref, hot, held, columns, sems):
+    size = held.shape[0]
     step = size // 3
     copies = []
     for i in range(3):
         part = pl.ds(i * step, step)
-        copy = pltpu.make_async_copy(inverse_ref.at[:, part], held.at[:, part], sems.at[i])
+        copy = pltpu.make_async_copy(inverse_hbm.at[part, :], held.at[part, :], sems.at[i])
         copy.start()
         copies.append(copy)
     order = order_ref[...]
     for i in range(size // 128):
         row = lax.broadcasted_iota(jnp.int32, (128, size), 0) + i * 128
         hot[i * 128 : (i + 1) * 128, :] = jnp.where(row == order, 1.0, 0.0).astype(BF16)
-        turned = jnp.transpose(jnp.broadcast_to(order[:, i * 128 : (i + 1) * 128], (128, 128)))
-        for k in range(size // 128):
-            column = lax.broadcasted_iota(jnp.int32, (128, 128), 1) + k * 128
-            gather_ref[i * 128 : (i + 1) * 128, k * 128 : (k + 1) * 128] = jnp.where(
-                turned == column, 1.0, 0.0
-            ).astype(BF16)
     for i in range(3):
         part = slice(i * step, (i + 1) * step)
         copies[i].wait()
-        out_ref[:, part] = jnp.dot(hot[...], held[:, part], preferred_element_type=F32).astype(BF16)
+        columns[part, :] = lax.dot_general(
+            held[part, :], hot[...], (((1,), (1,)), ((), ())), preferred_element_type=F32
+        ).astype(BF16)
+    for i in range(3):
+        part = slice(i * step, (i + 1) * step)
+        out_ref[part, :] = jnp.dot(hot[part, :], columns[...], preferred_element_type=F32).astype(BF16)
 
 
 def renumber(order, inverse):
     size = inverse.shape[0]
-    square = jax.ShapeDtypeStruct((size, size), BF16)
+    square = pltpu.VMEM((size, size), BF16)
     return pl.pallas_call(
         renumber_kernel,
-        out_shape=[square, square],
-        in_specs=[VMEM, pl.BlockSpec(memory_space=pl.ANY)],
-        out_specs=[VMEM, VMEM],
-        scratch_shapes=[
-            pltpu.VMEM((size, size), BF16),
-            pltpu.VMEM((size, size), BF16),
-            pltpu.SemaphoreType.DMA((3,)),
-        ],
-        compiler_params=PARAMS,
+        out_shape=jax.ShapeDtypeStruct((size, size), BF16),
+        in_specs=[VMEM, HBM],
+        out_specs=VMEM,
+        scratch_shapes=[square, square, square, pltpu.SemaphoreType.DMA((3,))],
+        compiler_params=MOST,
         cost_estimate=pl.CostEstimate(flops=4 * size**3, bytes_accessed=4 * size * size, transcendentals=0),
     )(order, inverse)
 
@@ -177,16 +195,15 @@
     return high, (x - high.astype(F32)).astype(BF16)
 
 
-def products(place_ref, inverse_ref, gather_ref, basis_ref, res_ref, t_ref, near_ref, far_ref, q_ref):
+def products(place_ref, inverse_ref, basis_ref, res_ref, t_ref, near_ref, far_ref, q_ref):
     slots, rows, cases = res_ref.shape[0] * 3, NY * NZ, res_ref.shape[-1]
     size = slots * rows
     res = res_ref[...].reshape(size, cases)
     high, low = split(res)
-    ordered = jnp.dot(gather_ref[...], high, preferred_element_type=F32).astype(BF16)
     step = size // 3
     t_planes = t_ref.shape[0]
     for i in range(3):
-        block = jnp.dot(inverse_ref[i * step : (i + 1) * step, :], ordered, preferred_element_type=F32)
+        block = jnp.dot(inverse_ref[i * step : (i + 1) * step, :], high, preferred_element_type=F32)
         per = t_planes // 3
         t_ref[i * per : (i + 1) * per] = block.reshape(per, 3, NY, NZ, cases)
     even = place_ref[0]
@@ -204,7 +221,7 @@
 
 
 def first_kernel(place_ref, loads_ref, near_in_ref, far_in_ref, mats_in_ref, wide_ref, own_rows_ref,
-                 inverse_ref, gather_ref, basis_ref,
+                 inverse_ref, basis_ref,
                  res_ref, t_ref, near_ref, far_ref, q_ref, mats_ref, extent_ref, rows_ref):
     planes, components = loads_ref.shape[:2]
     cases = loads_ref.shape[-1]
@@ -219,7 +236,7 @@
     res_ref[0] = left.reshape(components, NY, NZ, cases)
     res_ref[1 : planes + 1] = loads_ref[...]
     res_ref[planes + 1] = right.reshape(components, NY, NZ, cases)
-    products(place_ref, inverse_ref, gather_ref, basis_ref, res_ref, t_ref, near_ref, far_ref, q_ref)
+    products(place_ref, inverse_ref, basis_ref, res_ref, t_ref, near_ref, far_ref, q_ref)
 
     extent = extent_ref.shape[1]
     span = part_blocks(plane_rows)
@@ -285,7 +302,7 @@
                   far_in_ref, res_in_ref, *rest):
     if with_solution:
         solution_in_ref, *rest = rest
-    inverse_ref, gather_ref, basis_ref, solution_ref, res_ref, t_ref, near_ref, far_ref, q_ref, z_ref = rest
+    inverse_ref, basis_ref, solution_ref, res_ref, t_ref, near_ref, far_ref, q_ref, z_ref = rest
     correction(place_ref, q_in_ref, rows_ref, extent_ref, t_in_ref, near_in_ref, far_in_ref, z_ref)
     window = res_ref.shape[0]
     for plane in range(1, window + 1):
@@ -299,7 +316,7 @@
             res_ref[plane - 1, component] = value
     own = RELAXATION * z_ref[2 : window]
     solution_ref[...] = solution_in_ref[...] + own if with_solution else own
-    products(place_ref, inverse_ref, gather_ref, basis_ref, res_ref, t_ref, near_ref, far_ref, q_ref)
+    products(place_ref, inverse_ref, basis_ref, res_ref, t_ref, near_ref, far_ref, q_ref)
 
 
 def last_kernel(place_ref, q_in_ref, rows_ref, extent_ref, mats_ref, t_in_ref, near_in_ref, far_in_ref, res_in_ref,
@@ -343,26 +360,36 @@
         ]
     )
     basis = coarse_basis[0]
-    wide = jnp.pad(basis, ((0, 0), (plane_rows, plane_rows)))
     basis_pad = jnp.pad(basis, ((0, 16 - CV_DEV), (0, 0)))
     extent = size + 2 * plane_rows
 
     packed = jax.ShapeDtypeStruct((plane_rows + 8 * group_count(plane_rows, coarse_order) + 8, cases), F32)
-    near_out, far_out, mats_own, own_rows = pl.pallas_call(
+    near_out, far_out, mats_own, own_rows, wide = pl.pallas_call(
         pack_kernel,
         out_shape=[
             packed,
             packed,
             jax.ShapeDtypeStruct((planes, 2 * nodes), F32),
             jax.ShapeDtypeStruct((CV_DEV, coarse_order), F32),
+            jax.ShapeDtypeStruct((CV_DEV, extent), F32),
         ],
-        in_specs=[SMEM] * 3 + [VMEM] * 4,
-        out_specs=[VMEM] * 4,
-        compiler_params=PARAMS,
-    )(place, shear_modulus, stiff_ratio, applied_loads, labels, wide, coarse_inverse)
+        in_specs=[SMEM] + [HBM] * 6,
+        out_specs=[VMEM] * 5,
+        scratch_shapes=[
+            pltpu.VMEM((1, shear_modulus.shape[0]), F32),
+            pltpu.VMEM((1, shear_modulus.shape[0]), F32),
+            pltpu.VMEM((components, nodes, cases), F32),
+            pltpu.VMEM((components, nodes, cases), F32),
+            pltpu.VMEM((planes, nodes), jnp.int32),
+            pltpu.VMEM((CV_DEV, size), F32),
+            pltpu.VMEM(coarse_inverse.shape, F32),
+            pltpu.SemaphoreType.DMA((7,)),
+        ],
+        compiler_params=WHOLE,
+    )(place, shear_modulus[None], stiff_ratio[None], applied_loads, labels, basis, coarse_inverse)
     near_in = lax.ppermute(near_out, AXES, near_pairs)
     far_in = lax.ppermute(far_out, AXES, far_pairs)
-    ordered_inverse, gather = renumber(local_order, local_inverse[0])
+    natural = renumber(local_order, local_inverse[0])
 
     def field(depth):
         return jax.ShapeDtypeStruct((depth, components, NY, NZ, cases), F32)
@@ -390,18 +417,18 @@
             jax.ShapeDtypeStruct((16, extent), F32),
             jax.ShapeDtypeStruct((16, coarse_order), F32),
         ],
-        in_specs=[SMEM] + [VMEM] * 9,
+        in_specs=[SMEM] + [VMEM] * 8,
         out_specs=[VMEM] * 8,
         compiler_params=PARAMS,
         cost_estimate=cost,
-    )(place, loads, near_in, far_in, mats_own, wide, own_rows, ordered_inverse, gather, basis_pad)
+    )(place, loads, near_in, far_in, mats_own, wide, own_rows, natural, basis_pad)
     near_in, far_in, q_all = move(near_out, far_out, q)
     solution = None
     for iteration in range(1, ITERS):
         width = 2 if iteration == ITERS - 1 else 3
         extra = [] if solution is None else [solution]
         operands = [place, q_all, inverse_rows, extents, mats_all, t, near_in, far_in, res, *extra,
-                    ordered_inverse, gather, basis_pad]
+                    natural, basis_pad]
         solution, res, t, near_out, far_out, q = pl.pallas_call(
             functools.partial(middle_kernel, bool(extra)),
             out_shape=[field(planes), field(window), field(window), field(width), field(width), q_shape],

time: 75.5 us -> 70.3 us (0.931)
  local copies, waits for them, and re-layouts: 6.93 us -> 0.72 us
    unnamed x18 -> x14, local copies, waits for them, and re-layouts: 6.12 us -> 0.71 us
    pallas_call x1, Pallas kernels: 6.48 us -> 9.66 us  [renumber(): pl.pallas_call(renumber_kernel, out_shape=jax.ShapeDtypeStruct((size, siz...]
    pallas_call x2, Pallas kernels: 8.13 us -> 5.23 us  [body(): pl.pallas_call(functools.partial(middle_kernel, bool(extra)), out_shape=[...]
    pallas_call x1, Pallas kernels: 0.63 us -> 2.45 us  [body(): pl.pallas_call(pack_kernel, out_shape=[packed, packed, jax.ShapeDtypeStru...]
    pallas_call x1, Pallas kernels: 3.17 us -> 1.54 us  [body(): pl.pallas_call(first_kernel, out_shape=[field(window), field(window), fie...]
    pad x1 -> x0, local copies, waits for them, and re-layouts: 0.8 us -> none  [body(): wide = jnp.pad(basis, ((0, 0), (plane_rows, plane_rows)))]
  transfers between devices with their start and end apart: 8 -> 8, of which waited for: 0 -> 0; matrix products, arithmetic and copies ran while one was open for 0% -> 0% of each run, Pallas kernels for 9% -> 14%
where the time goes in v3:
time: 70.3 us; the launch traced here: 70 us
  blocking collectives  39.2 us (56%)
  Pallas kernels  21.1 us (30%)
  starting transfers between devices  7.46 us (11%)
  between operations  0.83 us (1%)
  local copies, waits for them, and re-layouts  0.72 us (1%)
    all_to_all x3, blocking collectives, move(): q_all = lax.all_to_all(q, AXES, 0, 0).reshape(count * CV_DEV, cases)  39.2 us
    pallas_call x1, Pallas kernels, renumber(): pl.pallas_call(renumber_kernel, out_shape=jax.ShapeDtypeStruct((size, siz...  9.66 us
    pallas_call x2, Pallas kernels, body(): pl.pallas_call(functools.partial(middle_kernel, bool(extra)), out_shape=[...  5.23 us
    ppermute x3, starting transfers between devices, move(): near_in = lax.ppermute(near_out, AXES, near_pairs)  4.29 us
    pallas_call x1, Pallas kernels, body(): pl.pallas_call(pack_kernel, out_shape=[packed, packed, jax.ShapeDtypeStru...  2.45 us
    pallas_call x1, Pallas kernels, body(): pl.pallas_call(last_kernel, out_shape=[field(planes), field(planes), jax....  2.23 us
    ppermute x3, starting transfers between devices, move(): far_in = lax.ppermute(far_out, AXES, far_pairs)  2 us
    pallas_call x1, Pallas kernels, body(): pl.pallas_call(first_kernel, out_shape=[field(window), field(window), fie...  1.54 us
  transfers between devices with their start and end apart: 8, of which 0 were waited for; matrix products, arithmetic and copies ran while one was open for 0% of the time, Pallas kernels for 14%

profile of v3, /device:TPU:0, one launch (start us, length us, event | category | flops | bytes accessed | tf_op | source)
XLA Modules:
  0.0 70.0 jit_solution(6761988525803952264)
XLA Ops:
  0.6 0.6 pad_add_fusion.place_ref
  1.3 2.5 %shard_map.103 = (f32[240,128]{1,0:T(8,128)}, f32[240,128]{1,0:T(8,128)}, f32[4,128]{1,0:T(4,128)}, f32[4,128]{1,0:T(4,128)}, f32[4,1536]{1,0:T(4,128)}) custom-call(s32[4]{0:T(128)} %pad_add_fusion.place_ref, f32[1,8]{1,0:T(1,128)} %bitcast.20, f32[1,8]{1,0:T(1,128)} %bitcast.21, f32[4,3,64,128]{3,2,1,0:T(8,128)} %loads_hbm.1, s32[4,64]{1,0:T(4,128)} %labels_hbm.1, ...), custom_call_target="tpu_custom_call" | custom-call | tf_op jit(solution)/shard_map/pallas_call | solution.py:367
  3.7 0.5 collective-permute-start
  4.2 0.7 collective-permute-start.1
  4.9 0.0 copy-start.5
  4.9 0.7 copy-done.5
  5.6 0.0 copy-start.3
  5.6 9.7 %shard_map.104.inverse_ref.rest_0_.rest_1_ = bf16[1152,1152]{1,0:T(8,128)(2,1)S(1)} custom-call(s32[1,1152]{1,0:T(1,128)S(1)} %copy-done.5, bf16[1152,1152]{1,0:T(8,128)(2,1)} %bitcast.22), custom_call_target="tpu_custom_call" | custom-call | flops 6115295232 | bytes 5308416 | tf_op jit(solution)/shard_map/pallas_call | solution.py:132
  15.3 0.0 collective-permute-done.near_in_ref
  15.3 0.0 collective-permute-done.1.far_in_ref
  15.4 1.5 %shard_map.105 = (f32[6,3,8,8,128]{4,3,2,1,0:T(8,128)S(1)}, f32[6,3,8,8,128]{4,3,2,1,0:T(8,128)S(1)}, f32[3,3,8,8,128]{4,3,2,1,0:T(8,128)S(1)}, f32[3,3,8,8,128]...) custom-call(s32[4]{0:T(128)S(1)} %copy-done.2, ...), custom_call_target="tpu_custom_call" | custom-call | flops 339738624 | bytes 2654208 | tf_op jit(solution)/shard_map/pallas_call | solution.py:408
  17.0 3.9 %collective-permute-start.2 = (f32[3,3,8,8,128]{4,3,2,1,0:T(8,128)S(1)}, f32[3,3,8,8,128]{4,3,2,1,0:T(8,128)S(1)}, u32[]{:S(2)}, u32[]{:S(2)}) collective-permute-start(f32[3,3,8,8,128]{4,3,2,1,0:T(8,128)S(1)} %get-tuple-element.41), channel_id=1, source_target_pairs={{0,1},{1,0},{2,3},{3,2},{4,5},{5,4},{6,7},{7,6},{8,9},{9,8},{10,11... | collective-permute-start | bytes 884744 | tf_op jit(solution)/shard_map/ppermute | solution.py:403
  20.9 0.7 collective-permute-start.3
  21.6 15.3 %all_to_all.15 = f32[32,4,128]{2,1,0:T(4,128)S(1)} all-to-all(f32[32,4,128]{2,1,0:T(4,128)S(1)} %get-tuple-element.36), channel_id=1, replica_groups=mesh['sub'=16,'grp'=2] {'sub','grp'}, dimensions={0} | all-to-all | bytes 131072 | tf_op jit(solution)/shard_map/all_to_all | solution.py:405
  36.9 2.6 %shard_map.106 = (f32[4,3,8,8,128]{4,3,2,1,0:T(8,128)S(1)}, f32[6,3,8,8,128]{4,3,2,1,0:T(8,128)S(1)}, f32[6,3,8,8,128]{4,3,2,1,0:T(8,128)S(1)}, f32[3,3,8,8,128]...) custom-call(s32[4]{0:T(128)S(1)} %copy-done.2, f32[128,128]{1,0:T(8,128)S(1)} %bitcast.16, ...), custom_call_target="tpu_custom_call" | custom-call | flops 339738624 | bytes 2654208 | tf_op jit(solution)/shard_map/pallas_call | solution.py:432
  39.5 0.2 collective-permute-start.4
  39.7 0.7 collective-permute-start.5
  40.4 11.8 %all_to_all.16 = f32[32,4,128]{2,1,0:T(4,128)S(1)} all-to-all(f32[32,4,128]{2,1,0:T(4,128)S(1)} %get-tuple-element.44), channel_id=1, replica_groups=mesh['sub'=16,'grp'=2] {'sub','grp'}, dimensions={0} | all-to-all | bytes 131072 | tf_op jit(solution)/shard_map/all_to_all | solution.py:405
  52.2 0.0 collective-permute-done.4.near_in_ref
  52.2 2.6 %shard_map.107 = (f32[4,3,8,8,128]{4,3,2,1,0:T(8,128)S(1)}, f32[6,3,8,8,128]{4,3,2,1,0:T(8,128)S(1)}, f32[6,3,8,8,128]{4,3,2,1,0:T(8,128)S(1)}, f32[2,3,8,8,128]...) custom-call(s32[4]{0:T(128)S(1)} %copy-done.2, f32[128,128]{1,0:T(8,128)S(1)} %bitcast.15, ...), custom_call_target="tpu_custom_call" | custom-call | flops 339738624 | bytes 2654208 | tf_op jit(solution)/shard_map/pallas_call | solution.py:432
  54.9 0.2 collective-permute-start.6
  55.0 0.7 collective-permute-start.7
  55.7 12.1 %all_to_all.17 = f32[32,4,128]{2,1,0:T(4,128)S(1)} all-to-all(f32[32,4,128]{2,1,0:T(4,128)S(1)} %get-tuple-element.50), channel_id=1, replica_groups=mesh['sub'=16,'grp'=2] {'sub','grp'}, dimensions={0} | all-to-all | bytes 131072 | tf_op jit(solution)/shard_map/all_to_all | solution.py:405
  67.8 2.2 %shard_map.108 = (f32[4,3,8,8,128]{4,3,2,1,0:T(8,128)}, f32[4,3,8,8,128]{4,3,2,1,0:T(8,128)}, f32[4,128]{1,0:T(4,128)}) custom-call(s32[4]{0:T(128)S(1)} %copy-done.2, f32[128,128]{1,0:T(8,128)S(1)} %bitcast.17, f32[16,128]{1,0:T(8,128)S(1)} %get-tuple-element.37.rows_ref, f32[16,1536]{1,0:T(8,128)S(1)} %get-tuple-element.38.extent_ref, ...), custom_call_target="tpu_custom_call" | custom-call | tf_op jit(solution)/shard_map/pallas_call | solution.py:442
  (17 shorter events, 0.0 us)
Async XLA Ops:
  3.7 11.6 %collective-permute-start = (f32[240,128]{1,0:T(8,128)}, f32[240,128]{1,0:T(8,128)S(1)}, u32[]{:S(2)}, u32[]{:S(2)}) collective-permute-start(f32[240,128]{1,0:T(8,128)} %get-tuple-element.31), channel_id=1, source_target_pairs={{0,1},{1,0},{2,3},{3,2},{4,5},{5,4},{6,7},{7,6},{8,9},{9,8},{10,11... | collective-permute-start | bytes 368648 | tf_op jit(solution)/shard_map/ppermute | solution.py:390
  4.2 11.1 %collective-permute-start.1 = (f32[240,128]{1,0:T(8,128)}, f32[240,128]{1,0:T(8,128)S(1)}, u32[]{:S(2)}, u32[]{:S(2)}) collective-permute-start(f32[240,128]{1,0:T(8,128)} %get-tuple-element.32), channel_id=1, source_target_pairs={{1,2},{2,1},{3,4},{4,3},{5,6},{6,5},{7,8},{8,7},{9,10},{10,9},{11,... | collective-permute-start | bytes 368648 | tf_op jit(solution)/shard_map/ppermute | solution.py:391
  4.9 0.7 copy-start.5
  5.6 9.7 %copy-start.6 = (f32[1,4,1152]{2,1,0:T(4,128)S(1)}, f32[1,4,1152]{2,1,0:T(4,128)}, u32[]{:S(2)}) copy-start(f32[1,4,1152]{2,1,0:T(4,128)} %param.14) | copy-start | bytes 55300
  5.6 9.8 %copy-start = (f32[4,3,64,128]{3,2,1,0:T(8,128)S(1)}, f32[4,3,64,128]{3,2,1,0:T(8,128)}, u32[]{:S(2)}) copy-start(f32[4,3,64,128]{3,2,1,0:T(8,128)} %loads_hbm.1) | copy-start | bytes 1179652
  5.6 9.8 %copy-start.1 = (f32[4,1536]{1,0:T(4,128)S(1)}, f32[4,1536]{1,0:T(4,128)}, u32[]{:S(2)}) copy-start(f32[4,1536]{1,0:T(4,128)} %get-tuple-element.34.wide_ref) | copy-start | bytes 73732
  5.6 9.8 %copy-start.2 = (s32[4]{0:T(128)S(1)}, s32[4]{0:T(128)}, u32[]{:S(2)}) copy-start(s32[4]{0:T(128)} %pad_add_fusion.place_ref) | copy-start | bytes 52
  5.6 9.8 %copy-start.3 = (f32[4,128]{1,0:T(4,128)S(1)}, f32[4,128]{1,0:T(4,128)}, u32[]{:S(2)}) copy-start(f32[4,128]{1,0:T(4,128)} %get-tuple-element.33.mats_in_ref) | copy-start | bytes 6148
  5.6 9.8 %copy-start.4 = (f32[4,128]{1,0:T(4,128)S(1)}, f32[4,128]{1,0:T(4,128)}, u32[]{:S(2)}) copy-start(f32[4,128]{1,0:T(4,128)} %get-tuple-element.35.own_rows_ref) | copy-start | bytes 6148
  17.0 19.9 %collective-permute-start.2 = (f32[3,3,8,8,128]{4,3,2,1,0:T(8,128)S(1)}, f32[3,3,8,8,128]{4,3,2,1,0:T(8,128)S(1)}, u32[]{:S(2)}, u32[]{:S(2)}) collective-permute-start(f32[3,3,8,8,128]{4,3,2,1,0:T(8,128)S(1)} %get-tuple-element.41), channel_id=1, source_target_pairs={{0,1},{1,0},{2,3},{3,2},{4,5},{5,4},{6,7},{7,6},{8,9},{9,8},{10,11... | collective-permute-start | bytes 884744 | tf_op jit(solution)/shard_map/ppermute | solution.py:403
  20.9 16.0 %collective-permute-start.3 = (f32[3,3,8,8,128]{4,3,2,1,0:T(8,128)S(1)}, f32[3,3,8,8,128]{4,3,2,1,0:T(8,128)S(1)}, u32[]{:S(2)}, u32[]{:S(2)}) collective-permute-start(f32[3,3,8,8,128]{4,3,2,1,0:T(8,128)S(1)} %get-tuple-element.42), channel_id=1, source_target_pairs={{1,2},{2,1},{3,4},{4,3},{5,6},{6,5},{7,8},{8,7},{9,10},{10,9},{11,... | collective-permute-start | bytes 884744 | tf_op jit(solution)/shard_map/ppermute | solution.py:404
  39.5 12.7 %collective-permute-start.4 = (f32[3,3,8,8,128]{4,3,2,1,0:T(8,128)S(1)}, f32[3,3,8,8,128]{4,3,2,1,0:T(8,128)S(1)}, u32[]{:S(2)}, u32[]{:S(2)}) collective-permute-start(f32[3,3,8,8,128]{4,3,2,1,0:T(8,128)S(1)} %get-tuple-element.46), channel_id=1, source_target_pairs={{0,1},{1,0},{2,3},{3,2},{4,5},{5,4},{6,7},{7,6},{8,9},{9,8},{10,11... | collective-permute-start | bytes 884744 | tf_op jit(solution)/shard_map/ppermute | solution.py:403
  39.7 12.5 %collective-permute-start.5 = (f32[3,3,8,8,128]{4,3,2,1,0:T(8,128)S(1)}, f32[3,3,8,8,128]{4,3,2,1,0:T(8,128)S(1)}, u32[]{:S(2)}, u32[]{:S(2)}) collective-permute-start(f32[3,3,8,8,128]{4,3,2,1,0:T(8,128)S(1)} %get-tuple-element.47), channel_id=1, source_target_pairs={{1,2},{2,1},{3,4},{4,3},{5,6},{6,5},{7,8},{8,7},{9,10},{10,9},{11,... | collective-permute-start | bytes 884744 | tf_op jit(solution)/shard_map/ppermute | solution.py:404
  54.9 12.9 %collective-permute-start.6 = (f32[2,3,8,8,128]{4,3,2,1,0:T(8,128)S(1)}, f32[2,3,8,8,128]{4,3,2,1,0:T(8,128)S(1)}, u32[]{:S(2)}, u32[]{:S(2)}) collective-permute-start(f32[2,3,8,8,128]{4,3,2,1,0:T(8,128)S(1)} %get-tuple-element.52), channel_id=1, source_target_pairs={{0,1},{1,0},{2,3},{3,2},{4,5},{5,4},{6,7},{7,6},{8,9},{9,8},{10,11... | collective-permute-start | bytes 589832 | tf_op jit(solution)/shard_map/ppermute | solution.py:403
  55.0 12.7 %collective-permute-start.7 = (f32[2,3,8,8,128]{4,3,2,1,0:T(8,128)S(1)}, f32[2,3,8,8,128]{4,3,2,1,0:T(8,128)S(1)}, u32[]{:S(2)}, u32[]{:S(2)}) collective-permute-start(f32[2,3,8,8,128]{4,3,2,1,0:T(8,128)S(1)} %get-tuple-element.53), channel_id=1, source_target_pairs={{1,2},{2,1},{3,4},{4,3},{5,6},{6,5},{7,8},{8,7},{9,10},{10,9},{11,... | collective-permute-start | bytes 589832 | tf_op jit(solution)/shard_map/ppermute | solution.py:404

commit v4 on v3

--- a/solution.py
+++ b/solution.py
@@ -19,8 +19,16 @@
 HBM = pl.BlockSpec(memory_space=pltpu.HBM)
 SMEM = pl.BlockSpec(memory_space=pltpu.SMEM)
 PARAMS = pltpu.CompilerParams(vmem_limit_bytes=24 * 1024 * 1024)
+STAGE = pltpu.CompilerParams(vmem_limit_bytes=50 * 1024 * 1024)
 WHOLE = pltpu.CompilerParams(vmem_limit_bytes=56 * 1024 * 1024)
-MOST = pltpu.CompilerParams(vmem_limit_bytes=50 * 1024 * 1024)
+
+
+def position():
+    place = lax.axis_index(AXES)
+    even = 1 - lax.rem(place, 2)
+    has_left = (place > 0).astype(F32)
+    has_right = (place < lax.axis_size(AXES) - 1).astype(F32)
+    return even, has_left, has_right
 
 
 def swap_pairs(count):
@@ -31,12 +39,12 @@
     return near, far
 
 
-def pack_kernel(place_ref, shear_hbm, ratio_hbm, loads_hbm, labels_hbm, basis_hbm, coarse_hbm,
+def pack_kernel(shear_hbm, ratio_hbm, loads_hbm, labels_hbm, basis_hbm, coarse_hbm,
                 near_ref, far_ref, mats_ref, rows_ref, wide_ref,
                 shear_ref, ratio_ref, near_load, far_load, labels_ref, basis_ref, coarse_ref, sems):
     planes, nodes = labels_ref.shape
     plane_rows, cases = near_load.shape[0] * near_load.shape[1], near_load.shape[2]
-    even = place_ref[0]
+    even, _, _ = position()
     moves = [
         (labels_hbm, labels_ref),
         (shear_hbm, shear_ref),
@@ -73,7 +81,7 @@
     wide_ref[:, plane_rows : plane_rows + basis_ref.shape[1]] = basis_ref[...]
     rows = coarse_ref[:CV_DEV]
     for member in range(1, coarse_ref.shape[0] // CV_DEV):
-        rows = jnp.where(place_ref[3] == member, coarse_ref[member * CV_DEV : (member + 1) * CV_DEV], rows)
+        rows = jnp.where(lax.axis_index("grp") == member, coarse_ref[member * CV_DEV : (member + 1) * CV_DEV], rows)
     rows_ref[...] = rows
     span = part_blocks(plane_rows)
     start_r = planes * plane_rows
@@ -94,50 +102,28 @@
     far_ref[:plane_rows] = far_load[...].reshape(plane_rows, cases)
 
 
-def part_blocks(plane_rows):
-    return -(-3 * plane_rows // 128)
-
-
-def group_count(plane_rows, coarse_order):
-    return max(part_blocks(plane_rows), coarse_order // 128)
-
-
-def renumber_kernel(order_ref, inverse_hbm, out_ref, hot, held, columns, sems):
-    size = held.shape[0]
-    step = size // 3
+def stage_kernel(inverse_hbm, inverse_ref, sems):
+    step = inverse_ref.shape[0] // 3
     copies = []
     for i in range(3):
         part = pl.ds(i * step, step)
-        copy = pltpu.make_async_copy(inverse_hbm.at[part, :], held.at[part, :], sems.at[i])
+        copies.append(pltpu.make_async_copy(inverse_hbm.at[part, :], inverse_ref.at[part, :], sems.at[i]))
+    for copy in copies:
         copy.start()
-        copies.append(copy)
-    order = order_ref[...]
-    for i in range(size // 128):
-        row = lax.broadcasted_iota(jnp.int32, (128, size), 0) + i * 128
-        hot[i * 128 : (i + 1) * 128, :] = jnp.where(row == order, 1.0, 0.0).astype(BF16)
-    for i in range(3):
-        part = slice(i * step, (i + 1) * step)
-        copies[i].wait()
-        columns[part, :] = lax.dot_general(
-            held[part, :], hot[...], (((1,), (1,)), ((), ())), preferred_element_type=F32
-        ).astype(BF16)
-    for i in range(3):
-        part = slice(i * step, (i + 1) * step)
-        out_ref[part, :] = jnp.dot(hot[part, :], columns[...], preferred_element_type=F32).astype(BF16)
-
-
-def renumber(order, inverse):
-    size = inverse.shape[0]
-    square = pltpu.VMEM((size, size), BF16)
-    return pl.pallas_call(
-        renumber_kernel,
-        out_shape=jax.ShapeDtypeStruct((size, size), BF16),
-        in_specs=[VMEM, HBM],
-        out_specs=VMEM,
-        scratch_shapes=[square, square, square, pltpu.SemaphoreType.DMA((3,))],
-        compiler_params=MOST,
-        cost_estimate=pl.CostEstimate(flops=4 * size**3, bytes_accessed=4 * size * size, transcendentals=0),
-    )(order, inverse)
+    for copy in copies:
+        copy.wait()
+
+
+def on_lanes(row, shape):
+    return jnp.transpose(jnp.broadcast_to(row, (shape[-1], row.shape[1]))).reshape(shape[1:])
+
+
+def part_blocks(plane_rows):
+    return -(-3 * plane_rows // 128)
+
+
+def group_count(plane_rows, coarse_order):
+    return max(part_blocks(plane_rows), coarse_order // 128)
 
 
 def up_a(u):
@@ -195,22 +181,32 @@
     return high, (x - high.astype(F32)).astype(BF16)
 
 
-def products(place_ref, inverse_ref, basis_ref, res_ref, t_ref, near_ref, far_ref, q_ref):
-    slots, rows, cases = res_ref.shape[0] * 3, NY * NZ, res_ref.shape[-1]
-    size = slots * rows
-    res = res_ref[...].reshape(size, cases)
-    high, low = split(res)
+def block(plane, component):
+    start = (plane * 3 + component) * NY * NZ
+    return slice(start, start + NY * NZ)
+
+
+def node_grid(rows):
+    return rows.reshape(rows.shape[0] // (NY * NZ), NY, NZ, rows.shape[1])
+
+
+def products(order_ref, inverse_ref, basis_ref, ordered_ref, product_ref, res_ref, t_ref, near_ref, far_ref, q_ref):
+    size = res_ref.shape[0]
+    for row in range(size):
+        ordered_ref[row : row + 1, :] = res_ref[pl.ds(order_ref[0, row], 1), :]
+    ordered = ordered_ref[...].astype(BF16)
     step = size // 3
-    t_planes = t_ref.shape[0]
     for i in range(3):
-        block = jnp.dot(inverse_ref[i * step : (i + 1) * step, :], high, preferred_element_type=F32)
-        per = t_planes // 3
-        t_ref[i * per : (i + 1) * per] = block.reshape(per, 3, NY, NZ, cases)
-    even = place_ref[0]
+        part = slice(i * step, (i + 1) * step)
+        product_ref[part, :] = jnp.dot(inverse_ref[part, :], ordered, preferred_element_type=F32)
+        for row in range(i * step, (i + 1) * step):
+            t_ref[pl.ds(order_ref[0, row], 1), :] = product_ref[row : row + 1, :]
+    even, _, _ = position()
     width = near_ref.shape[0]
-    to_right = t_planes - width
-    near_ref[...] = t_ref[pl.ds(to_right * even, width)]
-    far_ref[...] = t_ref[pl.ds(to_right * (1 - even), width)]
+    to_right = size - width
+    near_ref[...] = t_ref[pl.ds(pl.multiple_of(to_right * even, 8), width), :]
+    far_ref[...] = t_ref[pl.ds(pl.multiple_of(to_right * (1 - even), 8), width), :]
+    high, low = split(res_ref[...])
     b_high, b_low = split(basis_ref[...])
     both = jnp.concatenate([b_high, b_low], axis=0)
     first = jnp.dot(both, high, preferred_element_type=F32)
@@ -220,23 +216,24 @@
     q_ref[...] = jnp.broadcast_to(q[None], q_ref.shape)
 
 
-def first_kernel(place_ref, loads_ref, near_in_ref, far_in_ref, mats_in_ref, wide_ref, own_rows_ref,
+def first_kernel(order_ref, loads_ref, near_in_ref, far_in_ref, mats_in_ref, wide_ref, own_rows_ref,
                  inverse_ref, basis_ref,
-                 res_ref, t_ref, near_ref, far_ref, q_ref, mats_ref, extent_ref, rows_ref):
-    planes, components = loads_ref.shape[:2]
+                 res_ref, t_ref, near_ref, far_ref, q_ref, mats_ref, extent_ref, rows_ref,
+                 ordered_ref, product_ref):
     cases = loads_ref.shape[-1]
-    plane_rows = components * NY * NZ
-    even = place_ref[0] == 1
+    plane_rows = 3 * NY * NZ
+    planes = loads_ref.shape[0] // plane_rows
+    even = position()[0] == 1
 
     def beside(start, stop):
         near, far = near_in_ref[start:stop], far_in_ref[start:stop]
         return jnp.where(even, far, near), jnp.where(even, near, far)
 
     left, right = beside(0, plane_rows)
-    res_ref[0] = left.reshape(components, NY, NZ, cases)
-    res_ref[1 : planes + 1] = loads_ref[...]
-    res_ref[planes + 1] = right.reshape(components, NY, NZ, cases)
-    products(place_ref, inverse_ref, basis_ref, res_ref, t_ref, near_ref, far_ref, q_ref)
+    res_ref[:plane_rows] = left
+    res_ref[plane_rows : (planes + 1) * plane_rows] = loads_ref[...]
+    res_ref[(planes + 1) * plane_rows :] = right
+    products(order_ref, inverse_ref, basis_ref, ordered_ref, product_ref, res_ref, t_ref, near_ref, far_ref, q_ref)
 
     extent = extent_ref.shape[1]
     span = part_blocks(plane_rows)
@@ -258,16 +255,17 @@
             rows_ref[2 * CV_DEV : 3 * CV_DEV, 128 * i : 128 * (i + 1)] = right
     at = plane_rows + 8 * groups
     left, right = beside(at, at + 2)
-    everything = [left[0:1], left[1:2]] + [mats_in_ref[p : p + 1] for p in range(planes)] + [right[0:1], right[1:2]]
-    for plane, row in enumerate(everything):
-        turned = jnp.transpose(jnp.broadcast_to(row, (cases, row.shape[1])))
-        mats_ref[plane] = turned.reshape(2, NY, NZ, cases)
-
-
-def correction(place_ref, q_ref, rows_ref, extent_ref, t_ref, near_ref, far_ref, z_ref):
-    width = near_ref.shape[0]
-    out_planes = t_ref.shape[0] + 2
-    cases = t_ref.shape[-1]
+    for plane in range(2):
+        mats_ref[plane] = on_lanes(left[plane : plane + 1], mats_ref.shape)
+        mats_ref[planes + 2 + plane] = on_lanes(right[plane : plane + 1], mats_ref.shape)
+    for plane in range(planes):
+        mats_ref[2 + plane] = on_lanes(mats_in_ref[plane : plane + 1], mats_ref.shape)
+
+
+def correction(q_ref, rows_ref, extent_ref, t_ref, near_ref, far_ref, z_ref):
+    plane_rows = 3 * NY * NZ
+    width = near_ref.shape[0] // plane_rows
+    out_planes = t_ref.shape[0] // plane_rows + 2
     coarse = jnp.dot(rows_ref[...], q_ref[...], precision=lax.Precision.HIGHEST, preferred_element_type=F32)
     c_high, c_low = split(coarse)
     e_high, e_low = split(extent_ref[...])
@@ -276,61 +274,66 @@
         jnp.concatenate([c_high, c_high, c_low], axis=0),
         (((0,), (0,)), ((), ())),
         preferred_element_type=F32,
-    ).reshape(out_planes, 3, NY, NZ, cases)
-    even = place_ref[0] == 1
-    has_left = place_ref[1].astype(F32)
-    has_right = place_ref[2].astype(F32)
+    )
+    even, has_left, has_right = position()
+    even = even == 1
+
+    def rows_at(ref, plane):
+        return ref[plane * plane_rows : (plane + 1) * plane_rows]
+
     for plane in range(3 - width, out_planes - 3 + width):
-        value = spread[plane]
+        value = spread[plane * plane_rows : (plane + 1) * plane_rows]
         if 1 <= plane < out_planes - 1:
-            value = value + t_ref[plane - 1]
+            value = value + rows_at(t_ref, plane - 1)
         if plane < 3:
             at = plane - (3 - width)
-            value = value + jnp.where(even, far_ref[at], near_ref[at])
+            value = value + jnp.where(even, rows_at(far_ref, at), rows_at(near_ref, at))
         if plane >= out_planes - 3:
             at = plane - (out_planes - 3)
-            value = value + jnp.where(even, near_ref[at], far_ref[at])
+            value = value + jnp.where(even, rows_at(near_ref, at), rows_at(far_ref, at))
         if plane < 2:
             value = value * has_left
         if plane >= out_planes - 2:
             value = value * has_right
-        z_ref[plane] = value
+        z_ref[plane] = node_grid(value)
     return coarse
 
 
-def middle_kernel(with_solution, place_ref, q_in_ref, rows_ref, extent_ref, mats_ref, t_in_ref, near_in_ref,
+def middle_kernel(with_solution, order_ref, q_in_ref, rows_ref, extent_ref, mats_ref, t_in_ref, near_in_ref,
                   far_in_ref, res_in_ref, *rest):
     if with_solution:
         solution_in_ref, *rest = rest
-    inverse_ref, basis_ref, solution_ref, res_ref, t_ref, near_ref, far_ref, q_ref, z_ref = rest
-    correction(place_ref, q_in_ref, rows_ref, extent_ref, t_in_ref, near_in_ref, far_in_ref, z_ref)
-    window = res_ref.shape[0]
+    inverse_ref, basis_ref, solution_ref, res_ref, t_ref, near_ref, far_ref, q_ref, z_ref, *scratch = rest
+    correction(q_in_ref, rows_ref, extent_ref, t_in_ref, near_in_ref, far_in_ref, z_ref)
+    _, has_left, has_right = position()
+    window = z_ref.shape[0] - 2
     for plane in range(1, window + 1):
         applied = stencil_plane(mats_ref, plane, lambda p, c: z_ref[p, c])
         for component in range(3):
-            value = res_in_ref[plane - 1, component] - RELAXATION * applied[component]
+            at = block(plane - 1, component)
+            value = res_in_ref[at] - RELAXATION * applied[component].reshape(NY * NZ, res_ref.shape[1])
             if plane == 1:
-                value = value * place_ref[1].astype(F32)
+                value = value * has_left
             if plane == window:
-                value = value * place_ref[2].astype(F32)
-            res_ref[plane - 1, component] = value
-    own = RELAXATION * z_ref[2 : window]
+                value = value * has_right
+            res_ref[at] = value
+    own = RELAXATION * z_ref[2:window].reshape(solution_ref.shape)
     solution_ref[...] = solution_in_ref[...] + own if with_solution else own
-    products(place_ref, inverse_ref, basis_ref, res_ref, t_ref, near_ref, far_ref, q_ref)
-
-
-def last_kernel(place_ref, q_in_ref, rows_ref, extent_ref, mats_ref, t_in_ref, near_in_ref, far_in_ref, res_in_ref,
+    products(order_ref, inverse_ref, basis_ref, *scratch, res_ref, t_ref, near_ref, far_ref, q_ref)
+
+
+def last_kernel(q_in_ref, rows_ref, extent_ref, mats_ref, t_in_ref, near_in_ref, far_in_ref, res_in_ref,
                 solution_in_ref, solution_ref, residual_ref, coarse_ref, z_ref):
-    coarse = correction(place_ref, q_in_ref, rows_ref, extent_ref, t_in_ref, near_in_ref, far_in_ref, z_ref)
+    coarse = correction(q_in_ref, rows_ref, extent_ref, t_in_ref, near_in_ref, far_in_ref, z_ref)
     coarse_ref[...] = coarse[CV_DEV : 2 * CV_DEV]
-    planes = solution_ref.shape[0]
+    planes = z_ref.shape[0] - 4
+    solution_ref[...] = solution_in_ref[...] + RELAXATION * z_ref[2 : planes + 2].reshape(solution_ref.shape)
     for plane in range(2, planes + 2):
         applied = stencil_plane(mats_ref, plane, lambda p, c: z_ref[p, c])
         for component in range(3):
-            residual_ref[plane - 2, component] = (
-                res_in_ref[plane - 1, component] - RELAXATION * applied[component]
-            )
-    solution_ref[...] = solution_in_ref[...] + RELAXATION * z_ref[2 : planes + 2]
+            residual_ref[block(plane - 2, component)] = res_in_ref[
+                block(plane - 1, component)
+            ] - RELAXATION * applied[component].reshape(NY * NZ, residual_ref.shape[1])
 
 
 def body(
@@ -348,17 +351,8 @@
     plane_rows = components * nodes
     size = window * plane_rows
     coarse_order = coarse_inverse.shape[1]
-    position = lax.axis_index(AXES)
     count = lax.axis_size(AXES)
     near_pairs, far_pairs = swap_pairs(count)
-    place = jnp.stack(
-        [
-            (position % 2 == 0).astype(jnp.int32),
-            (position > 0).astype(jnp.int32),
-            (position < count - 1).astype(jnp.int32),
-            lax.axis_index("grp").astype(jnp.int32),
-        ]
-    )
     basis = coarse_basis[0]
     basis_pad = jnp.pad(basis, ((0, 16 - CV_DEV), (0, 0)))
     extent = size + 2 * plane_rows
@@ -373,7 +367,7 @@
             jax.ShapeDtypeStruct((CV_DEV, coarse_order), F32),
             jax.ShapeDtypeStruct((CV_DEV, extent), F32),
         ],
-        in_specs=[SMEM] + [HBM] * 6,
+        in_specs=[HBM] * 6,
         out_specs=[VMEM] * 5,
         scratch_shapes=[
             pltpu.VMEM((1, shear_modulus.shape[0]), F32),
@@ -386,18 +380,18 @@
             pltpu.SemaphoreType.DMA((7,)),
         ],
         compiler_params=WHOLE,
-    )(place, shear_modulus[None], stiff_ratio[None], applied_loads, labels, basis, coarse_inverse)
+    )(shear_modulus[None], stiff_ratio[None], applied_loads, labels, basis, coarse_inverse)
     near_in = lax.ppermute(near_out, AXES, near_pairs)
     far_in = lax.ppermute(far_out, AXES, far_pairs)
-    natural = renumber(local_order, local_inverse[0])
 
     def field(depth):
-        return jax.ShapeDtypeStruct((depth, components, NY, NZ, cases), F32)
+        return jax.ShapeDtypeStruct((depth * plane_rows, cases), F32)
 
     q_shape = jax.ShapeDtypeStruct((count, CV_DEV, cases), F32)
     cost = pl.CostEstimate(flops=2 * size * size * cases, bytes_accessed=2 * size * size, transcendentals=0)
     z_scratch = pltpu.VMEM((planes + 4, components, NY, NZ, cases), F32)
-    loads = applied_loads.reshape(planes, components, NY, NZ, cases)
+    scratch = [pltpu.VMEM((size, cases), F32), pltpu.VMEM((size, cases), F32)]
+    loads = applied_loads.reshape(planes * plane_rows, cases)
 
     def move(near_out, far_out, q):
         near_in = lax.ppermute(near_out, AXES, near_pairs)
@@ -405,6 +399,15 @@
         q_all = lax.all_to_all(q, AXES, 0, 0).reshape(count * CV_DEV, cases)
         return near_in, far_in, q_all
 
+    inverse = pl.pallas_call(
+        stage_kernel,
+        out_shape=jax.ShapeDtypeStruct((size, size), BF16),
+        in_specs=[HBM],
+        out_specs=VMEM,
+        scratch_shapes=[pltpu.SemaphoreType.DMA((3,))],
+        compiler_params=STAGE,
+        cost_estimate=pl.CostEstimate(flops=4 * size**3, bytes_accessed=4 * size * size, transcendentals=0),
+    )(local_inverse[0])
     res, t, near_out, far_out, q, mats_all, extents, inverse_rows = pl.pallas_call(
         first_kernel,
         out_shape=[
@@ -419,22 +422,23 @@
         ],
         in_specs=[SMEM] + [VMEM] * 8,
         out_specs=[VMEM] * 8,
+        scratch_shapes=scratch,
         compiler_params=PARAMS,
         cost_estimate=cost,
-    )(place, loads, near_in, far_in, mats_own, wide, own_rows, natural, basis_pad)
+    )(local_order, loads, near_in, far_in, mats_own, wide, own_rows, inverse, basis_pad)
     near_in, far_in, q_all = move(near_out, far_out, q)
     solution = None
     for iteration in range(1, ITERS):
         width = 2 if iteration == ITERS - 1 else 3
         extra = [] if solution is None else [solution]
-        operands = [place, q_all, inverse_rows, extents, mats_all, t, near_in, far_in, res, *extra,
-                    natural, basis_pad]
+        operands = [local_order, q_all, inverse_rows, extents, mats_all, t, near_in, far_in, res, *extra,
+                    inverse, basis_pad]
         solution, res, t, near_out, far_out, q = pl.pallas_call(
             functools.partial(middle_kernel, bool(extra)),
             out_shape=[field(planes), field(window), field(window), field(width), field(width), q_shape],
             in_specs=[SMEM] + [VMEM] * (len(operands) - 1),
             out_specs=[VMEM] * 6,
-            scratch_shapes=[z_scratch],
+            scratch_shapes=[z_scratch, *scratch],
             compiler_params=PARAMS,
             cost_estimate=cost,
         )(*operands)
@@ -442,11 +446,11 @@
     solution, residual, coarse_values = pl.pallas_call(
         last_kernel,
         out_shape=[field(planes), field(planes), jax.ShapeDtypeStruct((CV_DEV, cases), F32)],
-        in_specs=[SMEM] + [VMEM] * 9,
+        in_specs=[VMEM] * 9,
         out_specs=[VMEM] * 3,
         scratch_shapes=[z_scratch],
         compiler_params=PARAMS,
-    )(place, q_all, inverse_rows, extents, mats_all, t, near_in, far_in, res, solution)
+    )(q_all, inverse_rows, extents, mats_all, t, near_in, far_in, res, solution)
     return (
         solution.reshape(planes, components, nodes, cases),
         residual.reshape(planes, components, nodes, cases),

time: 70.3 us -> 65.8 us (0.936)
  Pallas kernels: 21.1 us -> 15.3 us
  blocking collectives: 39.2 us -> 40.7 us
  starting transfers between devices: 7.46 us -> 8.7 us
    pallas_call x1, Pallas kernels: 9.66 us -> 1.77 us  [body(): pl.pallas_call(stage_kernel, out_shape=jax.ShapeDtypeStruct((size, size),...]
    pallas_call x2, Pallas kernels: 5.23 us -> 7.38 us  [body(): pl.pallas_call(functools.partial(middle_kernel, bool(extra)), out_shape=[...]
    all_to_all x3, blocking collectives: 39.2 us -> 40.7 us  [move(): q_all = lax.all_to_all(q, AXES, 0, 0).reshape(count * CV_DEV, cases)]
    ppermute x3, starting transfers between devices: 4.29 us -> 5.53 us  [move(): near_in = lax.ppermute(near_out, AXES, near_pairs)]
    pallas_call x1, Pallas kernels: 1.54 us -> 2.61 us  [body(): pl.pallas_call(first_kernel, out_shape=[field(window), field(window), fie...]
  transfers between devices with their start and end apart: 8 -> 8, of which waited for: 0 -> 0; matrix products, arithmetic and copies ran while one was open for 0% -> 0% of each run, Pallas kernels for 14% -> 3%
where the time goes in v4:
time: 65.8 us; the launch traced here: 65.5 us
  blocking collectives  40.7 us (62%)
  Pallas kernels  15.3 us (23%)
  starting transfers between devices  8.7 us (13%)
  between operations  0.83 us (1%)
    all_to_all x3, blocking collectives, move(): q_all = lax.all_to_all(q, AXES, 0, 0).reshape(count * CV_DEV, cases)  40.7 us
    pallas_call x2, Pallas kernels, body(): pl.pallas_call(functools.partial(middle_kernel, bool(extra)), out_shape=[...  7.38 us
    ppermute x3, starting transfers between devices, move(): near_in = lax.ppermute(near_out, AXES, near_pairs)  5.53 us
    pallas_call x1, Pallas kernels, body(): pl.pallas_call(first_kernel, out_shape=[field(window), field(window), fie...  2.61 us
    ppermute x3, starting transfers between devices, move(): far_in = lax.ppermute(far_out, AXES, far_pairs)  2 us
    pallas_call x1, Pallas kernels, body(): pl.pallas_call(pack_kernel, out_shape=[packed, packed, jax.ShapeDtypeStru...  1.79 us
    pallas_call x1, Pallas kernels, body(): pl.pallas_call(stage_kernel, out_shape=jax.ShapeDtypeStruct((size, size),...  1.77 us
    pallas_call x1, Pallas kernels, body(): pl.pallas_call(last_kernel, out_shape=[field(planes), field(planes), jax....  1.71 us
  transfers between devices with their start and end apart: 8, of which 0 were waited for; matrix products, arithmetic and copies ran while one was open for 0% of the time, Pallas kernels for 3%

profile of v4, /device:TPU:0, one launch (start us, length us, event | category | flops | bytes accessed | tf_op | source)
XLA Modules:
  0.0 65.5 jit_solution(8252342917522528109)
XLA Ops:
  0.6 1.8 %shard_map.103 = (f32[240,128]{1,0:T(8,128)}, f32[240,128]{1,0:T(8,128)}, f32[4,128]{1,0:T(4,128)}, f32[4,128]{1,0:T(4,128)}, f32[4,1536]{1,0:T(4,128)}) custom-call(f32[1,8]{1,0:T(1,128)} %bitcast.16, f32[1,8]{1,0:T(1,128)} %bitcast.17, f32[4,3,64,128]{3,2,1,0:T(8,128)} %loads_hbm.1, s32[4,64]{1,0:T(4,128)} %labels_hbm.1, f32[4,1152]{1,0:T(4,128)} %bitcast.14, ...), custom_call_target="tpu_custom_call" | custom-call | tf_op jit(solution)/shard_map/pallas_call | solution.py:361
  2.4 0.5 collective-permute-start
  2.9 0.7 %collective-permute-start.1 = (f32[240,128]{1,0:T(8,128)}, f32[240,128]{1,0:T(8,128)S(1)}, u32[]{:S(2)}, u32[]{:S(2)}) collective-permute-start(f32[240,128]{1,0:T(8,128)} %get-tuple-element.32), channel_id=1, source_target_pairs={{1,2},{2,1},{3,4},{4,3},{5,6},{6,5},{7,8},{8,7},{9,10},{10,9},{11,... | collective-permute-start | bytes 368648 | tf_op jit(solution)/shard_map/ppermute | solution.py:385
  3.6 0.0 copy-start.5
  3.6 0.0 copy-start
  3.6 0.0 copy-start.1
  3.7 0.0 copy-start.3
  3.7 1.8 %shard_map.104.inverse_ref.rest_0_.rest_1_ = bf16[1152,1152]{1,0:T(8,128)(2,1)S(1)} custom-call(bf16[1152,1152]{1,0:T(8,128)(2,1)} %bitcast.18), custom_call_target="tpu_custom_call" | custom-call | flops 6115295232 | bytes 5308416 | tf_op jit(solution)/shard_map/pallas_call | solution.py:402
  5.5 0.0 collective-permute-done.near_in_ref
  5.6 2.6 %shard_map.105 = (f32[1152,128]{1,0:T(8,128)S(1)}, f32[1152,128]{1,0:T(8,128)S(1)}, f32[576,128]{1,0:T(8,128)S(1)}, f32[576,128]{1,0:T(8,128)S(1)}, f32[32,4,128...) custom-call(s32[1,1152]{1,0:T(1,128)S(1)} %copy-done.1, ...), custom_call_target="tpu_custom_call" | custom-call | flops 339738624 | bytes 2654208 | tf_op jit(solution)/shard_map/pallas_call | solution.py:411
  8.2 5.2 %collective-permute-start.2 = (f32[576,128]{1,0:T(8,128)S(1)}, f32[576,128]{1,0:T(8,128)S(1)}, u32[]{:S(2)}, u32[]{:S(2)}) collective-permute-start(f32[576,128]{1,0:T(8,128)S(1)} %get-tuple-element.41), channel_id=1, source_target_pairs={{0,1},{1,0},{2,3},{3,2},{4,5},{5,4},{6,7},{7,6},{8,9},{9,8},{10,11... | collective-permute-start | bytes 884744 | tf_op jit(solution)/shard_map/ppermute | solution.py:397
  13.4 0.7 %collective-permute-start.3 = (f32[576,128]{1,0:T(8,128)S(1)}, f32[576,128]{1,0:T(8,128)S(1)}, u32[]{:S(2)}, u32[]{:S(2)}) collective-permute-start(f32[576,128]{1,0:T(8,128)S(1)} %get-tuple-element.42), channel_id=1, source_target_pairs={{1,2},{2,1},{3,4},{4,3},{5,6},{6,5},{7,8},{8,7},{9,10},{10,9},{11,... | collective-permute-start | bytes 884744 | tf_op jit(solution)/shard_map/ppermute | solution.py:398
  14.0 16.6 %all_to_all.15 = f32[32,4,128]{2,1,0:T(4,128)S(1)} all-to-all(f32[32,4,128]{2,1,0:T(4,128)S(1)} %get-tuple-element.36), channel_id=1, replica_groups=mesh['sub'=16,'grp'=2] {'sub','grp'}, dimensions={0} | all-to-all | bytes 131072 | tf_op jit(solution)/shard_map/all_to_all | solution.py:399
  30.6 0.0 collective-permute-done.2.near_in_ref
  30.6 0.0 collective-permute-done.3.far_in_ref
  30.6 3.7 %shard_map.106 = (f32[768,128]{1,0:T(8,128)S(1)}, f32[1152,128]{1,0:T(8,128)S(1)}, f32[1152,128]{1,0:T(8,128)S(1)}, f32[576,128]{1,0:T(8,128)S(1)}, f32[576,128]{1,0:T(8,128)S(1)}, /*index=5*/f32[32,4,128]{2,1,0:T(4,128)S(1)}) custom-call(s32[1,1152]{1,0:T(1,128)S(1)} %copy-done.1, f32[128,128]{1,0:T(8,128)S(1)} %bitcast.12, ...), custom_call_target="tpu_custom_call" | custom-call | flops 339738624 | bytes 2654208 | tf_op jit(solution)/shard_map/pallas_call | solution.py:436
  34.3 0.2 collective-permute-start.4
  34.5 0.7 %collective-permute-start.5 = (f32[576,128]{1,0:T(8,128)S(1)}, f32[576,128]{1,0:T(8,128)S(1)}, u32[]{:S(2)}, u32[]{:S(2)}) collective-permute-start(f32[576,128]{1,0:T(8,128)S(1)} %get-tuple-element.47), channel_id=1, source_target_pairs={{1,2},{2,1},{3,4},{4,3},{5,6},{6,5},{7,8},{8,7},{9,10},{10,9},{11,... | collective-permute-start | bytes 884744 | tf_op jit(solution)/shard_map/ppermute | solution.py:398
  35.2 12.3 %all_to_all.16 = f32[32,4,128]{2,1,0:T(4,128)S(1)} all-to-all(f32[32,4,128]{2,1,0:T(4,128)S(1)} %get-tuple-element.44), channel_id=1, replica_groups=mesh['sub'=16,'grp'=2] {'sub','grp'}, dimensions={0} | all-to-all | bytes 131072 | tf_op jit(solution)/shard_map/all_to_all | solution.py:399
  47.5 3.7 %shard_map.107 = (f32[768,128]{1,0:T(8,128)S(1)}, f32[1152,128]{1,0:T(8,128)S(1)}, f32[1152,128]{1,0:T(8,128)S(1)}, f32[384,128]{1,0:T(8,128)S(1)}, f32[384,128]{1,0:T(8,128)S(1)}, /*index=5*/f32[32,4,128]{2,1,0:T(4,128)S(1)}) custom-call(s32[1,1152]{1,0:T(1,128)S(1)} %copy-done.1, f32[128,128]{1,0:T(8,128)S(1)} %bitcast.11, ...), custom_call_target="tpu_custom_call" | custom-call | flops 339738624 | bytes 2654208 | tf_op jit(solution)/shard_map/pallas_call | solution.py:436
  51.2 0.2 collective-permute-start.6
  51.4 0.7 %collective-permute-start.7 = (f32[384,128]{1,0:T(8,128)S(1)}, f32[384,128]{1,0:T(8,128)S(1)}, u32[]{:S(2)}, u32[]{:S(2)}) collective-permute-start(f32[384,128]{1,0:T(8,128)S(1)} %get-tuple-element.53), channel_id=1, source_target_pairs={{1,2},{2,1},{3,4},{4,3},{5,6},{6,5},{7,8},{8,7},{9,10},{10,9},{11,... | collective-permute-start | bytes 589832 | tf_op jit(solution)/shard_map/ppermute | solution.py:398
  52.1 11.8 %all_to_all.17 = f32[32,4,128]{2,1,0:T(4,128)S(1)} all-to-all(f32[32,4,128]{2,1,0:T(4,128)S(1)} %get-tuple-element.50), channel_id=1, replica_groups=mesh['sub'=16,'grp'=2] {'sub','grp'}, dimensions={0} | all-to-all | bytes 131072 | tf_op jit(solution)/shard_map/all_to_all | solution.py:399
  63.8 1.7 %shard_map.108 = (f32[768,128]{1,0:T(8,128)}, f32[768,128]{1,0:T(8,128)}, f32[4,128]{1,0:T(4,128)}) custom-call(f32[128,128]{1,0:T(8,128)S(1)} %bitcast.13, f32[16,128]{1,0:T(8,128)S(1)} %get-tuple-element.37.rows_ref, f32[16,1536]{1,0:T(8,128)S(1)} %get-tuple-element.38.extent_ref, f32[8,2,8,8,128]{4,3,2,1,0:T(8,128)S(1)} %get-tuple-element.39.mats_ref, ...), custom_call_target="tpu_custom_call" | custom-call | tf_op jit(solution)/shard_map/pallas_call | solution.py:446
  (14 shorter events, 0.0 us)
Async XLA Ops:
  2.4 3.1 %collective-permute-start = (f32[240,128]{1,0:T(8,128)}, f32[240,128]{1,0:T(8,128)S(1)}, u32[]{:S(2)}, u32[]{:S(2)}) collective-permute-start(f32[240,128]{1,0:T(8,128)} %get-tuple-element.31), channel_id=1, source_target_pairs={{0,1},{1,0},{2,3},{3,2},{4,5},{5,4},{6,7},{7,6},{8,9},{9,8},{10,11... | collective-permute-start | bytes 368648 | tf_op jit(solution)/shard_map/ppermute | solution.py:384
  2.9 2.5 %collective-permute-start.1 = (f32[240,128]{1,0:T(8,128)}, f32[240,128]{1,0:T(8,128)S(1)}, u32[]{:S(2)}, u32[]{:S(2)}) collective-permute-start(f32[240,128]{1,0:T(8,128)} %get-tuple-element.32), channel_id=1, source_target_pairs={{1,2},{2,1},{3,4},{4,3},{5,6},{6,5},{7,8},{8,7},{9,10},{10,9},{11,... | collective-permute-start | bytes 368648 | tf_op jit(solution)/shard_map/ppermute | solution.py:385
  3.6 1.8 %copy-start.5 = (f32[1,4,1152]{2,1,0:T(4,128)S(1)}, f32[1,4,1152]{2,1,0:T(4,128)}, u32[]{:S(2)}) copy-start(f32[1,4,1152]{2,1,0:T(4,128)} %param.14) | copy-start | bytes 55300
  3.6 1.9 %copy-start = (f32[4,3,64,128]{3,2,1,0:T(8,128)S(1)}, f32[4,3,64,128]{3,2,1,0:T(8,128)}, u32[]{:S(2)}) copy-start(f32[4,3,64,128]{3,2,1,0:T(8,128)} %loads_hbm.1) | copy-start | bytes 1179652
  3.6 1.9 %copy-start.1 = (s32[1,1152]{1,0:T(1,128)S(1)}, s32[1,1152]{1,0:T(1,128)}, u32[]{:S(2)}) copy-start(s32[1,1152]{1,0:T(1,128)} %order_ref.5) | copy-start | bytes 13828
  3.6 1.9 %copy-start.2 = (f32[4,1536]{1,0:T(4,128)S(1)}, f32[4,1536]{1,0:T(4,128)}, u32[]{:S(2)}) copy-start(f32[4,1536]{1,0:T(4,128)} %get-tuple-element.34.wide_ref) | copy-start | bytes 73732
  3.7 1.9 %copy-start.3 = (f32[4,128]{1,0:T(4,128)S(1)}, f32[4,128]{1,0:T(4,128)}, u32[]{:S(2)}) copy-start(f32[4,128]{1,0:T(4,128)} %get-tuple-element.33.mats_in_ref) | copy-start | bytes 6148
  3.7 1.9 %copy-start.4 = (f32[4,128]{1,0:T(4,128)S(1)}, f32[4,128]{1,0:T(4,128)}, u32[]{:S(2)}) copy-start(f32[4,128]{1,0:T(4,128)} %get-tuple-element.35.own_rows_ref) | copy-start | bytes 6148
  8.2 22.5 %collective-permute-start.2 = (f32[576,128]{1,0:T(8,128)S(1)}, f32[576,128]{1,0:T(8,128)S(1)}, u32[]{:S(2)}, u32[]{:S(2)}) collective-permute-start(f32[576,128]{1,0:T(8,128)S(1)} %get-tuple-element.41), channel_id=1, source_target_pairs={{0,1},{1,0},{2,3},{3,2},{4,5},{5,4},{6,7},{7,6},{8,9},{9,8},{10,11... | collective-permute-start | bytes 884744 | tf_op jit(solution)/shard_map/ppermute | solution.py:397
  13.4 17.3 %collective-permute-start.3 = (f32[576,128]{1,0:T(8,128)S(1)}, f32[576,128]{1,0:T(8,128)S(1)}, u32[]{:S(2)}, u32[]{:S(2)}) collective-permute-start(f32[576,128]{1,0:T(8,128)S(1)} %get-tuple-element.42), channel_id=1, source_target_pairs={{1,2},{2,1},{3,4},{4,3},{5,6},{6,5},{7,8},{8,7},{9,10},{10,9},{11,... | collective-permute-start | bytes 884744 | tf_op jit(solution)/shard_map/ppermute | solution.py:398
  34.3 13.2 %collective-permute-start.4 = (f32[576,128]{1,0:T(8,128)S(1)}, f32[576,128]{1,0:T(8,128)S(1)}, u32[]{:S(2)}, u32[]{:S(2)}) collective-permute-start(f32[576,128]{1,0:T(8,128)S(1)} %get-tuple-element.46), channel_id=1, source_target_pairs={{0,1},{1,0},{2,3},{3,2},{4,5},{5,4},{6,7},{7,6},{8,9},{9,8},{10,11... | collective-permute-start | bytes 884744 | tf_op jit(solution)/shard_map/ppermute | solution.py:397
  34.5 13.0 %collective-permute-start.5 = (f32[576,128]{1,0:T(8,128)S(1)}, f32[576,128]{1,0:T(8,128)S(1)}, u32[]{:S(2)}, u32[]{:S(2)}) collective-permute-start(f32[576,128]{1,0:T(8,128)S(1)} %get-tuple-element.47), channel_id=1, source_target_pairs={{1,2},{2,1},{3,4},{4,3},{5,6},{6,5},{7,8},{8,7},{9,10},{10,9},{11,... | collective-permute-start | bytes 884744 | tf_op jit(solution)/shard_map/ppermute | solution.py:398
  51.2 12.6 %collective-permute-start.6 = (f32[384,128]{1,0:T(8,128)S(1)}, f32[384,128]{1,0:T(8,128)S(1)}, u32[]{:S(2)}, u32[]{:S(2)}) collective-permute-start(f32[384,128]{1,0:T(8,128)S(1)} %get-tuple-element.52), channel_id=1, source_target_pairs={{0,1},{1,0},{2,3},{3,2},{4,5},{5,4},{6,7},{7,6},{8,9},{9,8},{10,11... | collective-permute-start | bytes 589832 | tf_op jit(solution)/shard_map/ppermute | solution.py:397
  51.4 12.4 %collective-permute-start.7 = (f32[384,128]{1,0:T(8,128)S(1)}, f32[384,128]{1,0:T(8,128)S(1)}, u32[]{:S(2)}, u32[]{:S(2)}) collective-permute-start(f32[384,128]{1,0:T(8,128)S(1)} %get-tuple-element.53), channel_id=1, source_target_pairs={{1,2},{2,1},{3,4},{4,3},{5,6},{6,5},{7,8},{8,7},{9,10},{10,9},{11,... | collective-permute-start | bytes 589832 | tf_op jit(solution)/shard_map/ppermute | solution.py:398

commit v5 on v4

--- a/solution.py
+++ b/solution.py
@@ -39,27 +39,24 @@
     return near, far
 
 
-def pack_kernel(shear_hbm, ratio_hbm, loads_hbm, labels_hbm, basis_hbm, coarse_hbm,
+def pack_kernel(shear_hbm, ratio_hbm, labels_hbm, basis_hbm, coarse_hbm,
                 near_ref, far_ref, mats_ref, rows_ref, wide_ref,
-                shear_ref, ratio_ref, near_load, far_load, labels_ref, basis_ref, coarse_ref, sems):
+                shear_ref, ratio_ref, labels_ref, basis_ref, coarse_ref, sems):
     planes, nodes = labels_ref.shape
-    plane_rows, cases = near_load.shape[0] * near_load.shape[1], near_load.shape[2]
-    even, _, _ = position()
+    plane_rows = 3 * NY * NZ
     moves = [
         (labels_hbm, labels_ref),
         (shear_hbm, shear_ref),
         (ratio_hbm, ratio_ref),
         (basis_hbm, basis_ref),
         (coarse_hbm, coarse_ref),
-        (loads_hbm.at[(planes - 1) * even], near_load),
-        (loads_hbm.at[(planes - 1) * (1 - even)], far_load),
     ]
     copies = [pltpu.make_async_copy(source, target, sems.at[i]) for i, (source, target) in enumerate(moves)]
     for copy in copies:
         copy.start()
-    even = even == 1
+    even = position()[0] == 1
     wide_ref[...] = jnp.zeros_like(wide_ref)
-    for copy in copies[:3]:
+    for copy in copies:
         copy.wait()
     labels = labels_ref[...]
     shear = jnp.zeros((planes, nodes), F32)
@@ -73,11 +70,10 @@
     mats_ref[...] = both
     mats_l, mats_r = both[:2], both[planes - 2 :]
     groups = group_count(plane_rows, coarse_ref.shape[1])
-    at = plane_rows + 8 * groups
-    near_ref[at : at + 2] = jnp.where(even, mats_r, mats_l)
-    far_ref[at : at + 2] = jnp.where(even, mats_l, mats_r)
-    for copy in copies[3:5]:
-        copy.wait()
+    near_ref[8 * groups : 8 * groups + 2] = jnp.where(even, mats_r, mats_l)
+    far_ref[8 * groups : 8 * groups + 2] = jnp.where(even, mats_l, mats_r)
+    near_ref[8 * groups + 2 :] = jnp.zeros_like(near_ref[8 * groups + 2 :])
+    far_ref[8 * groups + 2 :] = jnp.zeros_like(far_ref[8 * groups + 2 :])
     wide_ref[:, plane_rows : plane_rows + basis_ref.shape[1]] = basis_ref[...]
     rows = coarse_ref[:CV_DEV]
     for member in range(1, coarse_ref.shape[0] // CV_DEV):
@@ -86,20 +82,19 @@
     span = part_blocks(plane_rows)
     start_r = planes * plane_rows
     start_l = 4 * plane_rows - 128 * span
+    nothing = jnp.zeros((CV_DEV, 128), F32)
     for i in range(groups):
-        at = plane_rows + 8 * i
+        at = 8 * i
+        block_l = block_r = row = nothing
         if i < span:
             block_l = wide_ref[:, start_l + 128 * i : start_l + 128 * (i + 1)]
             block_r = wide_ref[:, start_r + 128 * i : start_r + 128 * (i + 1)]
-            near_ref[at : at + CV_DEV] = jnp.where(even, block_r, block_l)
-            far_ref[at : at + CV_DEV] = jnp.where(even, block_l, block_r)
         if i * 128 < coarse_ref.shape[1]:
-            near_ref[at + CV_DEV : at + 2 * CV_DEV] = rows[:, 128 * i : 128 * (i + 1)]
-            far_ref[at + CV_DEV : at + 2 * CV_DEV] = rows[:, 128 * i : 128 * (i + 1)]
-    for copy in copies[5:]:
-        copy.wait()
-    near_ref[:plane_rows] = near_load[...].reshape(plane_rows, cases)
-    far_ref[:plane_rows] = far_load[...].reshape(plane_rows, cases)
+            row = rows[:, 128 * i : 128 * (i + 1)]
+        near_ref[at : at + CV_DEV] = jnp.where(even, block_r, block_l)
+        far_ref[at : at + CV_DEV] = jnp.where(even, block_l, block_r)
+        near_ref[at + CV_DEV : at + 2 * CV_DEV] = row
+        far_ref[at + CV_DEV : at + 2 * CV_DEV] = row
 
 
 def stage_kernel(inverse_hbm, inverse_ref, sems):
@@ -190,7 +185,8 @@
     return rows.reshape(rows.shape[0] // (NY * NZ), NY, NZ, rows.shape[1])
 
 
-def products(order_ref, inverse_ref, basis_ref, ordered_ref, product_ref, res_ref, t_ref, near_ref, far_ref, q_ref):
+def products(width, order_ref, inverse_ref, basis_ref, ordered_ref, product_ref, res_ref, t_ref, near_ref, far_ref,
+             q_ref):
     size = res_ref.shape[0]
     for row in range(size):
         ordered_ref[row : row + 1, :] = res_ref[pl.ds(order_ref[0, row], 1), :]
@@ -202,10 +198,9 @@
         for row in range(i * step, (i + 1) * step):
             t_ref[pl.ds(order_ref[0, row], 1), :] = product_ref[row : row + 1, :]
     even, _, _ = position()
-    width = near_ref.shape[0]
     to_right = size - width
-    near_ref[...] = t_ref[pl.ds(pl.multiple_of(to_right * even, 8), width), :]
-    far_ref[...] = t_ref[pl.ds(pl.multiple_of(to_right * (1 - even), 8), width), :]
+    near_ref[:width] = t_ref[pl.ds(pl.multiple_of(to_right * even, 8), width), :]
+    far_ref[:width] = t_ref[pl.ds(pl.multiple_of(to_right * (1 - even), 8), width), :]
     high, low = split(res_ref[...])
     b_high, b_low = split(basis_ref[...])
     both = jnp.concatenate([b_high, b_low], axis=0)
@@ -216,24 +211,29 @@
     q_ref[...] = jnp.broadcast_to(q[None], q_ref.shape)
 
 
-def first_kernel(order_ref, loads_ref, near_in_ref, far_in_ref, mats_in_ref, wide_ref, own_rows_ref,
-                 inverse_ref, basis_ref,
-                 res_ref, t_ref, near_ref, far_ref, q_ref, mats_ref, extent_ref, rows_ref,
-                 ordered_ref, product_ref):
-    cases = loads_ref.shape[-1]
+def first_kernel(order_ref, loads_ref, near_in_ref, far_in_ref, near_pack_ref, far_pack_ref, inverse_ref, basis_ref,
+                 res_ref, t_ref, near_ref, far_ref, q_ref, ordered_ref, product_ref):
     plane_rows = 3 * NY * NZ
     planes = loads_ref.shape[0] // plane_rows
     even = position()[0] == 1
+    near, far = near_in_ref[...], far_in_ref[...]
+    res_ref[:plane_rows] = jnp.where(even, far, near)
+    res_ref[plane_rows : (planes + 1) * plane_rows] = loads_ref[...]
+    res_ref[(planes + 1) * plane_rows :] = jnp.where(even, near, far)
+    near_ref[3 * plane_rows :] = near_pack_ref[...]
+    far_ref[3 * plane_rows :] = far_pack_ref[...]
+    products(3 * plane_rows, order_ref, inverse_ref, basis_ref, ordered_ref, product_ref, res_ref, t_ref, near_ref,
+             far_ref, q_ref)
+
+
+def unpack(near_in_ref, far_in_ref, mats_in_ref, wide_ref, own_rows_ref, mats_ref, extent_ref, rows_ref):
+    plane_rows = 3 * NY * NZ
+    even = position()[0] == 1
 
     def beside(start, stop):
+        start, stop = 3 * plane_rows + start, 3 * plane_rows + stop
         near, far = near_in_ref[start:stop], far_in_ref[start:stop]
         return jnp.where(even, far, near), jnp.where(even, near, far)
-
-    left, right = beside(0, plane_rows)
-    res_ref[:plane_rows] = left
-    res_ref[plane_rows : (planes + 1) * plane_rows] = loads_ref[...]
-    res_ref[(planes + 1) * plane_rows :] = right
-    products(order_ref, inverse_ref, basis_ref, ordered_ref, product_ref, res_ref, t_ref, near_ref, far_ref, q_ref)
 
     extent = extent_ref.shape[1]
     span = part_blocks(plane_rows)
@@ -243,7 +243,7 @@
     rows_ref[CV_DEV : 2 * CV_DEV] = own_rows_ref[...]
     groups = group_count(plane_rows, rows_ref.shape[1])
     for i in range(groups):
-        at = plane_rows + 8 * i
+        at = 8 * i
         if i < span:
             left, right = beside(at, at + CV_DEV)
             extent_ref[:CV_DEV, 128 * i : 128 * (i + 1)] = left
@@ -253,8 +253,8 @@
             left, right = beside(at + CV_DEV, at + 2 * CV_DEV)
             rows_ref[:CV_DEV, 128 * i : 128 * (i + 1)] = left
             rows_ref[2 * CV_DEV : 3 * CV_DEV, 128 * i : 128 * (i + 1)] = right
-    at = plane_rows + 8 * groups
-    left, right = beside(at, at + 2)
+    left, right = beside(8 * groups, 8 * groups + 2)
+    planes = mats_in_ref.shape[0]
     for plane in range(2):
         mats_ref[plane] = on_lanes(left[plane : plane + 1], mats_ref.shape)
         mats_ref[planes + 2 + plane] = on_lanes(right[plane : plane + 1], mats_ref.shape)
@@ -262,9 +262,8 @@
         mats_ref[2 + plane] = on_lanes(mats_in_ref[plane : plane + 1], mats_ref.shape)
 
 
-def correction(q_ref, rows_ref, extent_ref, t_ref, near_ref, far_ref, z_ref):
+def correction(width, q_ref, rows_ref, extent_ref, t_ref, near_ref, far_ref, z_ref):
     plane_rows = 3 * NY * NZ
-    width = near_ref.shape[0] // plane_rows
     out_planes = t_ref.shape[0] // plane_rows + 2
     coarse = jnp.dot(rows_ref[...], q_ref[...], precision=lax.Precision.HIGHEST, preferred_element_type=F32)
     c_high, c_low = split(coarse)
@@ -299,12 +298,19 @@
     return coarse
 
 
-def middle_kernel(with_solution, order_ref, q_in_ref, rows_ref, extent_ref, mats_ref, t_in_ref, near_in_ref,
-                  far_in_ref, res_in_ref, *rest):
-    if with_solution:
-        solution_in_ref, *rest = rest
-    inverse_ref, basis_ref, solution_ref, res_ref, t_ref, near_ref, far_ref, q_ref, z_ref, *scratch = rest
-    correction(q_in_ref, rows_ref, extent_ref, t_in_ref, near_in_ref, far_in_ref, z_ref)
+def second_kernel(width, order_ref, q_in_ref, mats_in_ref, wide_ref, own_rows_ref, t_in_ref, near_in_ref, far_in_ref,
+                  res_in_ref, inverse_ref, basis_ref, solution_ref, res_ref, t_ref, near_ref, far_ref, q_ref,
+                  mats_ref, extent_ref, rows_ref, *scratch):
+    unpack(near_in_ref, far_in_ref, mats_in_ref, wide_ref, own_rows_ref, mats_ref, extent_ref, rows_ref)
+    middle_kernel(width, order_ref, q_in_ref, rows_ref, extent_ref, mats_ref, t_in_ref, near_in_ref, far_in_ref,
+                  res_in_ref, None, inverse_ref, basis_ref, solution_ref, res_ref, t_ref, near_ref, far_ref, q_ref,
+                  *scratch)
+
+
+def middle_kernel(width, order_ref, q_in_ref, rows_ref, extent_ref, mats_ref, t_in_ref, near_in_ref, far_in_ref,
+                  res_in_ref, solution_in_ref, inverse_ref, basis_ref, solution_ref, res_ref, t_ref, near_ref,
+                  far_ref, q_ref, z_ref, *scratch):
+    correction(3, q_in_ref, rows_ref, extent_ref, t_in_ref, near_in_ref, far_in_ref, z_ref)
     _, has_left, has_right = position()
     window = z_ref.shape[0] - 2
     for plane in range(1, window + 1):
@@ -318,13 +324,13 @@
                 value = value * has_right
             res_ref[at] = value
     own = RELAXATION * z_ref[2:window].reshape(solution_ref.shape)
-    solution_ref[...] = solution_in_ref[...] + own if with_solution else own
-    products(order_ref, inverse_ref, basis_ref, *scratch, res_ref, t_ref, near_ref, far_ref, q_ref)
+    solution_ref[...] = own if solution_in_ref is None else solution_in_ref[...] + own
+    products(width * 3 * NY * NZ, order_ref, inverse_ref, basis_ref, *scratch, res_ref, t_ref, near_ref, far_ref, q_ref)
 
 
 def last_kernel(q_in_ref, rows_ref, extent_ref, mats_ref, t_in_ref, near_in_ref, far_in_ref, res_in_ref,
                 solution_in_ref, solution_ref, residual_ref, coarse_ref, z_ref):
-    coarse = correction(q_in_ref, rows_ref, extent_ref, t_in_ref, near_in_ref, far_in_ref, z_ref)
+    coarse = correction(2, q_in_ref, rows_ref, extent_ref, t_in_ref, near_in_ref, far_in_ref, z_ref)
     coarse_ref[...] = coarse[CV_DEV : 2 * CV_DEV]
     planes = z_ref.shape[0] - 4
     solution_ref[...] = solution_in_ref[...] + RELAXATION * z_ref[2 : planes + 2].reshape(solution_ref.shape)
@@ -357,8 +363,17 @@
     basis_pad = jnp.pad(basis, ((0, 16 - CV_DEV), (0, 0)))
     extent = size + 2 * plane_rows
 
-    packed = jax.ShapeDtypeStruct((plane_rows + 8 * group_count(plane_rows, coarse_order) + 8, cases), F32)
-    near_out, far_out, mats_own, own_rows, wide = pl.pallas_call(
+    even = 1 - lax.rem(lax.axis_index(AXES), 2)
+
+    def loads_plane(plane):
+        return lax.dynamic_index_in_dim(applied_loads, plane, 0, keepdims=False).reshape(plane_rows, cases)
+
+    near_in = lax.ppermute(loads_plane((planes - 1) * even), AXES, near_pairs)
+    far_in = lax.ppermute(loads_plane((planes - 1) * (1 - even)), AXES, far_pairs)
+
+    pack_rows = 8 * group_count(plane_rows, coarse_order) + 8
+    packed = jax.ShapeDtypeStruct((pack_rows, cases), F32)
+    near_pack, far_pack, mats_own, own_rows, wide = pl.pallas_call(
         pack_kernel,
         out_shape=[
             packed,
@@ -367,22 +382,19 @@
             jax.ShapeDtypeStruct((CV_DEV, coarse_order), F32),
             jax.ShapeDtypeStruct((CV_DEV, extent), F32),
         ],
-        in_specs=[HBM] * 6,
+        in_specs=[HBM] * 5,
         out_specs=[VMEM] * 5,
         scratch_shapes=[
             pltpu.VMEM((1, shear_modulus.shape[0]), F32),
             pltpu.VMEM((1, shear_modulus.shape[0]), F32),
-            pltpu.VMEM((components, nodes, cases), F32),
-            pltpu.VMEM((components, nodes, cases), F32),
             pltpu.VMEM((planes, nodes), jnp.int32),
             pltpu.VMEM((CV_DEV, size), F32),
             pltpu.VMEM(coarse_inverse.shape, F32),
-            pltpu.SemaphoreType.DMA((7,)),
+            pltpu.SemaphoreType.DMA((5,)),
         ],
         compiler_params=WHOLE,
-    )(shear_modulus[None], stiff_ratio[None], applied_loads, labels, basis, coarse_inverse)
-    near_in = lax.ppermute(near_out, AXES, near_pairs)
-    far_in = lax.ppermute(far_out, AXES, far_pairs)
+        cost_estimate=pl.CostEstimate(flops=8 * size**3, bytes_accessed=4 * size * size, transcendentals=0),
+    )(shear_modulus[None], stiff_ratio[None], labels, basis, coarse_inverse)
 
     def field(depth):
         return jax.ShapeDtypeStruct((depth * plane_rows, cases), F32)
@@ -408,40 +420,43 @@
         compiler_params=STAGE,
         cost_estimate=pl.CostEstimate(flops=4 * size**3, bytes_accessed=4 * size * size, transcendentals=0),
     )(local_inverse[0])
-    res, t, near_out, far_out, q, mats_all, extents, inverse_rows = pl.pallas_call(
+    carried = jax.ShapeDtypeStruct((3 * plane_rows + pack_rows, cases), F32)
+    res, t, near_out, far_out, q = pl.pallas_call(
         first_kernel,
-        out_shape=[
-            field(window),
-            field(window),
-            field(3),
-            field(3),
-            q_shape,
-            jax.ShapeDtypeStruct((planes + 4, 2, NY, NZ, cases), F32),
-            jax.ShapeDtypeStruct((16, extent), F32),
-            jax.ShapeDtypeStruct((16, coarse_order), F32),
-        ],
-        in_specs=[SMEM] + [VMEM] * 8,
-        out_specs=[VMEM] * 8,
+        out_shape=[field(window), field(window), carried, carried, q_shape],
+        in_specs=[SMEM] + [VMEM] * 7,
+        out_specs=[VMEM] * 5,
         scratch_shapes=scratch,
         compiler_params=PARAMS,
         cost_estimate=cost,
-    )(local_order, loads, near_in, far_in, mats_own, wide, own_rows, inverse, basis_pad)
+    )(local_order, loads, near_in, far_in, near_pack, far_pack, inverse, basis_pad)
     near_in, far_in, q_all = move(near_out, far_out, q)
-    solution = None
     for iteration in range(1, ITERS):
         width = 2 if iteration == ITERS - 1 else 3
-        extra = [] if solution is None else [solution]
-        operands = [local_order, q_all, inverse_rows, extents, mats_all, t, near_in, far_in, res, *extra,
-                    inverse, basis_pad]
-        solution, res, t, near_out, far_out, q = pl.pallas_call(
-            functools.partial(middle_kernel, bool(extra)),
-            out_shape=[field(planes), field(window), field(window), field(width), field(width), q_shape],
+        outs = [field(planes), field(window), field(window), field(width), field(width), q_shape]
+        if iteration == 1:
+            kernel = second_kernel
+            operands = [local_order, q_all, mats_own, wide, own_rows, t, near_in, far_in, res, inverse, basis_pad]
+            outs += [
+                jax.ShapeDtypeStruct((planes + 4, 2, NY, NZ, cases), F32),
+                jax.ShapeDtypeStruct((16, extent), F32),
+                jax.ShapeDtypeStruct((16, coarse_order), F32),
+            ]
+        else:
+            kernel = middle_kernel
+            operands = [local_order, q_all, inverse_rows, extents, mats_all, t, near_in, far_in, res, solution,
+                        inverse, basis_pad]
+        solution, res, t, near_out, far_out, q, *setup = pl.pallas_call(
+            functools.partial(kernel, width),
+            out_shape=outs,
             in_specs=[SMEM] + [VMEM] * (len(operands) - 1),
-            out_specs=[VMEM] * 6,
+            out_specs=[VMEM] * len(outs),
             scratch_shapes=[z_scratch, *scratch],
             compiler_params=PARAMS,
             cost_estimate=cost,
         )(*operands)
+        if setup:
+            mats_all, extents, inverse_rows = setup
         near_in, far_in, q_all = move(near_out, far_out, q)
     solution, residual, coarse_values = pl.pallas_call(
         last_kernel,

time: 65.8 us -> 65 us (0.988)
  starting transfers between devices: 8.7 us -> 7.45 us
  local copies, waits for them, and re-layouts: 0.04 us -> 1.01 us
    ppermute x3, starting transfers between devices: 5.53 us -> 4.28 us  [move(): near_in = lax.ppermute(near_out, AXES, near_pairs)]
    dynamic_slice x0 -> x1, local copies, waits for them, and re-layouts: none -> 0.96 us  [loads_plane(): lax.dynamic_index_in_dim(applied_loads, plane, 0, keepdims=False)]
  transfers between devices with their start and end apart: 8 -> 8, of which waited for: 0 -> 0; matrix products, arithmetic and copies ran while one was open for 0% -> 0% of each run, Pallas kernels for 3% -> 5%
where the time goes in v5:
time: 65 us; the launch traced here: 64.7 us
  blocking collectives  40.3 us (62%)
  Pallas kernels  15 us (23%)
  starting transfers between devices  7.45 us (11%)
  local copies, waits for them, and re-layouts  1.01 us (2%)
  between operations  0.87 us (1%)
    all_to_all x3, blocking collectives, move(): q_all = lax.all_to_all(q, AXES, 0, 0).reshape(count * CV_DEV, cases)  40.3 us
    pallas_call x2, Pallas kernels, body(): pl.pallas_call(functools.partial(kernel, width), out_shape=outs, in_specs...  7.32 us
    ppermute x3, starting transfers between devices, move(): near_in = lax.ppermute(near_out, AXES, near_pairs)  4.28 us
    pallas_call x1, Pallas kernels, body(): pl.pallas_call(first_kernel, out_shape=[field(window), field(window), car...  2.59 us
    ppermute x3, starting transfers between devices, move(): far_in = lax.ppermute(far_out, AXES, far_pairs)  2 us
    pallas_call x1, Pallas kernels, body(): pl.pallas_call(stage_kernel, out_shape=jax.ShapeDtypeStruct((size, size),...  1.77 us
    pallas_call x1, Pallas kernels, body(): pl.pallas_call(last_kernel, out_shape=[field(planes), field(planes), jax....  1.72 us
    pallas_call x1, Pallas kernels, body(): pl.pallas_call(pack_kernel, out_shape=[packed, packed, jax.ShapeDtypeStru...  1.59 us
  transfers between devices with their start and end apart: 8, of which 0 were waited for; matrix products, arithmetic and copies ran while one was open for 0% of the time, Pallas kernels for 5%

profile of v5, /device:TPU:0, one launch (start us, length us, event | category | flops | bytes accessed | tf_op | source)
XLA Modules:
  0.0 64.7 jit_solution(17279329723344800004)
XLA Ops:
  0.6 1.0 %constant_dynamic-slice_fusion = (f32[1,3,64,128]{3,2,1,0:T(8,128)S(1)}, f32[1,3,64,128]{3,2,1,0:T(8,128)S(1)}) fusion(f32[4,3,64,128]{3,2,1,0:T(8,128)} %param.8, s32[]{:T(128)S(6)} %select_n.8, s32[]{:T(128)S(6)} %select_n.7), kind=kLoop, calls=%fused_computation | loop fusion | bytes 393224 | tf_op jit(solution)/shard_map/jit(dynamic_index_in_dim)/dynamic_slice | solution.py:369
  1.6 0.5 collective-permute-start
  2.1 0.7 %collective-permute-start.1 = (f32[192,128]{1,0:T(8,128)S(1)}, f32[192,128]{1,0:T(8,128)S(1)}, u32[]{:S(2)}, u32[]{:S(2)}) collective-permute-start(f32[192,128]{1,0:T(8,128)S(1)} %bitcast.16), channel_id=1, source_target_pairs={{1,2},{2,1},{3,4},{4,3},{5,6},{6,5},{7,8},{8,7},{9,10},{10,9},{11,... | collective-permute-start | bytes 294920 | tf_op jit(solution)/shard_map/ppermute | solution.py:372
  2.8 1.6 %shard_map.103 = (f32[48,128]{1,0:T(8,128)}, f32[48,128]{1,0:T(8,128)}, f32[4,128]{1,0:T(4,128)}, f32[4,128]{1,0:T(4,128)}, f32[4,1536]{1,0:T(4,128)}) custom-call(f32[1,8]{1,0:T(1,128)} %bitcast.23, f32[1,8]{1,0:T(1,128)} %bitcast.24, s32[4,64]{1,0:T(4,128)} %labels_hbm.1, f32[4,1152]{1,0:T(4,128)} %bitcast.18, f32[8,128]{1,0:T(8,128)} %coarse_hbm.1), custom_call_target="tpu_custom_call" | custom-call | flops 12230590464 | bytes 5308416 | tf_op jit(solution)/shard_map/pallas_call | solution.py:376
  4.4 0.0 copy-start.7
  4.4 0.0 copy-start
  4.4 0.0 copy-start.1
  4.4 0.0 copy-start.3
  4.4 0.0 copy-start.4
  4.4 1.8 %shard_map.104.inverse_ref = bf16[1152,1152]{1,0:T(8,128)(2,1)S(1)} custom-call(bf16[1152,1152]{1,0:T(8,128)(2,1)} %bitcast.20), custom_call_target="tpu_custom_call" | custom-call | flops 6115295232 | bytes 5308416 | tf_op jit(solution)/shard_map/pallas_call | solution.py:414
  6.2 0.0 copy-start.5
  6.3 2.6 %shard_map.105 = (f32[1152,128]{1,0:T(8,128)S(1)}, f32[1152,128]{1,0:T(8,128)S(1)}, f32[624,128]{1,0:T(8,128)S(1)}, f32[624,128]{1,0:T(8,128)S(1)}, f32[32,4,128]{2,1,0:T(4,128)S(1)}) custom-call(s32[1,1152]{1,0:T(1,128)S(1)} %copy-done.1, f32[768,128]{1,0:T(8,128)S(1)} %bitcast.12, f32[192,128]{1,0:T(8,128)S(1)} %collective-permute-done.near_in_ref, ...), custom_call_target="tpu_custom_call" | custom-call | flops 339738624 | bytes 2654208 | tf_op jit(solution)/shard_map/pallas_call | solution.py:424
  8.9 3.9 %collective-permute-start.2 = (f32[624,128]{1,0:T(8,128)S(1)}, f32[624,128]{1,0:T(8,128)S(1)}, u32[]{:S(2)}, u32[]{:S(2)}) collective-permute-start(f32[624,128]{1,0:T(8,128)S(1)} %get-tuple-element.38), channel_id=1, source_target_pairs={{0,1},{1,0},{2,3},{3,2},{4,5},{5,4},{6,7},{7,6},{8,9},{9,8},{10,11... | collective-permute-start | bytes 958472 | tf_op jit(solution)/shard_map/ppermute | solution.py:409
  12.9 0.7 %collective-permute-start.3 = (f32[624,128]{1,0:T(8,128)S(1)}, f32[624,128]{1,0:T(8,128)S(1)}, u32[]{:S(2)}, u32[]{:S(2)}) collective-permute-start(f32[624,128]{1,0:T(8,128)S(1)} %get-tuple-element.39), channel_id=1, source_target_pairs={{1,2},{2,1},{3,4},{4,3},{5,6},{6,5},{7,8},{8,7},{9,10},{10,9},{11,... | collective-permute-start | bytes 958472 | tf_op jit(solution)/shard_map/ppermute | solution.py:410
  13.5 15.5 %all_to_all.15 = f32[32,4,128]{2,1,0:T(4,128)S(1)} all-to-all(f32[32,4,128]{2,1,0:T(4,128)S(1)} %get-tuple-element.33), channel_id=1, replica_groups=mesh['sub'=16,'grp'=2] {'sub','grp'}, dimensions={0} | all-to-all | bytes 131072 | tf_op jit(solution)/shard_map/all_to_all | solution.py:411
  29.1 3.6 %shard_map.106 = (f32[768,128]{1,0:T(8,128)S(1)}, f32[1152,128]{1,0:T(8,128)S(1)}, f32[1152,128]{1,0:T(8,128)S(1)}, f32[576,128]{1,0:T(8,128)S(1)}, f32[576,128]...) custom-call(s32[1,1152]{1,0:T(1,128)S(1)} %copy-done.1, ...), custom_call_target="tpu_custom_call" | custom-call | flops 339738624 | bytes 2654208 | tf_op jit(solution)/shard_map/pallas_call | solution.py:449
  32.7 0.2 collective-permute-start.4
  32.9 0.7 %collective-permute-start.5 = (f32[576,128]{1,0:T(8,128)S(1)}, f32[576,128]{1,0:T(8,128)S(1)}, u32[]{:S(2)}, u32[]{:S(2)}) collective-permute-start(f32[576,128]{1,0:T(8,128)S(1)} %get-tuple-element.47), channel_id=1, source_target_pairs={{1,2},{2,1},{3,4},{4,3},{5,6},{6,5},{7,8},{8,7},{9,10},{10,9},{11,... | collective-permute-start | bytes 884744 | tf_op jit(solution)/shard_map/ppermute | solution.py:410
  33.6 12.8 %all_to_all.16 = f32[32,4,128]{2,1,0:T(4,128)S(1)} all-to-all(f32[32,4,128]{2,1,0:T(4,128)S(1)} %get-tuple-element.41), channel_id=1, replica_groups=mesh['sub'=16,'grp'=2] {'sub','grp'}, dimensions={0} | all-to-all | bytes 131072 | tf_op jit(solution)/shard_map/all_to_all | solution.py:411
  46.4 3.7 %shard_map.107 = (f32[768,128]{1,0:T(8,128)S(1)}, f32[1152,128]{1,0:T(8,128)S(1)}, f32[1152,128]{1,0:T(8,128)S(1)}, f32[384,128]{1,0:T(8,128)S(1)}, f32[384,128]{1,0:T(8,128)S(1)}, /*index=5*/f32[32,4,128]{2,1,0:T(4,128)S(1)}) custom-call(s32[1,1152]{1,0:T(1,128)S(1)} %copy-done.1, f32[128,128]{1,0:T(8,128)S(1)} %bitcast.14, ...), custom_call_target="tpu_custom_call" | custom-call | flops 339738624 | bytes 2654208 | tf_op jit(solution)/shard_map/pallas_call | solution.py:449
  50.1 0.2 collective-permute-start.6
  50.3 0.7 %collective-permute-start.7 = (f32[384,128]{1,0:T(8,128)S(1)}, f32[384,128]{1,0:T(8,128)S(1)}, u32[]{:S(2)}, u32[]{:S(2)}) collective-permute-start(f32[384,128]{1,0:T(8,128)S(1)} %get-tuple-element.53), channel_id=1, source_target_pairs={{1,2},{2,1},{3,4},{4,3},{5,6},{6,5},{7,8},{8,7},{9,10},{10,9},{11,... | collective-permute-start | bytes 589832 | tf_op jit(solution)/shard_map/ppermute | solution.py:410
  51.0 12.0 %all_to_all.17 = f32[32,4,128]{2,1,0:T(4,128)S(1)} all-to-all(f32[32,4,128]{2,1,0:T(4,128)S(1)} %get-tuple-element.50), channel_id=1, replica_groups=mesh['sub'=16,'grp'=2] {'sub','grp'}, dimensions={0} | all-to-all | bytes 131072 | tf_op jit(solution)/shard_map/all_to_all | solution.py:411
  62.9 1.7 %shard_map.108 = (f32[768,128]{1,0:T(8,128)}, f32[768,128]{1,0:T(8,128)}, f32[4,128]{1,0:T(4,128)}) custom-call(f32[128,128]{1,0:T(8,128)S(1)} %bitcast.15, f32[16,128]{1,0:T(8,128)S(1)} %get-tuple-element.42.rows_ref, f32[16,1536]{1,0:T(8,128)S(1)} %get-tuple-element.43.extent_ref, f32[8,2,8,8,128]{4,3,2,1,0:T(8,128)S(1)} %get-tuple-element.44.mats_ref, ...), custom_call_target="tpu_custom_call" | custom-call | tf_op jit(solution)/shard_map/pallas_call | solution.py:461
  (19 shorter events, 0.0 us)
Async XLA Ops:
  1.6 4.7 %collective-permute-start = (f32[192,128]{1,0:T(8,128)S(1)}, f32[192,128]{1,0:T(8,128)S(1)}, u32[]{:S(2)}, u32[]{:S(2)}) collective-permute-start(f32[192,128]{1,0:T(8,128)S(1)} %bitcast.17), channel_id=1, source_target_pairs={{0,1},{1,0},{2,3},{3,2},{4,5},{5,4},{6,7},{7,6},{8,9},{9,8},{10,11... | collective-permute-start | bytes 294920 | tf_op jit(solution)/shard_map/ppermute | solution.py:371
  2.1 4.2 %collective-permute-start.1 = (f32[192,128]{1,0:T(8,128)S(1)}, f32[192,128]{1,0:T(8,128)S(1)}, u32[]{:S(2)}, u32[]{:S(2)}) collective-permute-start(f32[192,128]{1,0:T(8,128)S(1)} %bitcast.16), channel_id=1, source_target_pairs={{1,2},{2,1},{3,4},{4,3},{5,6},{6,5},{7,8},{8,7},{9,10},{10,9},{11,... | collective-permute-start | bytes 294920 | tf_op jit(solution)/shard_map/ppermute | solution.py:372
  4.4 1.8 %copy-start.7 = (f32[1,4,1152]{2,1,0:T(4,128)S(1)}, f32[1,4,1152]{2,1,0:T(4,128)}, u32[]{:S(2)}) copy-start(f32[1,4,1152]{2,1,0:T(4,128)} %param.14) | copy-start | bytes 55300
  4.4 1.9 %copy-start = (f32[4,3,64,128]{3,2,1,0:T(8,128)S(1)}, f32[4,3,64,128]{3,2,1,0:T(8,128)}, u32[]{:S(2)}) copy-start(f32[4,3,64,128]{3,2,1,0:T(8,128)} %param.8) | copy-start | bytes 1179652
  4.4 1.9 %copy-start.1 = (s32[1,1152]{1,0:T(1,128)S(1)}, s32[1,1152]{1,0:T(1,128)}, u32[]{:S(2)}) copy-start(s32[1,1152]{1,0:T(1,128)} %order_ref.5) | copy-start | bytes 13828
  4.4 1.9 %copy-start.3 = (f32[48,128]{1,0:T(8,128)S(1)}, f32[48,128]{1,0:T(8,128)}, u32[]{:S(2)}) copy-start(f32[48,128]{1,0:T(8,128)} %get-tuple-element.31.near_pack_ref) | copy-start | bytes 73732
  4.4 1.9 %copy-start.4 = (f32[48,128]{1,0:T(8,128)S(1)}, f32[48,128]{1,0:T(8,128)}, u32[]{:S(2)}) copy-start(f32[48,128]{1,0:T(8,128)} %get-tuple-element.32.far_pack_ref) | copy-start | bytes 73732
  6.2 22.8 %copy-start.2 = (f32[4,1536]{1,0:T(4,128)S(1)}, f32[4,1536]{1,0:T(4,128)}, u32[]{:S(2)}) copy-start(f32[4,1536]{1,0:T(4,128)} %get-tuple-element.35.wide_ref) | copy-start | bytes 73732
  6.2 22.8 %copy-start.5 = (f32[4,128]{1,0:T(4,128)S(1)}, f32[4,128]{1,0:T(4,128)}, u32[]{:S(2)}) copy-start(f32[4,128]{1,0:T(4,128)} %get-tuple-element.34.mats_in_ref) | copy-start | bytes 6148
  6.3 22.8 %copy-start.6 = (f32[4,128]{1,0:T(4,128)S(1)}, f32[4,128]{1,0:T(4,128)}, u32[]{:S(2)}) copy-start(f32[4,128]{1,0:T(4,128)} %get-tuple-element.36.own_rows_ref) | copy-start | bytes 6148
  8.9 20.1 %collective-permute-start.2 = (f32[624,128]{1,0:T(8,128)S(1)}, f32[624,128]{1,0:T(8,128)S(1)}, u32[]{:S(2)}, u32[]{:S(2)}) collective-permute-start(f32[624,128]{1,0:T(8,128)S(1)} %get-tuple-element.38), channel_id=1, source_target_pairs={{0,1},{1,0},{2,3},{3,2},{4,5},{5,4},{6,7},{7,6},{8,9},{9,8},{10,11... | collective-permute-start | bytes 958472 | tf_op jit(solution)/shard_map/ppermute | solution.py:409
  12.9 16.2 %collective-permute-start.3 = (f32[624,128]{1,0:T(8,128)S(1)}, f32[624,128]{1,0:T(8,128)S(1)}, u32[]{:S(2)}, u32[]{:S(2)}) collective-permute-start(f32[624,128]{1,0:T(8,128)S(1)} %get-tuple-element.39), channel_id=1, source_target_pairs={{1,2},{2,1},{3,4},{4,3},{5,6},{6,5},{7,8},{8,7},{9,10},{10,9},{11,... | collective-permute-start | bytes 958472 | tf_op jit(solution)/shard_map/ppermute | solution.py:410
  32.7 13.7 %collective-permute-start.4 = (f32[576,128]{1,0:T(8,128)S(1)}, f32[576,128]{1,0:T(8,128)S(1)}, u32[]{:S(2)}, u32[]{:S(2)}) collective-permute-start(f32[576,128]{1,0:T(8,128)S(1)} %get-tuple-element.46), channel_id=1, source_target_pairs={{0,1},{1,0},{2,3},{3,2},{4,5},{5,4},{6,7},{7,6},{8,9},{9,8},{10,11... | collective-permute-start | bytes 884744 | tf_op jit(solution)/shard_map/ppermute | solution.py:409
  32.9 13.5 %collective-permute-start.5 = (f32[576,128]{1,0:T(8,128)S(1)}, f32[576,128]{1,0:T(8,128)S(1)}, u32[]{:S(2)}, u32[]{:S(2)}) collective-permute-start(f32[576,128]{1,0:T(8,128)S(1)} %get-tuple-element.47), channel_id=1, source_target_pairs={{1,2},{2,1},{3,4},{4,3},{5,6},{6,5},{7,8},{8,7},{9,10},{10,9},{11,... | collective-permute-start | bytes 884744 | tf_op jit(solution)/shard_map/ppermute | solution.py:410
  50.1 12.8 %collective-permute-start.6 = (f32[384,128]{1,0:T(8,128)S(1)}, f32[384,128]{1,0:T(8,128)S(1)}, u32[]{:S(2)}, u32[]{:S(2)}) collective-permute-start(f32[384,128]{1,0:T(8,128)S(1)} %get-tuple-element.52), channel_id=1, source_target_pairs={{0,1},{1,0},{2,3},{3,2},{4,5},{5,4},{6,7},{7,6},{8,9},{9,8},{10,11... | collective-permute-start | bytes 589832 | tf_op jit(solution)/shard_map/ppermute | solution.py:409
  50.3 12.7 %collective-permute-start.7 = (f32[384,128]{1,0:T(8,128)S(1)}, f32[384,128]{1,0:T(8,128)S(1)}, u32[]{:S(2)}, u32[]{:S(2)}) collective-permute-start(f32[384,128]{1,0:T(8,128)S(1)} %get-tuple-element.53), channel_id=1, source_target_pairs={{1,2},{2,1},{3,4},{4,3},{5,6},{6,5},{7,8},{8,7},{9,10},{10,9},{11,... | collective-permute-start | bytes 589832 | tf_op jit(solution)/shard_map/ppermute | solution.py:410

commit v6 on v5

--- a/solution.py
+++ b/solution.py
@@ -25,10 +25,10 @@
 
 def position():
     place = lax.axis_index(AXES)
-    even = 1 - lax.rem(place, 2)
+    odd = lax.rem(place, 2)
     has_left = (place > 0).astype(F32)
     has_right = (place < lax.axis_size(AXES) - 1).astype(F32)
-    return even, has_left, has_right
+    return odd, has_left, has_right
 
 
 def swap_pairs(count):
@@ -40,7 +40,7 @@
 
 
 def pack_kernel(shear_hbm, ratio_hbm, labels_hbm, basis_hbm, coarse_hbm,
-                near_ref, far_ref, mats_ref, rows_ref, wide_ref,
+                far_ref, near_ref, mats_ref, rows_ref, wide_ref,
                 shear_ref, ratio_ref, labels_ref, basis_ref, coarse_ref, sems):
     planes, nodes = labels_ref.shape
     plane_rows = 3 * NY * NZ
@@ -54,7 +54,7 @@
     copies = [pltpu.make_async_copy(source, target, sems.at[i]) for i, (source, target) in enumerate(moves)]
     for copy in copies:
         copy.start()
-    even = position()[0] == 1
+    odd = position()[0] == 1
     wide_ref[...] = jnp.zeros_like(wide_ref)
     for copy in copies:
         copy.wait()
@@ -70,10 +70,10 @@
     mats_ref[...] = both
     mats_l, mats_r = both[:2], both[planes - 2 :]
     groups = group_count(plane_rows, coarse_ref.shape[1])
-    near_ref[8 * groups : 8 * groups + 2] = jnp.where(even, mats_r, mats_l)
-    far_ref[8 * groups : 8 * groups + 2] = jnp.where(even, mats_l, mats_r)
+    far_ref[8 * groups : 8 * groups + 2] = jnp.where(odd, mats_r, mats_l)
+    near_ref[8 * groups : 8 * groups + 2] = jnp.where(odd, mats_l, mats_r)
+    far_ref[8 * groups + 2 :] = jnp.zeros_like(far_ref[8 * groups + 2 :])
     near_ref[8 * groups + 2 :] = jnp.zeros_like(near_ref[8 * groups + 2 :])
-    far_ref[8 * groups + 2 :] = jnp.zeros_like(far_ref[8 * groups + 2 :])
     wide_ref[:, plane_rows : plane_rows + basis_ref.shape[1]] = basis_ref[...]
     rows = coarse_ref[:CV_DEV]
     for member in range(1, coarse_ref.shape[0] // CV_DEV):
@@ -91,10 +91,10 @@
             block_r = wide_ref[:, start_r + 128 * i : start_r + 128 * (i + 1)]
         if i * 128 < coarse_ref.shape[1]:
             row = rows[:, 128 * i : 128 * (i + 1)]
-        near_ref[at : at + CV_DEV] = jnp.where(even, block_r, block_l)
-        far_ref[at : at + CV_DEV] = jnp.where(even, block_l, block_r)
+        far_ref[at : at + CV_DEV] = jnp.where(odd, block_r, block_l)
+        near_ref[at : at + CV_DEV] = jnp.where(odd, block_l, block_r)
+        far_ref[at + CV_DEV : at + 2 * CV_DEV] = row
         near_ref[at + CV_DEV : at + 2 * CV_DEV] = row
-        far_ref[at + CV_DEV : at + 2 * CV_DEV] = row
 
 
 def stage_kernel(inverse_hbm, inverse_ref, sems):
@@ -185,7 +185,7 @@
     return rows.reshape(rows.shape[0] // (NY * NZ), NY, NZ, rows.shape[1])
 
 
-def products(width, order_ref, inverse_ref, basis_ref, ordered_ref, product_ref, res_ref, t_ref, near_ref, far_ref,
+def products(width, order_ref, inverse_ref, basis_ref, ordered_ref, product_ref, res_ref, t_ref, far_ref, near_ref,
              q_ref):
     size = res_ref.shape[0]
     for row in range(size):
@@ -197,10 +197,10 @@
         product_ref[part, :] = jnp.dot(inverse_ref[part, :], ordered, preferred_element_type=F32)
         for row in range(i * step, (i + 1) * step):
             t_ref[pl.ds(order_ref[0, row], 1), :] = product_ref[row : row + 1, :]
-    even, _, _ = position()
+    odd, _, _ = position()
     to_right = size - width
-    near_ref[:width] = t_ref[pl.ds(pl.multiple_of(to_right * even, 8), width), :]
-    far_ref[:width] = t_ref[pl.ds(pl.multiple_of(to_right * (1 - even), 8), width), :]
+    far_ref[:width] = t_ref[pl.ds(pl.multiple_of(to_right * odd, 8), width), :]
+    near_ref[:width] = t_ref[pl.ds(pl.multiple_of(to_right * (1 - odd), 8), width), :]
     high, low = split(res_ref[...])
     b_high, b_low = split(basis_ref[...])
     both = jnp.concatenate([b_high, b_low], axis=0)
@@ -211,29 +211,29 @@
     q_ref[...] = jnp.broadcast_to(q[None], q_ref.shape)
 
 
-def first_kernel(order_ref, loads_ref, near_in_ref, far_in_ref, near_pack_ref, far_pack_ref, inverse_ref, basis_ref,
-                 res_ref, t_ref, near_ref, far_ref, q_ref, ordered_ref, product_ref):
+def first_kernel(order_ref, loads_ref, far_in_ref, near_in_ref, far_pack_ref, near_pack_ref, inverse_ref, basis_ref,
+                 res_ref, t_ref, far_ref, near_ref, q_ref, ordered_ref, product_ref):
     plane_rows = 3 * NY * NZ
     planes = loads_ref.shape[0] // plane_rows
-    even = position()[0] == 1
-    near, far = near_in_ref[...], far_in_ref[...]
-    res_ref[:plane_rows] = jnp.where(even, far, near)
+    odd = position()[0] == 1
+    far, near = far_in_ref[...], near_in_ref[...]
+    res_ref[:plane_rows] = jnp.where(odd, near, far)
     res_ref[plane_rows : (planes + 1) * plane_rows] = loads_ref[...]
-    res_ref[(planes + 1) * plane_rows :] = jnp.where(even, near, far)
+    res_ref[(planes + 1) * plane_rows :] = jnp.where(odd, far, near)
+    far_ref[3 * plane_rows :] = far_pack_ref[...]
     near_ref[3 * plane_rows :] = near_pack_ref[...]
-    far_ref[3 * plane_rows :] = far_pack_ref[...]
-    products(3 * plane_rows, order_ref, inverse_ref, basis_ref, ordered_ref, product_ref, res_ref, t_ref, near_ref,
-             far_ref, q_ref)
-
-
-def unpack(near_in_ref, far_in_ref, mats_in_ref, wide_ref, own_rows_ref, mats_ref, extent_ref, rows_ref):
+    products(3 * plane_rows, order_ref, inverse_ref, basis_ref, ordered_ref, product_ref, res_ref, t_ref, far_ref,
+             near_ref, q_ref)
+
+
+def unpack(far_in_ref, near_in_ref, mats_in_ref, wide_ref, own_rows_ref, mats_ref, extent_ref, rows_ref):
     plane_rows = 3 * NY * NZ
-    even = position()[0] == 1
+    odd = position()[0] == 1
 
     def beside(start, stop):
         start, stop = 3 * plane_rows + start, 3 * plane_rows + stop
-        near, far = near_in_ref[start:stop], far_in_ref[start:stop]
-        return jnp.where(even, far, near), jnp.where(even, near, far)
+        far, near = far_in_ref[start:stop], near_in_ref[start:stop]
+        return jnp.where(odd, near, far), jnp.where(odd, far, near)
 
     extent = extent_ref.shape[1]
     span = part_blocks(plane_rows)
@@ -262,7 +262,7 @@
         mats_ref[2 + plane] = on_lanes(mats_in_ref[plane : plane + 1], mats_ref.shape)
 
 
-def correction(width, q_ref, rows_ref, extent_ref, t_ref, near_ref, far_ref, z_ref):
+def correction(width, q_ref, rows_ref, extent_ref, t_ref, far_ref, near_ref, z_ref):
     plane_rows = 3 * NY * NZ
     out_planes = t_ref.shape[0] // plane_rows + 2
     coarse = jnp.dot(rows_ref[...], q_ref[...], precision=lax.Precision.HIGHEST, preferred_element_type=F32)
@@ -274,8 +274,8 @@
         (((0,), (0,)), ((), ())),
         preferred_element_type=F32,
     )
-    even, has_left, has_right = position()
-    even = even == 1
+    odd, has_left, has_right = position()
+    odd = odd == 1
 
     def rows_at(ref, plane):
         return ref[plane * plane_rows : (plane + 1) * plane_rows]
@@ -286,10 +286,10 @@
             value = value + rows_at(t_ref, plane - 1)
         if plane < 3:
             at = plane - (3 - width)
-            value = value + jnp.where(even, rows_at(far_ref, at), rows_at(near_ref, at))
+            value = value + jnp.where(odd, rows_at(near_ref, at), rows_at(far_ref, at))
         if plane >= out_planes - 3:
             at = plane - (out_planes - 3)
-            value = value + jnp.where(even, rows_at(near_ref, at), rows_at(far_ref, at))
+            value = value + jnp.where(odd, rows_at(far_ref, at), rows_at(near_ref, at))
         if plane < 2:
             value = value * has_left
         if plane >= out_planes - 2:
@@ -298,19 +298,19 @@
     return coarse
 
 
-def second_kernel(width, order_ref, q_in_ref, mats_in_ref, wide_ref, own_rows_ref, t_in_ref, near_in_ref, far_in_ref,
-                  res_in_ref, inverse_ref, basis_ref, solution_ref, res_ref, t_ref, near_ref, far_ref, q_ref,
+def second_kernel(width, order_ref, q_in_ref, mats_in_ref, wide_ref, own_rows_ref, t_in_ref, far_in_ref, near_in_ref,
+                  res_in_ref, inverse_ref, basis_ref, solution_ref, res_ref, t_ref, far_ref, near_ref, q_ref,
                   mats_ref, extent_ref, rows_ref, *scratch):
-    unpack(near_in_ref, far_in_ref, mats_in_ref, wide_ref, own_rows_ref, mats_ref, extent_ref, rows_ref)
-    middle_kernel(width, order_ref, q_in_ref, rows_ref, extent_ref, mats_ref, t_in_ref, near_in_ref, far_in_ref,
-                  res_in_ref, None, inverse_ref, basis_ref, solution_ref, res_ref, t_ref, near_ref, far_ref, q_ref,
+    unpack(far_in_ref, near_in_ref, mats_in_ref, wide_ref, own_rows_ref, mats_ref, extent_ref, rows_ref)
+    middle_kernel(width, order_ref, q_in_ref, rows_ref, extent_ref, mats_ref, t_in_ref, far_in_ref, near_in_ref,
+                  res_in_ref, None, inverse_ref, basis_ref, solution_ref, res_ref, t_ref, far_ref, near_ref, q_ref,
                   *scratch)
 
 
-def middle_kernel(width, order_ref, q_in_ref, rows_ref, extent_ref, mats_ref, t_in_ref, near_in_ref, far_in_ref,
-                  res_in_ref, solution_in_ref, inverse_ref, basis_ref, solution_ref, res_ref, t_ref, near_ref,
-                  far_ref, q_ref, z_ref, *scratch):
-    correction(3, q_in_ref, rows_ref, extent_ref, t_in_ref, near_in_ref, far_in_ref, z_ref)
+def middle_kernel(width, order_ref, q_in_ref, rows_ref, extent_ref, mats_ref, t_in_ref, far_in_ref, near_in_ref,
+                  res_in_ref, solution_in_ref, inverse_ref, basis_ref, solution_ref, res_ref, t_ref, far_ref,
+                  near_ref, q_ref, z_ref, *scratch):
+    correction(3, q_in_ref, rows_ref, extent_ref, t_in_ref, far_in_ref, near_in_ref, z_ref)
     _, has_left, has_right = position()
     window = z_ref.shape[0] - 2
     for plane in range(1, window + 1):
@@ -325,12 +325,12 @@
             res_ref[at] = value
     own = RELAXATION * z_ref[2:window].reshape(solution_ref.shape)
     solution_ref[...] = own if solution_in_ref is None else solution_in_ref[...] + own
-    products(width * 3 * NY * NZ, order_ref, inverse_ref, basis_ref, *scratch, res_ref, t_ref, near_ref, far_ref, q_ref)
-
-
-def last_kernel(q_in_ref, rows_ref, extent_ref, mats_ref, t_in_ref, near_in_ref, far_in_ref, res_in_ref,
+    products(width * 3 * NY * NZ, order_ref, inverse_ref, basis_ref, *scratch, res_ref, t_ref, far_ref, near_ref, q_ref)
+
+
+def last_kernel(q_in_ref, rows_ref, extent_ref, mats_ref, t_in_ref, far_in_ref, near_in_ref, res_in_ref,
                 solution_in_ref, solution_ref, residual_ref, coarse_ref, z_ref):
-    coarse = correction(2, q_in_ref, rows_ref, extent_ref, t_in_ref, near_in_ref, far_in_ref, z_ref)
+    coarse = correction(2, q_in_ref, rows_ref, extent_ref, t_in_ref, far_in_ref, near_in_ref, z_ref)
     coarse_ref[...] = coarse[CV_DEV : 2 * CV_DEV]
     planes = z_ref.shape[0] - 4
     solution_ref[...] = solution_in_ref[...] + RELAXATION * z_ref[2 : planes + 2].reshape(solution_ref.shape)
@@ -363,17 +363,17 @@
     basis_pad = jnp.pad(basis, ((0, 16 - CV_DEV), (0, 0)))
     extent = size + 2 * plane_rows
 
-    even = 1 - lax.rem(lax.axis_index(AXES), 2)
+    odd = lax.rem(lax.axis_index(AXES), 2)
 
     def loads_plane(plane):
         return lax.dynamic_index_in_dim(applied_loads, plane, 0, keepdims=False).reshape(plane_rows, cases)
 
-    near_in = lax.ppermute(loads_plane((planes - 1) * even), AXES, near_pairs)
-    far_in = lax.ppermute(loads_plane((planes - 1) * (1 - even)), AXES, far_pairs)
+    far_in = lax.ppermute(loads_plane((planes - 1) * odd), AXES, far_pairs)
+    near_in = lax.ppermute(loads_plane((planes - 1) * (1 - odd)), AXES, near_pairs)
 
     pack_rows = 8 * group_count(plane_rows, coarse_order) + 8
     packed = jax.ShapeDtypeStruct((pack_rows, cases), F32)
-    near_pack, far_pack, mats_own, own_rows, wide = pl.pallas_call(
+    far_pack, near_pack, mats_own, own_rows, wide = pl.pallas_call(
         pack_kernel,
         out_shape=[
             packed,
@@ -405,11 +405,11 @@
     scratch = [pltpu.VMEM((size, cases), F32), pltpu.VMEM((size, cases), F32)]
     loads = applied_loads.reshape(planes * plane_rows, cases)
 
-    def move(near_out, far_out, q):
+    def move(far_out, near_out, q):
+        far_in = lax.ppermute(far_out, AXES, far_pairs)
         near_in = lax.ppermute(near_out, AXES, near_pairs)
-        far_in = lax.ppermute(far_out, AXES, far_pairs)
         q_all = lax.all_to_all(q, AXES, 0, 0).reshape(count * CV_DEV, cases)
-        return near_in, far_in, q_all
+        return far_in, near_in, q_all
 
     inverse = pl.pallas_call(
         stage_kernel,
@@ -421,7 +421,7 @@
         cost_estimate=pl.CostEstimate(flops=4 * size**3, bytes_accessed=4 * size * size, transcendentals=0),
     )(local_inverse[0])
     carried = jax.ShapeDtypeStruct((3 * plane_rows + pack_rows, cases), F32)
-    res, t, near_out, far_out, q = pl.pallas_call(
+    res, t, far_out, near_out, q = pl.pallas_call(
         first_kernel,
         out_shape=[field(window), field(window), carried, carried, q_shape],
         in_specs=[SMEM] + [VMEM] * 7,
@@ -429,14 +429,14 @@
         scratch_shapes=scratch,
         compiler_params=PARAMS,
         cost_estimate=cost,
-    )(local_order, loads, near_in, far_in, near_pack, far_pack, inverse, basis_pad)
-    near_in, far_in, q_all = move(near_out, far_out, q)
+    )(local_order, loads, far_in, near_in, far_pack, near_pack, inverse, basis_pad)
+    far_in, near_in, q_all = move(far_out, near_out, q)
     for iteration in range(1, ITERS):
         width = 2 if iteration == ITERS - 1 else 3
         outs = [field(planes), field(window), field(window), field(width), field(width), q_shape]
         if iteration == 1:
             kernel = second_kernel
-            operands = [local_order, q_all, mats_own, wide, own_rows, t, near_in, far_in, res, inverse, basis_pad]
+            operands = [local_order, q_all, mats_own, wide, own_rows, t, far_in, near_in, res, inverse, basis_pad]
             outs += [
                 jax.ShapeDtypeStruct((planes + 4, 2, NY, NZ, cases), F32),
                 jax.ShapeDtypeStruct((16, extent), F32),
@@ -444,9 +444,9 @@
             ]
         else:
             kernel = middle_kernel
-            operands = [local_order, q_all, inverse_rows, extents, mats_all, t, near_in, far_in, res, solution,
+            operands = [local_order, q_all, inverse_rows, extents, mats_all, t, far_in, near_in, res, solution,
                         inverse, basis_pad]
-        solution, res, t, near_out, far_out, q, *setup = pl.pallas_call(
+        solution, res, t, far_out, near_out, q, *setup = pl.pallas_call(
             functools.partial(kernel, width),
             out_shape=outs,
             in_specs=[SMEM] + [VMEM] * (len(operands) - 1),
@@ -457,7 +457,7 @@
         )(*operands)
         if setup:
             mats_all, extents, inverse_rows = setup
-        near_in, far_in, q_all = move(near_out, far_out, q)
+        far_in, near_in, q_all = move(far_out, near_out, q)
     solution, residual, coarse_values = pl.pallas_call(
         last_kernel,
         out_shape=[field(planes), field(planes), jax.ShapeDtypeStruct((CV_DEV, cases), F32)],
@@ -465,7 +465,7 @@
         out_specs=[VMEM] * 3,
         scratch_shapes=[z_scratch],
         compiler_params=PARAMS,
-    )(q_all, inverse_rows, extents, mats_all, t, near_in, far_in, res, solution)
+    )(q_all, inverse_rows, extents, mats_all, t, far_in, near_in, res, solution)
     return (
         solution.reshape(planes, components, nodes, cases),
         residual.reshape(planes, components, nodes, cases),

time: 65 us -> 64.5 us (level)
  blocking collectives: 40.3 us -> 33.6 us
  starting transfers between devices: 7.45 us -> 13.7 us
    all_to_all x3, blocking collectives: 40.3 us -> 33.6 us  [move(): q_all = lax.all_to_all(q, AXES, 0, 0).reshape(count * CV_DEV, cases)]
    ppermute x2, starting transfers between devices: 1.17 us -> 5.03 us  [the longest x1 4.36 us: body(): lax.ppermute(loads_plane((planes - 1) * (1 - odd)), AXES, near_pairs)]
    ppermute x3, starting transfers between devices: 4.28 us -> 6.59 us  [move(): near_in = lax.ppermute(near_out, AXES, near_pairs)]
where the time goes in v6:
time: 64.5 us; the launch traced here: 64.1 us
  blocking collectives  33.6 us (52%)
  Pallas kernels  15 us (23%)
  starting transfers between devices  13.7 us (21%)
  local copies, waits for them, and re-layouts  1.01 us (2%)
  between operations  0.87 us (1%)
    all_to_all x3, blocking collectives, move(): q_all = lax.all_to_all(q, AXES, 0, 0).reshape(count * CV_DEV, cases)  33.6 us
    pallas_call x2, Pallas kernels, body(): pl.pallas_call(functools.partial(kernel, width), out_shape=outs, in_specs...  7.3 us
    ppermute x3, starting transfers between devices, move(): near_in = lax.ppermute(near_out, AXES, near_pairs)  6.59 us
    ppermute x1, starting transfers between devices, body(): lax.ppermute(loads_plane((planes - 1) * (1 - odd)), AXES, near_pairs)  4.36 us
    pallas_call x1, Pallas kernels, body(): pl.pallas_call(first_kernel, out_shape=[field(window), field(window), car...  2.58 us
    ppermute x3, starting transfers between devices, move(): far_in = lax.ppermute(far_out, AXES, far_pairs)  2.03 us
    pallas_call x1, Pallas kernels, body(): pl.pallas_call(stage_kernel, out_shape=jax.ShapeDtypeStruct((size, size),...  1.77 us
    pallas_call x1, Pallas kernels, body(): pl.pallas_call(last_kernel, out_shape=[field(planes), field(planes), jax....  1.74 us
  transfers between devices with their start and end apart: 8, of which 0 were waited for; matrix products, arithmetic and copies ran while one was open for 0% of the time, Pallas kernels for 5%

profile of v6, /device:TPU:0, one launch (start us, length us, event | category | flops | bytes accessed | tf_op | source)
XLA Modules:
  0.0 64.1 jit_solution(15978018706002138830)
XLA Ops:
  0.6 1.0 %constant_dynamic-slice_fusion = (f32[1,3,64,128]{3,2,1,0:T(8,128)S(1)}, f32[1,3,64,128]{3,2,1,0:T(8,128)S(1)}) fusion(f32[4,3,64,128]{3,2,1,0:T(8,128)} %param.8, s32[]{:T(128)S(6)} %select_n.8, s32[]{:T(128)S(6)} %select_n.7), kind=kLoop, calls=%fused_computation | loop fusion | bytes 393224 | tf_op jit(solution)/shard_map/jit(dynamic_index_in_dim)/dynamic_slice | solution.py:369
  1.6 0.7 %collective-permute-start = (f32[192,128]{1,0:T(8,128)S(1)}, f32[192,128]{1,0:T(8,128)S(1)}, u32[]{:S(2)}, u32[]{:S(2)}) collective-permute-start(f32[192,128]{1,0:T(8,128)S(1)} %bitcast.17), channel_id=1, source_target_pairs={{1,2},{2,1},{3,4},{4,3},{5,6},{6,5},{7,8},{8,7},{9,10},{10,9},{11,... | collective-permute-start | bytes 294920 | tf_op jit(solution)/shard_map/ppermute | solution.py:371
  2.3 4.4 %collective-permute-start.1 = (f32[192,128]{1,0:T(8,128)S(1)}, f32[192,128]{1,0:T(8,128)S(1)}, u32[]{:S(2)}, u32[]{:S(2)}) collective-permute-start(f32[192,128]{1,0:T(8,128)S(1)} %bitcast.16), channel_id=1, source_target_pairs={{0,1},{1,0},{2,3},{3,2},{4,5},{5,4},{6,7},{7,6},{8,9},{9,8},{10,11... | collective-permute-start | bytes 294920 | tf_op jit(solution)/shard_map/ppermute | solution.py:372
  6.6 1.6 %shard_map.103 = (f32[48,128]{1,0:T(8,128)}, f32[48,128]{1,0:T(8,128)}, f32[4,128]{1,0:T(4,128)}, f32[4,128]{1,0:T(4,128)}, f32[4,1536]{1,0:T(4,128)}) custom-call(f32[1,8]{1,0:T(1,128)} %bitcast.23, f32[1,8]{1,0:T(1,128)} %bitcast.24, s32[4,64]{1,0:T(4,128)} %labels_hbm.1, f32[4,1152]{1,0:T(4,128)} %bitcast.18, f32[8,128]{1,0:T(8,128)} %coarse_hbm.1), custom_call_target="tpu_custom_call" | custom-call | flops 12230590464 | bytes 5308416 | tf_op jit(solution)/shard_map/pallas_call | solution.py:376
  8.2 0.0 copy-start.7
  8.2 0.0 copy-start
  8.3 0.0 copy-start.1
  8.3 0.0 copy-start.3
  8.3 0.0 copy-start.4
  8.3 1.8 %shard_map.104.inverse_ref = bf16[1152,1152]{1,0:T(8,128)(2,1)S(1)} custom-call(bf16[1152,1152]{1,0:T(8,128)(2,1)} %bitcast.20), custom_call_target="tpu_custom_call" | custom-call | flops 6115295232 | bytes 5308416 | tf_op jit(solution)/shard_map/pallas_call | solution.py:414
  10.1 0.0 copy-start.5
  10.2 2.6 %shard_map.105 = (f32[1152,128]{1,0:T(8,128)S(1)}, f32[1152,128]{1,0:T(8,128)S(1)}, f32[624,128]{1,0:T(8,128)S(1)}, f32[624,128]{1,0:T(8,128)S(1)}, f32[32,4,128]{2,1,0:T(4,128)S(1)}) custom-call(s32[1,1152]{1,0:T(1,128)S(1)} %copy-done.1, f32[768,128]{1,0:T(8,128)S(1)} %bitcast.12, f32[192,128]{1,0:T(8,128)S(1)} %collective-permute-done.far_in_ref, ...), custom_call_target="tpu_custom_call" | custom-call | flops 339738624 | bytes 2654208 | tf_op jit(solution)/shard_map/pallas_call | solution.py:424
  12.8 0.7 %collective-permute-start.2 = (f32[624,128]{1,0:T(8,128)S(1)}, f32[624,128]{1,0:T(8,128)S(1)}, u32[]{:S(2)}, u32[]{:S(2)}) collective-permute-start(f32[624,128]{1,0:T(8,128)S(1)} %get-tuple-element.38), channel_id=1, source_target_pairs={{1,2},{2,1},{3,4},{4,3},{5,6},{6,5},{7,8},{8,7},{9,10},{10,9},{11,... | collective-permute-start | bytes 958472 | tf_op jit(solution)/shard_map/ppermute | solution.py:409
  13.5 2.9 %collective-permute-start.3 = (f32[624,128]{1,0:T(8,128)S(1)}, f32[624,128]{1,0:T(8,128)S(1)}, u32[]{:S(2)}, u32[]{:S(2)}) collective-permute-start(f32[624,128]{1,0:T(8,128)S(1)} %get-tuple-element.39), channel_id=1, source_target_pairs={{0,1},{1,0},{2,3},{3,2},{4,5},{5,4},{6,7},{7,6},{8,9},{9,8},{10,11... | collective-permute-start | bytes 958472 | tf_op jit(solution)/shard_map/ppermute | solution.py:410
  16.4 12.8 %all_to_all.15 = f32[32,4,128]{2,1,0:T(4,128)S(1)} all-to-all(f32[32,4,128]{2,1,0:T(4,128)S(1)} %get-tuple-element.33), channel_id=1, replica_groups=mesh['sub'=16,'grp'=2] {'sub','grp'}, dimensions={0} | all-to-all | bytes 131072 | tf_op jit(solution)/shard_map/all_to_all | solution.py:411
  29.2 3.6 %shard_map.106 = (f32[768,128]{1,0:T(8,128)S(1)}, f32[1152,128]{1,0:T(8,128)S(1)}, f32[1152,128]{1,0:T(8,128)S(1)}, f32[576,128]{1,0:T(8,128)S(1)}, f32[576,128]...) custom-call(s32[1,1152]{1,0:T(1,128)S(1)} %copy-done.1, ...), custom_call_target="tpu_custom_call" | custom-call | flops 339738624 | bytes 2654208 | tf_op jit(solution)/shard_map/pallas_call | solution.py:449
  32.8 0.7 %collective-permute-start.4 = (f32[576,128]{1,0:T(8,128)S(1)}, f32[576,128]{1,0:T(8,128)S(1)}, u32[]{:S(2)}, u32[]{:S(2)}) collective-permute-start(f32[576,128]{1,0:T(8,128)S(1)} %get-tuple-element.46), channel_id=1, source_target_pairs={{1,2},{2,1},{3,4},{4,3},{5,6},{6,5},{7,8},{8,7},{9,10},{10,9},{11,... | collective-permute-start | bytes 884744 | tf_op jit(solution)/shard_map/ppermute | solution.py:409
  33.5 1.8 %collective-permute-start.5 = (f32[576,128]{1,0:T(8,128)S(1)}, f32[576,128]{1,0:T(8,128)S(1)}, u32[]{:S(2)}, u32[]{:S(2)}) collective-permute-start(f32[576,128]{1,0:T(8,128)S(1)} %get-tuple-element.47), channel_id=1, source_target_pairs={{0,1},{1,0},{2,3},{3,2},{4,5},{5,4},{6,7},{7,6},{8,9},{9,8},{10,11... | collective-permute-start | bytes 884744 | tf_op jit(solution)/shard_map/ppermute | solution.py:410
  35.3 10.4 %all_to_all.16 = f32[32,4,128]{2,1,0:T(4,128)S(1)} all-to-all(f32[32,4,128]{2,1,0:T(4,128)S(1)} %get-tuple-element.41), channel_id=1, replica_groups=mesh['sub'=16,'grp'=2] {'sub','grp'}, dimensions={0} | all-to-all | bytes 131072 | tf_op jit(solution)/shard_map/all_to_all | solution.py:411
  45.7 3.7 %shard_map.107 = (f32[768,128]{1,0:T(8,128)S(1)}, f32[1152,128]{1,0:T(8,128)S(1)}, f32[1152,128]{1,0:T(8,128)S(1)}, f32[384,128]{1,0:T(8,128)S(1)}, f32[384,128]{1,0:T(8,128)S(1)}, /*index=5*/f32[32,4,128]{2,1,0:T(4,128)S(1)}) custom-call(s32[1,1152]{1,0:T(1,128)S(1)} %copy-done.1, f32[128,128]{1,0:T(8,128)S(1)} %bitcast.14, ...), custom_call_target="tpu_custom_call" | custom-call | flops 339738624 | bytes 2654208 | tf_op jit(solution)/shard_map/pallas_call | solution.py:449
  49.4 0.7 %collective-permute-start.6 = (f32[384,128]{1,0:T(8,128)S(1)}, f32[384,128]{1,0:T(8,128)S(1)}, u32[]{:S(2)}, u32[]{:S(2)}) collective-permute-start(f32[384,128]{1,0:T(8,128)S(1)} %get-tuple-element.52), channel_id=1, source_target_pairs={{1,2},{2,1},{3,4},{4,3},{5,6},{6,5},{7,8},{8,7},{9,10},{10,9},{11,... | collective-permute-start | bytes 589832 | tf_op jit(solution)/shard_map/ppermute | solution.py:409
  50.1 1.9 %collective-permute-start.7 = (f32[384,128]{1,0:T(8,128)S(1)}, f32[384,128]{1,0:T(8,128)S(1)}, u32[]{:S(2)}, u32[]{:S(2)}) collective-permute-start(f32[384,128]{1,0:T(8,128)S(1)} %get-tuple-element.53), channel_id=1, source_target_pairs={{0,1},{1,0},{2,3},{3,2},{4,5},{5,4},{6,7},{7,6},{8,9},{9,8},{10,11... | collective-permute-start | bytes 589832 | tf_op jit(solution)/shard_map/ppermute | solution.py:410
  52.0 10.4 %all_to_all.17 = f32[32,4,128]{2,1,0:T(4,128)S(1)} all-to-all(f32[32,4,128]{2,1,0:T(4,128)S(1)} %get-tuple-element.50), channel_id=1, replica_groups=mesh['sub'=16,'grp'=2] {'sub','grp'}, dimensions={0} | all-to-all | bytes 131072 | tf_op jit(solution)/shard_map/all_to_all | solution.py:411
  62.4 1.7 %shard_map.108 = (f32[768,128]{1,0:T(8,128)}, f32[768,128]{1,0:T(8,128)}, f32[4,128]{1,0:T(4,128)}) custom-call(f32[128,128]{1,0:T(8,128)S(1)} %bitcast.15, f32[16,128]{1,0:T(8,128)S(1)} %get-tuple-element.42.rows_ref, f32[16,1536]{1,0:T(8,128)S(1)} %get-tuple-element.43.extent_ref, f32[8,2,8,8,128]{4,3,2,1,0:T(8,128)S(1)} %get-tuple-element.44.mats_ref, ...), custom_call_target="tpu_custom_call" | custom-call | tf_op jit(solution)/shard_map/pallas_call | solution.py:461
  (19 shorter events, 0.0 us)
Async XLA Ops:
  1.6 8.5 %collective-permute-start = (f32[192,128]{1,0:T(8,128)S(1)}, f32[192,128]{1,0:T(8,128)S(1)}, u32[]{:S(2)}, u32[]{:S(2)}) collective-permute-start(f32[192,128]{1,0:T(8,128)S(1)} %bitcast.17), channel_id=1, source_target_pairs={{1,2},{2,1},{3,4},{4,3},{5,6},{6,5},{7,8},{8,7},{9,10},{10,9},{11,... | collective-permute-start | bytes 294920 | tf_op jit(solution)/shard_map/ppermute | solution.py:371
  2.3 7.9 %collective-permute-start.1 = (f32[192,128]{1,0:T(8,128)S(1)}, f32[192,128]{1,0:T(8,128)S(1)}, u32[]{:S(2)}, u32[]{:S(2)}) collective-permute-start(f32[192,128]{1,0:T(8,128)S(1)} %bitcast.16), channel_id=1, source_target_pairs={{0,1},{1,0},{2,3},{3,2},{4,5},{5,4},{6,7},{7,6},{8,9},{9,8},{10,11... | collective-permute-start | bytes 294920 | tf_op jit(solution)/shard_map/ppermute | solution.py:372
  8.2 1.8 %copy-start.7 = (f32[1,4,1152]{2,1,0:T(4,128)S(1)}, f32[1,4,1152]{2,1,0:T(4,128)}, u32[]{:S(2)}) copy-start(f32[1,4,1152]{2,1,0:T(4,128)} %param.14) | copy-start | bytes 55300
  8.2 1.9 %copy-start = (f32[4,3,64,128]{3,2,1,0:T(8,128)S(1)}, f32[4,3,64,128]{3,2,1,0:T(8,128)}, u32[]{:S(2)}) copy-start(f32[4,3,64,128]{3,2,1,0:T(8,128)} %param.8) | copy-start | bytes 1179652
  8.3 1.9 %copy-start.1 = (s32[1,1152]{1,0:T(1,128)S(1)}, s32[1,1152]{1,0:T(1,128)}, u32[]{:S(2)}) copy-start(s32[1,1152]{1,0:T(1,128)} %order_ref.5) | copy-start | bytes 13828
  8.3 1.9 %copy-start.3 = (f32[48,128]{1,0:T(8,128)S(1)}, f32[48,128]{1,0:T(8,128)}, u32[]{:S(2)}) copy-start(f32[48,128]{1,0:T(8,128)} %get-tuple-element.31.far_pack_ref) | copy-start | bytes 73732
  8.3 1.9 %copy-start.4 = (f32[48,128]{1,0:T(8,128)S(1)}, f32[48,128]{1,0:T(8,128)}, u32[]{:S(2)}) copy-start(f32[48,128]{1,0:T(8,128)} %get-tuple-element.32.near_pack_ref) | copy-start | bytes 73732
  10.1 19.1 %copy-start.2 = (f32[4,1536]{1,0:T(4,128)S(1)}, f32[4,1536]{1,0:T(4,128)}, u32[]{:S(2)}) copy-start(f32[4,1536]{1,0:T(4,128)} %get-tuple-element.35.wide_ref) | copy-start | bytes 73732
  10.1 19.0 %copy-start.5 = (f32[4,128]{1,0:T(4,128)S(1)}, f32[4,128]{1,0:T(4,128)}, u32[]{:S(2)}) copy-start(f32[4,128]{1,0:T(4,128)} %get-tuple-element.34.mats_in_ref) | copy-start | bytes 6148
  10.1 19.0 %copy-start.6 = (f32[4,128]{1,0:T(4,128)S(1)}, f32[4,128]{1,0:T(4,128)}, u32[]{:S(2)}) copy-start(f32[4,128]{1,0:T(4,128)} %get-tuple-element.36.own_rows_ref) | copy-start | bytes 6148
  12.8 16.4 %collective-permute-start.2 = (f32[624,128]{1,0:T(8,128)S(1)}, f32[624,128]{1,0:T(8,128)S(1)}, u32[]{:S(2)}, u32[]{:S(2)}) collective-permute-start(f32[624,128]{1,0:T(8,128)S(1)} %get-tuple-element.38), channel_id=1, source_target_pairs={{1,2},{2,1},{3,4},{4,3},{5,6},{6,5},{7,8},{8,7},{9,10},{10,9},{11,... | collective-permute-start | bytes 958472 | tf_op jit(solution)/shard_map/ppermute | solution.py:409
  13.5 15.7 %collective-permute-start.3 = (f32[624,128]{1,0:T(8,128)S(1)}, f32[624,128]{1,0:T(8,128)S(1)}, u32[]{:S(2)}, u32[]{:S(2)}) collective-permute-start(f32[624,128]{1,0:T(8,128)S(1)} %get-tuple-element.39), channel_id=1, source_target_pairs={{0,1},{1,0},{2,3},{3,2},{4,5},{5,4},{6,7},{7,6},{8,9},{9,8},{10,11... | collective-permute-start | bytes 958472 | tf_op jit(solution)/shard_map/ppermute | solution.py:410
  32.8 12.9 %collective-permute-start.4 = (f32[576,128]{1,0:T(8,128)S(1)}, f32[576,128]{1,0:T(8,128)S(1)}, u32[]{:S(2)}, u32[]{:S(2)}) collective-permute-start(f32[576,128]{1,0:T(8,128)S(1)} %get-tuple-element.46), channel_id=1, source_target_pairs={{1,2},{2,1},{3,4},{4,3},{5,6},{6,5},{7,8},{8,7},{9,10},{10,9},{11,... | collective-permute-start | bytes 884744 | tf_op jit(solution)/shard_map/ppermute | solution.py:409
  33.5 12.3 %collective-permute-start.5 = (f32[576,128]{1,0:T(8,128)S(1)}, f32[576,128]{1,0:T(8,128)S(1)}, u32[]{:S(2)}, u32[]{:S(2)}) collective-permute-start(f32[576,128]{1,0:T(8,128)S(1)} %get-tuple-element.47), channel_id=1, source_target_pairs={{0,1},{1,0},{2,3},{3,2},{4,5},{5,4},{6,7},{7,6},{8,9},{9,8},{10,11... | collective-permute-start | bytes 884744 | tf_op jit(solution)/shard_map/ppermute | solution.py:410
  49.4 12.9 %collective-permute-start.6 = (f32[384,128]{1,0:T(8,128)S(1)}, f32[384,128]{1,0:T(8,128)S(1)}, u32[]{:S(2)}, u32[]{:S(2)}) collective-permute-start(f32[384,128]{1,0:T(8,128)S(1)} %get-tuple-element.52), channel_id=1, source_target_pairs={{1,2},{2,1},{3,4},{4,3},{5,6},{6,5},{7,8},{8,7},{9,10},{10,9},{11,... | collective-permute-start | bytes 589832 | tf_op jit(solution)/shard_map/ppermute | solution.py:409
  50.1 12.3 %collective-permute-start.7 = (f32[384,128]{1,0:T(8,128)S(1)}, f32[384,128]{1,0:T(8,128)S(1)}, u32[]{:S(2)}, u32[]{:S(2)}) collective-permute-start(f32[384,128]{1,0:T(8,128)S(1)} %get-tuple-element.53), channel_id=1, source_target_pairs={{0,1},{1,0},{2,3},{3,2},{4,5},{5,4},{6,7},{7,6},{8,9},{9,8},{10,11... | collective-permute-start | bytes 589832 | tf_op jit(solution)/shard_map/ppermute | solution.py:410

commit v7 on v6

--- a/solution.py
+++ b/solution.py
@@ -12,6 +12,7 @@
 CV_DEV = 4
 ITERS = 3
 RELAXATION = 0.5
+DEPTH = 640
 AXES = ("sub", "grp")
 F32 = jnp.float32
 BF16 = jnp.bfloat16
@@ -188,15 +189,19 @@
 def products(width, order_ref, inverse_ref, basis_ref, ordered_ref, product_ref, res_ref, t_ref, far_ref, near_ref,
              q_ref):
     size = res_ref.shape[0]
-    for row in range(size):
-        ordered_ref[row : row + 1, :] = res_ref[pl.ds(order_ref[0, row], 1), :]
-    ordered = ordered_ref[...].astype(BF16)
     step = size // 3
-    for i in range(3):
-        part = slice(i * step, (i + 1) * step)
-        product_ref[part, :] = jnp.dot(inverse_ref[part, :], ordered, preferred_element_type=F32)
-        for row in range(i * step, (i + 1) * step):
-            t_ref[pl.ds(order_ref[0, row], 1), :] = product_ref[row : row + 1, :]
+    for start in range(0, size, DEPTH):
+        chunk = slice(start, min(start + DEPTH, size))
+        for row in range(chunk.start, chunk.stop):
+            ordered_ref[row : row + 1, :] = res_ref[pl.ds(order_ref[0, row], 1), :]
+        ordered = ordered_ref[chunk, :].astype(BF16)
+        for i in range(3):
+            part = slice(i * step, (i + 1) * step)
+            value = jnp.dot(inverse_ref[part, chunk], ordered, preferred_element_type=F32)
+            product_ref[part, :] = value if start == 0 else product_ref[part, :] + value
+            if chunk.stop == size:
+                for row in range(part.start, part.stop):
+                    t_ref[pl.ds(order_ref[0, row], 1), :] = product_ref[row : row + 1, :]
     odd, _, _ = position()
     to_right = size - width
     far_ref[:width] = t_ref[pl.ds(pl.multiple_of(to_right * odd, 8), width), :]

time: 64.5 us -> 64.4 us (level)
  no operation moved by 1% of the time
where the time goes in v7:
time: 64.4 us; the launch traced here: 64 us
  blocking collectives  33.6 us (52%)
  Pallas kernels  14.9 us (23%)
  starting transfers between devices  13.6 us (21%)
  local copies, waits for them, and re-layouts  1.01 us (2%)
  between operations  0.87 us (1%)
    all_to_all x3, blocking collectives, move(): q_all = lax.all_to_all(q, AXES, 0, 0).reshape(count * CV_DEV, cases)  33.6 us
    pallas_call x2, Pallas kernels, body(): pl.pallas_call(functools.partial(kernel, width), out_shape=outs, in_specs...  7.18 us
    ppermute x3, starting transfers between devices, move(): near_in = lax.ppermute(near_out, AXES, near_pairs)  6.57 us
    ppermute x1, starting transfers between devices, body(): lax.ppermute(loads_plane((planes - 1) * (1 - odd)), AXES, near_pairs)  4.36 us
    pallas_call x1, Pallas kernels, body(): pl.pallas_call(first_kernel, out_shape=[field(window), field(window), car...  2.62 us
    ppermute x3, starting transfers between devices, move(): far_in = lax.ppermute(far_out, AXES, far_pairs)  2.03 us
    pallas_call x1, Pallas kernels, body(): pl.pallas_call(stage_kernel, out_shape=jax.ShapeDtypeStruct((size, size),...  1.77 us
    pallas_call x1, Pallas kernels, body(): pl.pallas_call(last_kernel, out_shape=[field(planes), field(planes), jax....  1.74 us
  transfers between devices with their start and end apart: 8, of which 0 were waited for; matrix products, arithmetic and copies ran while one was open for 0% of the time, Pallas kernels for 5%

profile of v7, /device:TPU:0, one launch (start us, length us, event | category | flops | bytes accessed | tf_op | source)
XLA Modules:
  0.0 64.0 jit_solution(8314821747840737569)
XLA Ops:
  0.6 1.0 %constant_dynamic-slice_fusion = (f32[1,3,64,128]{3,2,1,0:T(8,128)S(1)}, f32[1,3,64,128]{3,2,1,0:T(8,128)S(1)}) fusion(f32[4,3,64,128]{3,2,1,0:T(8,128)} %param.8, s32[]{:T(128)S(6)} %select_n.8, s32[]{:T(128)S(6)} %select_n.7), kind=kLoop, calls=%fused_computation | loop fusion | bytes 393224 | tf_op jit(solution)/shard_map/jit(dynamic_index_in_dim)/dynamic_slice | solution.py:374
  1.6 0.7 %collective-permute-start = (f32[192,128]{1,0:T(8,128)S(1)}, f32[192,128]{1,0:T(8,128)S(1)}, u32[]{:S(2)}, u32[]{:S(2)}) collective-permute-start(f32[192,128]{1,0:T(8,128)S(1)} %bitcast.17), channel_id=1, source_target_pairs={{1,2},{2,1},{3,4},{4,3},{5,6},{6,5},{7,8},{8,7},{9,10},{10,9},{11,... | collective-permute-start | bytes 294920 | tf_op jit(solution)/shard_map/ppermute | solution.py:376
  2.3 4.4 %collective-permute-start.1 = (f32[192,128]{1,0:T(8,128)S(1)}, f32[192,128]{1,0:T(8,128)S(1)}, u32[]{:S(2)}, u32[]{:S(2)}) collective-permute-start(f32[192,128]{1,0:T(8,128)S(1)} %bitcast.16), channel_id=1, source_target_pairs={{0,1},{1,0},{2,3},{3,2},{4,5},{5,4},{6,7},{7,6},{8,9},{9,8},{10,11... | collective-permute-start | bytes 294920 | tf_op jit(solution)/shard_map/ppermute | solution.py:377
  6.6 1.6 %shard_map.103 = (f32[48,128]{1,0:T(8,128)}, f32[48,128]{1,0:T(8,128)}, f32[4,128]{1,0:T(4,128)}, f32[4,128]{1,0:T(4,128)}, f32[4,1536]{1,0:T(4,128)}) custom-call(f32[1,8]{1,0:T(1,128)} %bitcast.23, f32[1,8]{1,0:T(1,128)} %bitcast.24, s32[4,64]{1,0:T(4,128)} %labels_hbm.1, f32[4,1152]{1,0:T(4,128)} %bitcast.18, f32[8,128]{1,0:T(8,128)} %coarse_hbm.1), custom_call_target="tpu_custom_call" | custom-call | flops 12230590464 | bytes 5308416 | tf_op jit(solution)/shard_map/pallas_call | solution.py:381
  8.2 0.0 copy-start.7
  8.2 0.0 copy-start
  8.3 0.0 copy-start.1
  8.3 0.0 copy-start.3
  8.3 0.0 copy-start.4
  8.3 1.8 %shard_map.104.inverse_ref = bf16[1152,1152]{1,0:T(8,128)(2,1)S(1)} custom-call(bf16[1152,1152]{1,0:T(8,128)(2,1)} %bitcast.20), custom_call_target="tpu_custom_call" | custom-call | flops 6115295232 | bytes 5308416 | tf_op jit(solution)/shard_map/pallas_call | solution.py:419
  10.1 0.0 copy-start.5
  10.2 2.6 %shard_map.105 = (f32[1152,128]{1,0:T(8,128)S(1)}, f32[1152,128]{1,0:T(8,128)S(1)}, f32[624,128]{1,0:T(8,128)S(1)}, f32[624,128]{1,0:T(8,128)S(1)}, f32[32,4,128]{2,1,0:T(4,128)S(1)}) custom-call(s32[1,1152]{1,0:T(1,128)S(1)} %copy-done.1, f32[768,128]{1,0:T(8,128)S(1)} %bitcast.12, f32[192,128]{1,0:T(8,128)S(1)} %collective-permute-done.far_in_ref, ...), custom_call_target="tpu_custom_call" | custom-call | flops 339738624 | bytes 2654208 | tf_op jit(solution)/shard_map/pallas_call | solution.py:429
  12.8 0.7 %collective-permute-start.2 = (f32[624,128]{1,0:T(8,128)S(1)}, f32[624,128]{1,0:T(8,128)S(1)}, u32[]{:S(2)}, u32[]{:S(2)}) collective-permute-start(f32[624,128]{1,0:T(8,128)S(1)} %get-tuple-element.38), channel_id=1, source_target_pairs={{1,2},{2,1},{3,4},{4,3},{5,6},{6,5},{7,8},{8,7},{9,10},{10,9},{11,... | collective-permute-start | bytes 958472 | tf_op jit(solution)/shard_map/ppermute | solution.py:414
  13.5 2.9 %collective-permute-start.3 = (f32[624,128]{1,0:T(8,128)S(1)}, f32[624,128]{1,0:T(8,128)S(1)}, u32[]{:S(2)}, u32[]{:S(2)}) collective-permute-start(f32[624,128]{1,0:T(8,128)S(1)} %get-tuple-element.39), channel_id=1, source_target_pairs={{0,1},{1,0},{2,3},{3,2},{4,5},{5,4},{6,7},{7,6},{8,9},{9,8},{10,11... | collective-permute-start | bytes 958472 | tf_op jit(solution)/shard_map/ppermute | solution.py:415
  16.4 12.8 %all_to_all.15 = f32[32,4,128]{2,1,0:T(4,128)S(1)} all-to-all(f32[32,4,128]{2,1,0:T(4,128)S(1)} %get-tuple-element.33), channel_id=1, replica_groups=mesh['sub'=16,'grp'=2] {'sub','grp'}, dimensions={0} | all-to-all | bytes 131072 | tf_op jit(solution)/shard_map/all_to_all | solution.py:416
  29.2 3.5 %shard_map.106 = (f32[768,128]{1,0:T(8,128)S(1)}, f32[1152,128]{1,0:T(8,128)S(1)}, f32[1152,128]{1,0:T(8,128)S(1)}, f32[576,128]{1,0:T(8,128)S(1)}, f32[576,128]...) custom-call(s32[1,1152]{1,0:T(1,128)S(1)} %copy-done.1, ...), custom_call_target="tpu_custom_call" | custom-call | flops 339738624 | bytes 2654208 | tf_op jit(solution)/shard_map/pallas_call | solution.py:454
  32.8 0.7 %collective-permute-start.4 = (f32[576,128]{1,0:T(8,128)S(1)}, f32[576,128]{1,0:T(8,128)S(1)}, u32[]{:S(2)}, u32[]{:S(2)}) collective-permute-start(f32[576,128]{1,0:T(8,128)S(1)} %get-tuple-element.46), channel_id=1, source_target_pairs={{1,2},{2,1},{3,4},{4,3},{5,6},{6,5},{7,8},{8,7},{9,10},{10,9},{11,... | collective-permute-start | bytes 884744 | tf_op jit(solution)/shard_map/ppermute | solution.py:414
  33.5 1.8 %collective-permute-start.5 = (f32[576,128]{1,0:T(8,128)S(1)}, f32[576,128]{1,0:T(8,128)S(1)}, u32[]{:S(2)}, u32[]{:S(2)}) collective-permute-start(f32[576,128]{1,0:T(8,128)S(1)} %get-tuple-element.47), channel_id=1, source_target_pairs={{0,1},{1,0},{2,3},{3,2},{4,5},{5,4},{6,7},{7,6},{8,9},{9,8},{10,11... | collective-permute-start | bytes 884744 | tf_op jit(solution)/shard_map/ppermute | solution.py:415
  35.3 10.4 %all_to_all.16 = f32[32,4,128]{2,1,0:T(4,128)S(1)} all-to-all(f32[32,4,128]{2,1,0:T(4,128)S(1)} %get-tuple-element.41), channel_id=1, replica_groups=mesh['sub'=16,'grp'=2] {'sub','grp'}, dimensions={0} | all-to-all | bytes 131072 | tf_op jit(solution)/shard_map/all_to_all | solution.py:416
  45.7 3.6 %shard_map.107 = (f32[768,128]{1,0:T(8,128)S(1)}, f32[1152,128]{1,0:T(8,128)S(1)}, f32[1152,128]{1,0:T(8,128)S(1)}, f32[384,128]{1,0:T(8,128)S(1)}, f32[384,128]{1,0:T(8,128)S(1)}, /*index=5*/f32[32,4,128]{2,1,0:T(4,128)S(1)}) custom-call(s32[1,1152]{1,0:T(1,128)S(1)} %copy-done.1, f32[128,128]{1,0:T(8,128)S(1)} %bitcast.14, ...), custom_call_target="tpu_custom_call" | custom-call | flops 339738624 | bytes 2654208 | tf_op jit(solution)/shard_map/pallas_call | solution.py:454
  49.3 0.7 %collective-permute-start.6 = (f32[384,128]{1,0:T(8,128)S(1)}, f32[384,128]{1,0:T(8,128)S(1)}, u32[]{:S(2)}, u32[]{:S(2)}) collective-permute-start(f32[384,128]{1,0:T(8,128)S(1)} %get-tuple-element.52), channel_id=1, source_target_pairs={{1,2},{2,1},{3,4},{4,3},{5,6},{6,5},{7,8},{8,7},{9,10},{10,9},{11,... | collective-permute-start | bytes 589832 | tf_op jit(solution)/shard_map/ppermute | solution.py:414
  50.0 1.9 %collective-permute-start.7 = (f32[384,128]{1,0:T(8,128)S(1)}, f32[384,128]{1,0:T(8,128)S(1)}, u32[]{:S(2)}, u32[]{:S(2)}) collective-permute-start(f32[384,128]{1,0:T(8,128)S(1)} %get-tuple-element.53), channel_id=1, source_target_pairs={{0,1},{1,0},{2,3},{3,2},{4,5},{5,4},{6,7},{7,6},{8,9},{9,8},{10,11... | collective-permute-start | bytes 589832 | tf_op jit(solution)/shard_map/ppermute | solution.py:415
  51.9 10.4 %all_to_all.17 = f32[32,4,128]{2,1,0:T(4,128)S(1)} all-to-all(f32[32,4,128]{2,1,0:T(4,128)S(1)} %get-tuple-element.50), channel_id=1, replica_groups=mesh['sub'=16,'grp'=2] {'sub','grp'}, dimensions={0} | all-to-all | bytes 131072 | tf_op jit(solution)/shard_map/all_to_all | solution.py:416
  62.3 1.7 %shard_map.108 = (f32[768,128]{1,0:T(8,128)}, f32[768,128]{1,0:T(8,128)}, f32[4,128]{1,0:T(4,128)}) custom-call(f32[128,128]{1,0:T(8,128)S(1)} %bitcast.15, f32[16,128]{1,0:T(8,128)S(1)} %get-tuple-element.42.rows_ref, f32[16,1536]{1,0:T(8,128)S(1)} %get-tuple-element.43.extent_ref, f32[8,2,8,8,128]{4,3,2,1,0:T(8,128)S(1)} %get-tuple-element.44.mats_ref, ...), custom_call_target="tpu_custom_call" | custom-call | tf_op jit(solution)/shard_map/pallas_call | solution.py:466
  (19 shorter events, 0.0 us)
Async XLA Ops:
  1.6 8.5 %collective-permute-start = (f32[192,128]{1,0:T(8,128)S(1)}, f32[192,128]{1,0:T(8,128)S(1)}, u32[]{:S(2)}, u32[]{:S(2)}) collective-permute-start(f32[192,128]{1,0:T(8,128)S(1)} %bitcast.17), channel_id=1, source_target_pairs={{1,2},{2,1},{3,4},{4,3},{5,6},{6,5},{7,8},{8,7},{9,10},{10,9},{11,... | collective-permute-start | bytes 294920 | tf_op jit(solution)/shard_map/ppermute | solution.py:376
  2.3 7.9 %collective-permute-start.1 = (f32[192,128]{1,0:T(8,128)S(1)}, f32[192,128]{1,0:T(8,128)S(1)}, u32[]{:S(2)}, u32[]{:S(2)}) collective-permute-start(f32[192,128]{1,0:T(8,128)S(1)} %bitcast.16), channel_id=1, source_target_pairs={{0,1},{1,0},{2,3},{3,2},{4,5},{5,4},{6,7},{7,6},{8,9},{9,8},{10,11... | collective-permute-start | bytes 294920 | tf_op jit(solution)/shard_map/ppermute | solution.py:377
  8.2 1.8 %copy-start.7 = (f32[1,4,1152]{2,1,0:T(4,128)S(1)}, f32[1,4,1152]{2,1,0:T(4,128)}, u32[]{:S(2)}) copy-start(f32[1,4,1152]{2,1,0:T(4,128)} %param.14) | copy-start | bytes 55300
  8.2 1.9 %copy-start = (f32[4,3,64,128]{3,2,1,0:T(8,128)S(1)}, f32[4,3,64,128]{3,2,1,0:T(8,128)}, u32[]{:S(2)}) copy-start(f32[4,3,64,128]{3,2,1,0:T(8,128)} %param.8) | copy-start | bytes 1179652
  8.3 1.9 %copy-start.1 = (s32[1,1152]{1,0:T(1,128)S(1)}, s32[1,1152]{1,0:T(1,128)}, u32[]{:S(2)}) copy-start(s32[1,1152]{1,0:T(1,128)} %order_ref.5) | copy-start | bytes 13828
  8.3 1.9 %copy-start.3 = (f32[48,128]{1,0:T(8,128)S(1)}, f32[48,128]{1,0:T(8,128)}, u32[]{:S(2)}) copy-start(f32[48,128]{1,0:T(8,128)} %get-tuple-element.31.far_pack_ref) | copy-start | bytes 73732
  8.3 1.9 %copy-start.4 = (f32[48,128]{1,0:T(8,128)S(1)}, f32[48,128]{1,0:T(8,128)}, u32[]{:S(2)}) copy-start(f32[48,128]{1,0:T(8,128)} %get-tuple-element.32.near_pack_ref) | copy-start | bytes 73732
  10.1 19.1 %copy-start.2 = (f32[4,1536]{1,0:T(4,128)S(1)}, f32[4,1536]{1,0:T(4,128)}, u32[]{:S(2)}) copy-start(f32[4,1536]{1,0:T(4,128)} %get-tuple-element.35.wide_ref) | copy-start | bytes 73732
  10.1 19.1 %copy-start.5 = (f32[4,128]{1,0:T(4,128)S(1)}, f32[4,128]{1,0:T(4,128)}, u32[]{:S(2)}) copy-start(f32[4,128]{1,0:T(4,128)} %get-tuple-element.34.mats_in_ref) | copy-start | bytes 6148
  10.1 19.1 %copy-start.6 = (f32[4,128]{1,0:T(4,128)S(1)}, f32[4,128]{1,0:T(4,128)}, u32[]{:S(2)}) copy-start(f32[4,128]{1,0:T(4,128)} %get-tuple-element.36.own_rows_ref) | copy-start | bytes 6148
  12.8 16.4 %collective-permute-start.2 = (f32[624,128]{1,0:T(8,128)S(1)}, f32[624,128]{1,0:T(8,128)S(1)}, u32[]{:S(2)}, u32[]{:S(2)}) collective-permute-start(f32[624,128]{1,0:T(8,128)S(1)} %get-tuple-element.38), channel_id=1, source_target_pairs={{1,2},{2,1},{3,4},{4,3},{5,6},{6,5},{7,8},{8,7},{9,10},{10,9},{11,... | collective-permute-start | bytes 958472 | tf_op jit(solution)/shard_map/ppermute | solution.py:414
  13.5 15.7 %collective-permute-start.3 = (f32[624,128]{1,0:T(8,128)S(1)}, f32[624,128]{1,0:T(8,128)S(1)}, u32[]{:S(2)}, u32[]{:S(2)}) collective-permute-start(f32[624,128]{1,0:T(8,128)S(1)} %get-tuple-element.39), channel_id=1, source_target_pairs={{0,1},{1,0},{2,3},{3,2},{4,5},{5,4},{6,7},{7,6},{8,9},{9,8},{10,11... | collective-permute-start | bytes 958472 | tf_op jit(solution)/shard_map/ppermute | solution.py:415
  32.8 12.9 %collective-permute-start.4 = (f32[576,128]{1,0:T(8,128)S(1)}, f32[576,128]{1,0:T(8,128)S(1)}, u32[]{:S(2)}, u32[]{:S(2)}) collective-permute-start(f32[576,128]{1,0:T(8,128)S(1)} %get-tuple-element.46), channel_id=1, source_target_pairs={{1,2},{2,1},{3,4},{4,3},{5,6},{6,5},{7,8},{8,7},{9,10},{10,9},{11,... | collective-permute-start | bytes 884744 | tf_op jit(solution)/shard_map/ppermute | solution.py:414
  33.5 12.2 %collective-permute-start.5 = (f32[576,128]{1,0:T(8,128)S(1)}, f32[576,128]{1,0:T(8,128)S(1)}, u32[]{:S(2)}, u32[]{:S(2)}) collective-permute-start(f32[576,128]{1,0:T(8,128)S(1)} %get-tuple-element.47), channel_id=1, source_target_pairs={{0,1},{1,0},{2,3},{3,2},{4,5},{5,4},{6,7},{7,6},{8,9},{9,8},{10,11... | collective-permute-start | bytes 884744 | tf_op jit(solution)/shard_map/ppermute | solution.py:415
  49.3 12.9 %collective-permute-start.6 = (f32[384,128]{1,0:T(8,128)S(1)}, f32[384,128]{1,0:T(8,128)S(1)}, u32[]{:S(2)}, u32[]{:S(2)}) collective-permute-start(f32[384,128]{1,0:T(8,128)S(1)} %get-tuple-element.52), channel_id=1, source_target_pairs={{1,2},{2,1},{3,4},{4,3},{5,6},{6,5},{7,8},{8,7},{9,10},{10,9},{11,... | collective-permute-start | bytes 589832 | tf_op jit(solution)/shard_map/ppermute | solution.py:414
  50.0 12.3 %collective-permute-start.7 = (f32[384,128]{1,0:T(8,128)S(1)}, f32[384,128]{1,0:T(8,128)S(1)}, u32[]{:S(2)}, u32[]{:S(2)}) collective-permute-start(f32[384,128]{1,0:T(8,128)S(1)} %get-tuple-element.53), channel_id=1, source_target_pairs={{0,1},{1,0},{2,3},{3,2},{4,5},{5,4},{6,7},{7,6},{8,9},{9,8},{10,11... | collective-permute-start | bytes 589832 | tf_op jit(solution)/shard_map/ppermute | solution.py:415
